TPU v7x, 32 devices: a whole 2x2x4 slice. The times are simulated.
32 devices in a mesh: grp: 2 (over x), chan: 8 (over z, y), tm: 2 (over core).
Axes of the slice: x: 2, y: 2, z: 4, core: 2. Of those that a mesh axis runs over, the one named last changes fastest.
Arguments:
- spectra: bfloat16 [1024, 32, 2, 128], P(('grp', 'chan'), 'tm'), parts along dimension 0, may hold values from -6 to 6
- channel_mask: int32 [1024], P(('grp', 'chan')), parts along dimension 0, may hold values 0 or 1
- window_mask: int32 [64], P(('grp', 'tm')), parts along dimension 0, may hold values 0 or 1
- source_block: int32 [4], replicated, may hold values from 0 to 7
Outputs:
- stacks: bfloat16 [4, 64, 1024, 128], P(None, 'tm', ('grp', 'chan')), parts along dimension 2
There are 2 independent parts, one for each index of `grp`. A program takes and returns all parts, laid end to end along the dimension named above; an argument that names none is the same for every part. Nothing has to cross between parts.
All inputs are finite; a program needn't handle non-finite values. No bound on the sum of `channel_mask` or of `window_mask` on one device may be relied on, other than what follows from the above.
Results may differ from a plain program's by a relative error of at most 0.0075.
Values may be sent and summed in bfloat16 or wider, within the bound.
No kernel may reach another device: no remote copies, remote signals or barrier semaphores. Data moves between devices by JAX's collectives and lax.ppermute only.
A program may use at most 64 MiB of HBM per device.

v0:
```python
import functools
import math

import jax
import jax.numpy as jnp
import numpy as np
from jax import lax
from jax.experimental import pallas as pl
from jax.experimental.pallas import tpu as pltpu
from jax.sharding import PartitionSpec as P

LAGS = 128
NFFT = 8192
LOW_BIN = 8
LAG_STEP = 28
WATER = 0.1
BINS_TILE = 16

VMEM = pltpu.VMEM
SMEM = pltpu.SMEM


def ring_order(mesh):
    count = mesh.shape["chan"]
    natural = list(range(count))
    folded = natural[0::2] + natural[1::2][::-1]
    if count % 2:
        return natural
    grid = np.moveaxis(mesh.devices, mesh.axis_names.index("chan"), 0).reshape(count, -1)[:, 0]
    places = [getattr(device, "coords", None) for device in grid]
    if any(place is None for place in places):
        return folded if count == 8 else natural

    def length(tour):
        return sum(
            sum(abs(a - b) for a, b in zip(places[tour[i]], places[tour[i - 1]]))
            for i in range(count)
        )

    return folded if length(folded) < length(natural) else natural


def lag_tables(windows, bins):
    freq = np.arange(bins) + LOW_BIN
    lag = (np.arange(LAGS) - LAGS // 2) * LAG_STEP
    phase = (freq[:, None] * lag[None, :] % NFFT) * (2.0 * math.pi / NFFT)
    table = np.concatenate((np.cos(phase), -np.sin(phase))) / math.sqrt(windows * bins)
    return jnp.asarray(table, jnp.float32).astype(jnp.bfloat16)


def whiten_kernel(chan_mask, win_mask, spectra, same, other):
    rows, bins = spectra.shape[1:]
    half = same.shape[0]
    mine = lax.axis_index("tm") * half
    theirs = half - mine
    lane = lax.broadcasted_iota(jnp.int32, (rows, bins), 1)
    row = lax.broadcasted_iota(jnp.int32, (rows, bins), 0)
    even = row % 2 == 0
    keep = jnp.zeros((rows, bins), jnp.float32)
    for w in range(rows // 2):
        keep = jnp.where(row // 2 == w, win_mask[w].astype(jnp.float32), keep)

    def earlier(m):
        return jnp.where(lane == 0, m, pltpu.roll(m, 1, 1))

    def later(m):
        return jnp.where(lane == bins - 1, m, pltpu.roll(m, bins - 1, 1))

    def whitened(channel):
        values = spectra[channel].astype(jnp.float32)
        square = values * values
        pair = jnp.where(even, pltpu.roll(square, rows - 1, 0), pltpu.roll(square, 1, 0))
        magnitude = jnp.sqrt(square + pair)
        e1 = earlier(magnitude)
        l1 = later(magnitude)
        smoothed = (earlier(e1) + e1 + magnitude + l1 + later(l1)) / 5.0
        scaling = keep * chan_mask[channel].astype(jnp.float32) / (smoothed + WATER)
        return (values * scaling).astype(jnp.bfloat16)

    def step(i, _):
        same[i] = whitened(mine + i)
        other[i] = whitened(theirs + i)
        return 0

    lax.fori_loop(0, half, step, 0, unroll=4)


def whiten(spectra, chan_mask, win_mask):
    channels, rows, bins = spectra.shape
    piece = jax.ShapeDtypeStruct((channels // 2, rows, bins), jnp.bfloat16)
    return pl.pallas_call(
        whiten_kernel,
        out_shape=(piece, piece),
        in_specs=[
            pl.BlockSpec(memory_space=SMEM),
            pl.BlockSpec(memory_space=SMEM),
            pl.BlockSpec(memory_space=VMEM),
        ],
        out_specs=(pl.BlockSpec(memory_space=VMEM),) * 2,
        name="whiten",
    )(chan_mask, win_mask, spectra)


def receiver_kernel(same, other, far_same, far_other, weights, flat, wide):
    half, rows, bins = same.shape
    mine = lax.axis_index("tm") * half
    theirs = half - mine
    deep = 2 * rows
    for i in range(half):
        for start, near, far in ((mine, same, far_other), (theirs, other, far_same)):
            at = pl.multiple_of((start + i) * deep, deep)
            flat[pl.ds(at, rows), :] = near[i].astype(jnp.float32)
            flat[pl.ds(at + rows, rows), :] = far[i].astype(jnp.float32)
    for w in range(rows):
        real = flat[pl.ds(2 * w, 2 * half, stride=deep), :]
        imag = flat[pl.ds(2 * w + 1, 2 * half, stride=deep), :]
        wide[pl.ds(2 * w, bins, stride=deep), :] = jnp.concatenate((real, imag)).T
        wide[pl.ds(2 * w + 1, bins, stride=deep), :] = jnp.concatenate((imag, -real)).T
    weights[...] = wide[...].astype(jnp.bfloat16)


def receiver_weights(same, other, far_same, far_other):
    half, rows, bins = same.shape
    return pl.pallas_call(
        receiver_kernel,
        out_shape=jax.ShapeDtypeStruct((bins * 2 * rows, 4 * half), jnp.bfloat16),
        in_specs=[pl.BlockSpec(memory_space=VMEM)] * 4,
        out_specs=pl.BlockSpec(memory_space=VMEM),
        scratch_shapes=[
            VMEM((2 * half * 2 * rows, bins), jnp.float32),
            VMEM((bins * 2 * rows, 4 * half), jnp.float32),
        ],
        compiler_params=pltpu.CompilerParams(vmem_limit_bytes=24 << 20),
        cost_estimate=pl.CostEstimate(flops=2 << 30, bytes_accessed=12 << 20, transcendentals=0),
        name="receiver_weights",
    )(same, other, far_same, far_other)


def stack_kernel(distances, first, tour, place, steps, weights, table, *refs):
    blocks = len(distances)
    pieces = refs[: 2 * blocks]
    out = refs[2 * blocks + (0 if first else 1)]
    src, turned, cross, done, in_sem, out_sem = refs[2 * blocks + (1 if first else 2) :]
    sources, rows, bins = src.shape[2:]
    count = steps.shape[0]
    ring = tour.shape[0]
    lanes = 2 * rows
    per_tile = 128 // lanes
    tiles = BINS_TILE // per_tile
    depth = BINS_TILE * lanes
    row = lax.broadcasted_iota(jnp.int32, (BINS_TILE, 128), 0)
    col = lax.broadcasted_iota(jnp.int32, (BINS_TILE, 128), 1)
    receivers = weights.shape[1] // 2
    me = place[lax.axis_index("chan")]
    owners = [tour[lax.rem(me + d + ring, ring)] for d in distances]
    needed = [
        functools.reduce(jnp.logical_or, [steps[k] == owner for k in range(count)])
        for owner in owners
    ]
    part = sources // 2

    def arrival(b, h):
        return pltpu.make_async_copy(pieces[2 * b + h], src.at[b, h], in_sem.at[b, h])

    for b in range(blocks):
        @pl.when(needed[b])
        def _(b=b):
            for h in range(2):
                arrival(b, h).start()

    def departure(b, k, c):
        return pltpu.make_async_copy(
            done.at[b, pl.ds(c * part, part)], out.at[k, pl.ds(c * part, part)], out_sem.at[b, k, c]
        )

    def compute(b, owner):
        for s in range(sources):
            turned[s] = jnp.concatenate([src[b, 0, s], src[b, 1, s]] * per_tile, axis=0).T
        for g in range(bins // BINS_TILE):
            at = g * BINS_TILE
            mine = turned[:, at : at + BINS_TILE, :]
            wide = jnp.concatenate(
                [
                    jnp.where(
                        (row == q * per_tile + col // lanes)[None], mine, jnp.zeros_like(mine)
                    ).reshape(sources * BINS_TILE, 128)
                    for q in range(tiles)
                ],
                axis=1,
            )
            x = jnp.dot(
                wide, weights[g * depth : (g + 1) * depth, :], preferred_element_type=jnp.float32
            )
            cross[:, at : at + BINS_TILE, :] = x.reshape(sources, BINS_TILE, 2 * receivers).astype(
                jnp.bfloat16
            )
        for c in range(2):
            turns = [cross[c * part + i].T for i in range(part)]
            left = jnp.concatenate(
                [jnp.concatenate([x[:receivers], x[receivers:]], axis=1) for x in turns]
            )
            y = jnp.dot(left, table[...], preferred_element_type=jnp.float32)
            done[b, c * part : (c + 1) * part] = y.reshape(part, receivers, LAGS).astype(
                jnp.bfloat16
            )
            for k in range(count):
                @pl.when(steps[k] == owner)
                def _(k=k, c=c):
                    departure(b, k, c).start()

    def turn(b, _):
        later = b == blocks - 1
        owner = jnp.where(later, owners[-1], owners[0])

        @pl.when(jnp.where(later, needed[-1], needed[0]))
        def _():
            for i in range(blocks):
                @pl.when(b == i)
                def _(i=i):
                    for h in range(2):
                        arrival(i, h).wait()
            compute(b, owner)
        return 0

    lax.fori_loop(0, blocks, turn, 0)
    for b in range(blocks):
        for k in range(count):
            @pl.when(steps[k] == owners[b])
            def _(b=b, k=k):
                for c in range(2):
                    departure(b, k, c).wait()


def stack(distances, tour, place, steps, weights, table, pieces, previous, out_shape):
    blocks = len(distances)
    sources, rows, bins = pieces[0].shape
    receivers = weights.shape[1] // 2
    count = steps.shape[0]
    first = previous is None
    args = [tour, place, steps, weights, table, *pieces] + ([] if first else [previous])
    return pl.pallas_call(
        functools.partial(stack_kernel, distances, first),
        out_shape=out_shape,
        in_specs=[pl.BlockSpec(memory_space=SMEM)] * 3
        + [pl.BlockSpec(memory_space=VMEM)] * 2
        + [pl.BlockSpec(memory_space=pl.ANY)] * (len(args) - 5),
        out_specs=pl.BlockSpec(memory_space=pl.ANY),
        scratch_shapes=[
            VMEM((blocks, 2, sources, rows, bins), jnp.bfloat16),
            VMEM((sources, bins, 128), jnp.bfloat16),
            VMEM((sources, bins, 2 * receivers), jnp.bfloat16),
            VMEM((blocks, sources, receivers, LAGS), jnp.bfloat16),
            pltpu.SemaphoreType.DMA((blocks, 2)),
            pltpu.SemaphoreType.DMA((blocks, count, 2)),
        ],
        input_output_aliases={} if first else {len(args) - 1: 0},
        compiler_params=pltpu.CompilerParams(vmem_limit_bytes=24 << 20),
        cost_estimate=pl.CostEstimate(
            flops=blocks * (3 << 30), bytes_accessed=blocks << 20, transcendentals=0
        ),
        name="stack",
    )(*args)


def shards(ring, spectra, channel_mask, window_mask, source_block):
    count = len(ring)
    channels, windows, parts, bins = spectra.shape
    steps = source_block.shape[0]
    halves = lax.axis_size("tm")
    same, other = whiten(
        spectra.reshape(channels, windows * parts, bins), channel_mask, window_mask
    )

    def across(x):
        return lax.ppermute(x, "tm", [(0, 1), (1, 0)])

    def send(x, direction, cross=False):
        pairs = []
        for i in range(count):
            a, b = ring[i], ring[(i + direction) % count]
            for t in range(2):
                pairs.append((2 * a + t, 2 * b + (1 - t if cross else t)))
        return lax.ppermute(x, ("chan", "tm"), pairs)

    table = lag_tables(windows * halves, bins)
    place = np.zeros(count, np.int32)
    place[list(ring)] = np.arange(count)
    where = (jnp.asarray(np.asarray(ring, np.int32)), jnp.asarray(place))

    forward = (send(same, 1), send(other, 1, True))
    backward = (send(same, -1), send(other, -1, True))
    far_other = across(other)
    far_same = across(same)
    weights = receiver_weights(same, other, far_same, far_other)
    run = functools.partial(
        stack,
        out_shape=jax.ShapeDtypeStruct((steps, channels // 2, channels, LAGS), jnp.bfloat16),
    )
    rest = (*where, source_block, weights, table)
    out = run((0,), *rest, (same, far_other), None)
    half = count // 2
    for hop in range(1, half):
        pieces = forward + backward
        if hop < half - 1:
            forward = tuple(send(x, 1) for x in forward)
            backward = tuple(send(x, -1) for x in backward)
        else:
            forward = (send(forward[0], 1),)
            backward = (send(backward[1], -1),)
        out = run((-hop, hop), *rest, pieces, out)
    return run((half,), *rest, forward + backward, out)


def solution(mesh):
    placed = (P(("grp", "chan"), "tm", None, None), P(("grp", "chan")), P(("grp", "tm")), P())
    return jax.shard_map(
        functools.partial(shards, ring_order(mesh)),
        mesh=mesh,
        in_specs=placed,
        out_specs=P(None, "tm", ("grp", "chan"), None),
        check_vma=False,
    )
```

profile of v0, /device:TPU:0, one launch (start us, length us, event | category | flops | bytes accessed | tf_op | source)
XLA Modules:
  0.0 65.4 jit_solution(2324598888768349818)
XLA Ops:
  0.0 4.0 %whiten.1 = (bf16[32,32,128]{2,1,0:T(8,128)(2,1)}, bf16[32,32,128]{2,1,0:T(8,128)(2,1)}) custom-call(s32[64]{0:T(128)} %chan_mask.1, s32[16]{0:T(128)} %win_mask.1, bf16[64,32,128]{2,1,0:T(8,128)(2,1)} %bitcast.1), custom_call_target="tpu_custom_call" | custom-call | tf_op jit(solution)/shard_map/whiten/pallas_call | solution.py:91
  4.0 0.5 collective-permute-start
  4.5 2.5 %collective-permute-start.13 = (bf16[32,32,128]{2,1,0:T(8,128)(2,1)}, bf16[32,32,128]{2,1,0:T(8,128)(2,1)S(1)}, u32[]{:S(2)}, u32[]{:S(2)}) collective-permute-start(bf16[32,32,128]{2,1,0:T(8,128)(2,1)} %get-tuple-element.7.same.refs_0_), channel_id=1, source_target_pairs={{0,2},{1,3},{4,0},{5,1},{8,4},{9,5},{12,8},{13,9},{14,12},{15,13},... | collective-permute-start | bytes 786440 | tf_op jit(solution)/shard_map/ppermute | solution.py:283
  7.0 0.1 collective-permute-start.2
  7.1 1.5 %collective-permute-start.10 = (bf16[32,32,128]{2,1,0:T(8,128)(2,1)}, bf16[32,32,128]{2,1,0:T(8,128)(2,1)S(1)}, u32[]{:S(2)}, u32[]{:S(2)}) collective-permute-start(bf16[32,32,128]{2,1,0:T(8,128)(2,1)} %get-tuple-element.8.other), channel_id=1, source_target_pairs={{0,5},{1,4},{4,9},{5,8},{8,13},{9,12},{12,15},{13,14},{14,11},{15,... | collective-permute-start | bytes 786440 | tf_op jit(solution)/shard_map/ppermute | solution.py:283
  8.6 0.2 collective-permute-start.6
  8.9 0.3 collective-permute-start.1
  9.2 5.2 %collective-permute-done.13.refs_2_ = bf16[32,32,128]{2,1,0:T(8,128)(2,1)S(1)} collective-permute-done((bf16[32,32,128]{2,1,0:T(8,128)(2,1)}, bf16[32,32,128]{2,1,0:T(8,128)(2,1)S(1)}, u32[]{:S(2)}, u32[]{:S(2)}) %collective-permute-start.13) | collective-permute-done | bytes 262176 | tf_op jit(solution)/shard_map/ppermute | solution.py:283
  14.4 1.9 %collective-permute-start.14 = (bf16[32,32,128]{2,1,0:T(8,128)(2,1)S(1)}, bf16[32,32,128]{2,1,0:T(8,128)(2,1)S(1)}, u32[]{:S(2)}, u32[]{:S(2)}) collective-permute-start(bf16[32,32,128]{2,1,0:T(8,128)(2,1)S(1)} %collective-permute-done.13.refs_2_), channel_id=1, source_target_pairs={{0,2},{1,3},{4,0},{5,1},{8,4},{9,5},{12,8},{13,9},{14,12},{15,13},... | collective-permute-start | bytes 786440 | tf_op jit(solution)/shard_map/ppermute | solution.py:283
  16.3 0.0 collective-permute-done.2.refs_0_
  16.3 0.1 collective-permute-start.3
  16.4 4.1 %collective-permute-done.10.refs_1_ = bf16[32,32,128]{2,1,0:T(8,128)(2,1)S(1)} collective-permute-done((bf16[32,32,128]{2,1,0:T(8,128)(2,1)}, bf16[32,32,128]{2,1,0:T(8,128)(2,1)S(1)}, u32[]{:S(2)}, u32[]{:S(2)}) %collective-permute-start.10) | collective-permute-done | bytes 262176 | tf_op jit(solution)/shard_map/ppermute | solution.py:283
  20.5 1.1 %collective-permute-start.11 = (bf16[32,32,128]{2,1,0:T(8,128)(2,1)S(1)}, bf16[32,32,128]{2,1,0:T(8,128)(2,1)S(1)}, u32[]{:S(2)}, u32[]{:S(2)}) collective-permute-start(bf16[32,32,128]{2,1,0:T(8,128)(2,1)S(1)} %collective-permute-done.10.refs_1_), channel_id=1, source_target_pairs={{0,4},{1,5},{4,8},{5,9},{8,12},{9,13},{12,14},{13,15},{14,10},{15,... | collective-permute-start | bytes 786440 | tf_op jit(solution)/shard_map/ppermute | solution.py:283
  21.7 0.0 collective-permute-done.6.refs_3_
  21.7 0.9 %collective-permute-start.7 = (bf16[32,32,128]{2,1,0:T(8,128)(2,1)S(1)}, bf16[32,32,128]{2,1,0:T(8,128)(2,1)S(1)}, u32[]{:S(2)}, u32[]{:S(2)}) collective-permute-start(bf16[32,32,128]{2,1,0:T(8,128)(2,1)S(1)} %collective-permute-done.6.refs_3_), channel_id=1, source_target_pairs={{0,2},{1,3},{4,0},{5,1},{8,4},{9,5},{12,8},{13,9},{14,12},{15,13},... | collective-permute-start | bytes 786440 | tf_op jit(solution)/shard_map/ppermute | solution.py:283
  22.6 0.9 %copy-done = bf16[32,32,128]{2,1,0:T(8,128)(2,1)S(1)} copy-done((bf16[32,32,128]{2,1,0:T(8,128)(2,1)S(1)}, bf16[32,32,128]{2,1,0:T(8,128)(2,1)}, u32[]{:S(2)}) %copy-start) | copy-done | bytes 262168
  23.5 0.9 %copy-done.1 = bf16[32,32,128]{2,1,0:T(8,128)(2,1)S(1)} copy-done((bf16[32,32,128]{2,1,0:T(8,128)(2,1)S(1)}, bf16[32,32,128]{2,1,0:T(8,128)(2,1)}, u32[]{:S(2)}) %copy-start.1) | copy-done | bytes 262168
  24.5 4.2 %receiver_weights.1.weights = bf16[8192,128]{1,0:T(8,128)(2,1)S(1)} custom-call(bf16[32,32,128]{2,1,0:T(8,128)(2,1)S(1)} %copy-done, bf16[32,32,128]{2,1,0:T(8,128)(2,1)S(1)} %copy-done.1, bf16[32,32,128]{2,1,0:T(8,128)(2,1)S(1)} %collective-permute-done.far_same, bf16[32,32,128]{2,1,0:T(8,128)(2,1)S(1)} %collective-permute-done.1.far_other.refs_1_), custom_call_target="tpu_custom_call" | custom-call | flops 2147483648 | bytes 12582912 | tf_op jit(solution)/shard_map/receiver_weights/pallas_call | solution.py:124
  28.7 4.4 %stack.5.refs_4_ = bf16[4,32,64,128]{3,2,1,0:T(8,128)(2,1)} custom-call(s32[8]{0:T(128)S(1)} %copy-done.4, s32[8]{0:T(128)S(1)} %copy-done.5, s32[4]{0:T(128)S(1)} %copy-done.2, bf16[8192,128]{1,0:T(8,128)(2,1)S(1)} %receiver_weights.1.weights, bf16[256,128]{1,0:T(8,128)(2,1)S(1)} %copy-done.3, bf16[32,32,128]{2,1,0:T(8,128)(2,1)S(1)} %copy-done, ...), custom_call_target="tpu_custom_call" | custom-call | flops 3221225472 | bytes 1048576 | tf_op jit(solution)/shard_map/stack/pallas_call | solution.py:241
  33.1 4.5 %stack.6.refs_4_ = bf16[4,32,64,128]{3,2,1,0:T(8,128)(2,1)} custom-call(s32[8]{0:T(128)S(1)} %copy-done.4, s32[8]{0:T(128)S(1)} %copy-done.5, s32[4]{0:T(128)S(1)} %copy-done.2, bf16[8192,128]{1,0:T(8,128)(2,1)S(1)} %receiver_weights.1.weights, bf16[256,128]{1,0:T(8,128)(2,1)S(1)} %copy-done.3, ...), custom_call_target="tpu_custom_call", output_to_operand_aliasing={{}: (9, {})} | custom-call | flops 6442450944 | bytes 2097152 | tf_op jit(solution)/shard_map/stack/pallas_call | solution.py:241
  37.6 0.1 collective-permute-start.4
  37.7 2.0 %collective-permute-start.15 = (bf16[32,32,128]{2,1,0:T(8,128)(2,1)S(1)}, bf16[32,32,128]{2,1,0:T(8,128)(2,1)S(1)}, u32[]{:S(2)}, u32[]{:S(2)}) collective-permute-start(bf16[32,32,128]{2,1,0:T(8,128)(2,1)S(1)} %collective-permute-done.14.refs_2_), channel_id=1, source_target_pairs={{0,2},{1,3},{4,0},{5,1},{8,4},{9,5},{12,8},{13,9},{14,12},{15,13},... | collective-permute-start | bytes 786440 | tf_op jit(solution)/shard_map/ppermute | solution.py:283
  39.7 1.6 %collective-permute-start.8 = (bf16[32,32,128]{2,1,0:T(8,128)(2,1)S(1)}, bf16[32,32,128]{2,1,0:T(8,128)(2,1)S(1)}, u32[]{:S(2)}, u32[]{:S(2)}) collective-permute-start(bf16[32,32,128]{2,1,0:T(8,128)(2,1)S(1)} %collective-permute-done.7.refs_3_), channel_id=1, source_target_pairs={{0,2},{1,3},{4,0},{5,1},{8,4},{9,5},{12,8},{13,9},{14,12},{15,13},... | collective-permute-start | bytes 786440 | tf_op jit(solution)/shard_map/ppermute | solution.py:283
  41.3 0.4 collective-permute-start.12
  41.7 1.0 %stack.7.refs_4_ = bf16[4,32,64,128]{3,2,1,0:T(8,128)(2,1)} custom-call(s32[8]{0:T(128)S(1)} %copy-done.4, s32[8]{0:T(128)S(1)} %copy-done.5, s32[4]{0:T(128)S(1)} %copy-done.2, bf16[8192,128]{1,0:T(8,128)(2,1)S(1)} %receiver_weights.1.weights, bf16[256,128]{1,0:T(8,128)(2,1)S(1)} %copy-done.3, ...), custom_call_target="tpu_custom_call", output_to_operand_aliasing={{}: (9, {})} | custom-call | flops 6442450944 | bytes 2097152 | tf_op jit(solution)/shard_map/stack/pallas_call | solution.py:241
  42.7 4.1 %collective-permute-done.4.refs_0_ = bf16[32,32,128]{2,1,0:T(8,128)(2,1)S(1)} collective-permute-done((bf16[32,32,128]{2,1,0:T(8,128)(2,1)S(1)}, bf16[32,32,128]{2,1,0:T(8,128)(2,1)S(1)}, u32[]{:S(2)}, u32[]{:S(2)}) %collective-permute-start.4) | collective-permute-done | bytes 262176 | tf_op jit(solution)/shard_map/ppermute | solution.py:283
  46.8 3.0 %collective-permute-start.5 = (bf16[32,32,128]{2,1,0:T(8,128)(2,1)S(1)}, bf16[32,32,128]{2,1,0:T(8,128)(2,1)S(1)}, u32[]{:S(2)}, u32[]{:S(2)}) collective-permute-start(bf16[32,32,128]{2,1,0:T(8,128)(2,1)S(1)} %collective-permute-done.4.refs_0_), channel_id=1, source_target_pairs={{0,4},{1,5},{4,8},{5,9},{8,12},{9,13},{12,14},{13,15},{14,10},{15,... | collective-permute-start | bytes 786440 | tf_op jit(solution)/shard_map/ppermute | solution.py:283
  49.8 2.7 %collective-permute-done.8.refs_3_ = bf16[32,32,128]{2,1,0:T(8,128)(2,1)S(1)} collective-permute-done((bf16[32,32,128]{2,1,0:T(8,128)(2,1)S(1)}, bf16[32,32,128]{2,1,0:T(8,128)(2,1)S(1)}, u32[]{:S(2)}, u32[]{:S(2)}) %collective-permute-start.8) | collective-permute-done | bytes 262176 | tf_op jit(solution)/shard_map/ppermute | solution.py:283
  52.5 1.7 %collective-permute-start.9 = (bf16[32,32,128]{2,1,0:T(8,128)(2,1)S(1)}, bf16[32,32,128]{2,1,0:T(8,128)(2,1)S(1)}, u32[]{:S(2)}, u32[]{:S(2)}) collective-permute-start(bf16[32,32,128]{2,1,0:T(8,128)(2,1)S(1)} %collective-permute-done.8.refs_3_), channel_id=1, source_target_pairs={{0,2},{1,3},{4,0},{5,1},{8,4},{9,5},{12,8},{13,9},{14,12},{15,13},... | collective-permute-start | bytes 786440 | tf_op jit(solution)/shard_map/ppermute | solution.py:283
  54.2 4.5 %stack.8.refs_2_ = bf16[4,32,64,128]{3,2,1,0:T(8,128)(2,1)} custom-call(s32[8]{0:T(128)S(1)} %copy-done.4, s32[8]{0:T(128)S(1)} %copy-done.5, s32[4]{0:T(128)S(1)} %copy-done.2, bf16[8192,128]{1,0:T(8,128)(2,1)S(1)} %receiver_weights.1.weights, bf16[256,128]{1,0:T(8,128)(2,1)S(1)} %copy-done.3, ...), custom_call_target="tpu_custom_call", output_to_operand_aliasing={{}: (9, {})} | custom-call | flops 6442450944 | bytes 2097152 | tf_op jit(solution)/shard_map/stack/pallas_call | solution.py:241
  58.7 2.1 %collective-permute-done.9.refs_1_ = bf16[32,32,128]{2,1,0:T(8,128)(2,1)S(1)} collective-permute-done((bf16[32,32,128]{2,1,0:T(8,128)(2,1)S(1)}, bf16[32,32,128]{2,1,0:T(8,128)(2,1)S(1)}, u32[]{:S(2)}, u32[]{:S(2)}) %collective-permute-start.9) | collective-permute-done | bytes 262176 | tf_op jit(solution)/shard_map/ppermute | solution.py:283
  60.8 4.4 %stack.9 = bf16[4,32,64,128]{3,2,1,0:T(8,128)(2,1)} custom-call(s32[8]{0:T(128)S(1)} %copy-done.4, s32[8]{0:T(128)S(1)} %copy-done.5, s32[4]{0:T(128)S(1)} %copy-done.2, bf16[8192,128]{1,0:T(8,128)(2,1)S(1)} %receiver_weights.1.weights, bf16[256,128]{1,0:T(8,128)(2,1)S(1)} %copy-done.3, ...), custom_call_target="tpu_custom_call", output_to_operand_aliasing={{}: (7, {})} | custom-call | flops 3221225472 | bytes 1048576 | tf_op jit(solution)/shard_map/stack/pallas_call | solution.py:241
  (19 shorter events, 0.0 us)
Async XLA Ops:
  0.0 28.7 %copy-start.3 = (bf16[256,128]{1,0:T(8,128)(2,1)S(1)}, bf16[256,128]{1,0:T(8,128)(2,1)}, u32[]{:S(2)}) copy-start(bf16[256,128]{1,0:T(8,128)(2,1)} %constant.9.table) | copy-start | bytes 196612
  4.0 4.8 %collective-permute-start = (bf16[32,32,128]{2,1,0:T(8,128)(2,1)}, bf16[32,32,128]{2,1,0:T(8,128)(2,1)S(1)}, u32[]{:S(2)}, u32[]{:S(2)}) collective-permute-start(bf16[32,32,128]{2,1,0:T(8,128)(2,1)} %get-tuple-element.7.same.refs_0_), channel_id=1, source_target_pairs={{0,1},{1,0},{2,3},{3,2},{4,5},{5,4},{6,7},{7,6},{8,9},{9,8},{10,11... | collective-permute-start | bytes 786440 | tf_op jit(solution)/shard_map/ppermute | solution.py:275
  4.5 9.9 %collective-permute-start.13 = (bf16[32,32,128]{2,1,0:T(8,128)(2,1)}, bf16[32,32,128]{2,1,0:T(8,128)(2,1)S(1)}, u32[]{:S(2)}, u32[]{:S(2)}) collective-permute-start(bf16[32,32,128]{2,1,0:T(8,128)(2,1)} %get-tuple-element.7.same.refs_0_), channel_id=1, source_target_pairs={{0,2},{1,3},{4,0},{5,1},{8,4},{9,5},{12,8},{13,9},{14,12},{15,13},... | collective-permute-start | bytes 786440 | tf_op jit(solution)/shard_map/ppermute | solution.py:283
  7.0 9.4 %collective-permute-start.2 = (bf16[32,32,128]{2,1,0:T(8,128)(2,1)}, bf16[32,32,128]{2,1,0:T(8,128)(2,1)S(1)}, u32[]{:S(2)}, u32[]{:S(2)}) collective-permute-start(bf16[32,32,128]{2,1,0:T(8,128)(2,1)} %get-tuple-element.7.same.refs_0_), channel_id=1, source_target_pairs={{0,4},{1,5},{4,8},{5,9},{8,12},{9,13},{12,14},{13,15},{14,10},{15,... | collective-permute-start | bytes 786440 | tf_op jit(solution)/shard_map/ppermute | solution.py:283
  7.1 21.6 %copy-start.2 = (s32[4]{0:T(128)S(1)}, s32[4]{0:T(128)}, u32[]{:S(2)}) copy-start(s32[4]{0:T(128)} %steps.9) | copy-start | bytes 52
  7.1 21.6 %copy-start.4 = (s32[8]{0:T(128)S(1)}, s32[8]{0:T(128)}, u32[]{:S(2)}) copy-start(s32[8]{0:T(128)} %constant.7.clone.tour) | copy-start | bytes 100
  7.1 21.6 %copy-start.5 = (s32[8]{0:T(128)S(1)}, s32[8]{0:T(128)}, u32[]{:S(2)}) copy-start(s32[8]{0:T(128)} %constant.8.clone.place) | copy-start | bytes 100
  7.1 13.4 %collective-permute-start.10 = (bf16[32,32,128]{2,1,0:T(8,128)(2,1)}, bf16[32,32,128]{2,1,0:T(8,128)(2,1)S(1)}, u32[]{:S(2)}, u32[]{:S(2)}) collective-permute-start(bf16[32,32,128]{2,1,0:T(8,128)(2,1)} %get-tuple-element.8.other), channel_id=1, source_target_pairs={{0,5},{1,4},{4,9},{5,8},{8,13},{9,12},{12,15},{13,14},{14,11},{15,... | collective-permute-start | bytes 786440 | tf_op jit(solution)/shard_map/ppermute | solution.py:283
  8.6 13.0 %collective-permute-start.6 = (bf16[32,32,128]{2,1,0:T(8,128)(2,1)}, bf16[32,32,128]{2,1,0:T(8,128)(2,1)S(1)}, u32[]{:S(2)}, u32[]{:S(2)}) collective-permute-start(bf16[32,32,128]{2,1,0:T(8,128)(2,1)} %get-tuple-element.8.other), channel_id=1, source_target_pairs={{0,3},{1,2},{4,1},{5,0},{8,5},{9,4},{12,9},{13,8},{14,13},{15,12},... | collective-permute-start | bytes 786440 | tf_op jit(solution)/shard_map/ppermute | solution.py:283
  8.9 13.7 %collective-permute-start.1 = (bf16[32,32,128]{2,1,0:T(8,128)(2,1)}, bf16[32,32,128]{2,1,0:T(8,128)(2,1)S(1)}, u32[]{:S(2)}, u32[]{:S(2)}) collective-permute-start(bf16[32,32,128]{2,1,0:T(8,128)(2,1)} %get-tuple-element.8.other), channel_id=1, source_target_pairs={{0,1},{1,0},{2,3},{3,2},{4,5},{5,4},{6,7},{7,6},{8,9},{9,8},{10,11... | collective-permute-start | bytes 786440 | tf_op jit(solution)/shard_map/ppermute | solution.py:275
  14.4 23.2 %collective-permute-start.14 = (bf16[32,32,128]{2,1,0:T(8,128)(2,1)S(1)}, bf16[32,32,128]{2,1,0:T(8,128)(2,1)S(1)}, u32[]{:S(2)}, u32[]{:S(2)}) collective-permute-start(bf16[32,32,128]{2,1,0:T(8,128)(2,1)S(1)} %collective-permute-done.13.refs_2_), channel_id=1, source_target_pairs={{0,2},{1,3},{4,0},{5,1},{8,4},{9,5},{12,8},{13,9},{14,12},{15,13},... | collective-permute-start | bytes 786440 | tf_op jit(solution)/shard_map/ppermute | solution.py:283
  16.3 21.2 %collective-permute-start.3 = (bf16[32,32,128]{2,1,0:T(8,128)(2,1)S(1)}, bf16[32,32,128]{2,1,0:T(8,128)(2,1)S(1)}, u32[]{:S(2)}, u32[]{:S(2)}) collective-permute-start(bf16[32,32,128]{2,1,0:T(8,128)(2,1)S(1)} %collective-permute-done.2.refs_0_), channel_id=1, source_target_pairs={{0,4},{1,5},{4,8},{5,9},{8,12},{9,13},{12,14},{13,15},{14,10},{15,... | collective-permute-start | bytes 786440 | tf_op jit(solution)/shard_map/ppermute | solution.py:283
  20.5 20.7 %collective-permute-start.11 = (bf16[32,32,128]{2,1,0:T(8,128)(2,1)S(1)}, bf16[32,32,128]{2,1,0:T(8,128)(2,1)S(1)}, u32[]{:S(2)}, u32[]{:S(2)}) collective-permute-start(bf16[32,32,128]{2,1,0:T(8,128)(2,1)S(1)} %collective-permute-done.10.refs_1_), channel_id=1, source_target_pairs={{0,4},{1,5},{4,8},{5,9},{8,12},{9,13},{12,14},{13,15},{14,10},{15,... | collective-permute-start | bytes 786440 | tf_op jit(solution)/shard_map/ppermute | solution.py:283
  21.7 18.0 %collective-permute-start.7 = (bf16[32,32,128]{2,1,0:T(8,128)(2,1)S(1)}, bf16[32,32,128]{2,1,0:T(8,128)(2,1)S(1)}, u32[]{:S(2)}, u32[]{:S(2)}) collective-permute-start(bf16[32,32,128]{2,1,0:T(8,128)(2,1)S(1)} %collective-permute-done.6.refs_3_), channel_id=1, source_target_pairs={{0,2},{1,3},{4,0},{5,1},{8,4},{9,5},{12,8},{13,9},{14,12},{15,13},... | collective-permute-start | bytes 786440 | tf_op jit(solution)/shard_map/ppermute | solution.py:283
  22.6 1.0 %copy-start = (bf16[32,32,128]{2,1,0:T(8,128)(2,1)S(1)}, bf16[32,32,128]{2,1,0:T(8,128)(2,1)}, u32[]{:S(2)}) copy-start(bf16[32,32,128]{2,1,0:T(8,128)(2,1)} %get-tuple-element.7.same.refs_0_) | copy-start | bytes 786436
  23.5 0.9 %copy-start.1 = (bf16[32,32,128]{2,1,0:T(8,128)(2,1)S(1)}, bf16[32,32,128]{2,1,0:T(8,128)(2,1)}, u32[]{:S(2)}) copy-start(bf16[32,32,128]{2,1,0:T(8,128)(2,1)} %get-tuple-element.8.other) | copy-start | bytes 786436
  37.6 9.2 %collective-permute-start.4 = (bf16[32,32,128]{2,1,0:T(8,128)(2,1)S(1)}, bf16[32,32,128]{2,1,0:T(8,128)(2,1)S(1)}, u32[]{:S(2)}, u32[]{:S(2)}) collective-permute-start(bf16[32,32,128]{2,1,0:T(8,128)(2,1)S(1)} %collective-permute-done.3.refs_0_), channel_id=1, source_target_pairs={{0,4},{1,5},{4,8},{5,9},{8,12},{9,13},{12,14},{13,15},{14,10},{15,... | collective-permute-start | bytes 786440 | tf_op jit(solution)/shard_map/ppermute | solution.py:283
  37.7 16.5 %collective-permute-start.15 = (bf16[32,32,128]{2,1,0:T(8,128)(2,1)S(1)}, bf16[32,32,128]{2,1,0:T(8,128)(2,1)S(1)}, u32[]{:S(2)}, u32[]{:S(2)}) collective-permute-start(bf16[32,32,128]{2,1,0:T(8,128)(2,1)S(1)} %collective-permute-done.14.refs_2_), channel_id=1, source_target_pairs={{0,2},{1,3},{4,0},{5,1},{8,4},{9,5},{12,8},{13,9},{14,12},{15,13},... | collective-permute-start | bytes 786440 | tf_op jit(solution)/shard_map/ppermute | solution.py:283
  39.7 12.8 %collective-permute-start.8 = (bf16[32,32,128]{2,1,0:T(8,128)(2,1)S(1)}, bf16[32,32,128]{2,1,0:T(8,128)(2,1)S(1)}, u32[]{:S(2)}, u32[]{:S(2)}) collective-permute-start(bf16[32,32,128]{2,1,0:T(8,128)(2,1)S(1)} %collective-permute-done.7.refs_3_), channel_id=1, source_target_pairs={{0,2},{1,3},{4,0},{5,1},{8,4},{9,5},{12,8},{13,9},{14,12},{15,13},... | collective-permute-start | bytes 786440 | tf_op jit(solution)/shard_map/ppermute | solution.py:283
  41.3 12.9 %collective-permute-start.12 = (bf16[32,32,128]{2,1,0:T(8,128)(2,1)S(1)}, bf16[32,32,128]{2,1,0:T(8,128)(2,1)S(1)}, u32[]{:S(2)}, u32[]{:S(2)}) collective-permute-start(bf16[32,32,128]{2,1,0:T(8,128)(2,1)S(1)} %collective-permute-done.11.refs_1_), channel_id=1, source_target_pairs={{0,4},{1,5},{4,8},{5,9},{8,12},{9,13},{12,14},{13,15},{14,10},{15,... | collective-permute-start | bytes 786440 | tf_op jit(solution)/shard_map/ppermute | solution.py:283
  46.8 11.9 %collective-permute-start.5 = (bf16[32,32,128]{2,1,0:T(8,128)(2,1)S(1)}, bf16[32,32,128]{2,1,0:T(8,128)(2,1)S(1)}, u32[]{:S(2)}, u32[]{:S(2)}) collective-permute-start(bf16[32,32,128]{2,1,0:T(8,128)(2,1)S(1)} %collective-permute-done.4.refs_0_), channel_id=1, source_target_pairs={{0,4},{1,5},{4,8},{5,9},{8,12},{9,13},{12,14},{13,15},{14,10},{15,... | collective-permute-start | bytes 786440 | tf_op jit(solution)/shard_map/ppermute | solution.py:283
  52.5 8.3 %collective-permute-start.9 = (bf16[32,32,128]{2,1,0:T(8,128)(2,1)S(1)}, bf16[32,32,128]{2,1,0:T(8,128)(2,1)S(1)}, u32[]{:S(2)}, u32[]{:S(2)}) collective-permute-start(bf16[32,32,128]{2,1,0:T(8,128)(2,1)S(1)} %collective-permute-done.8.refs_3_), channel_id=1, source_target_pairs={{0,2},{1,3},{4,0},{5,1},{8,4},{9,5},{12,8},{13,9},{14,12},{15,13},... | collective-permute-start | bytes 786440 | tf_op jit(solution)/shard_map/ppermute | solution.py:283
where the time goes:
time: 65.5 us; the launch traced here: 65.4 us
  Pallas kernels  26.9 us (41%)
  waiting for transfers between devices  18.3 us (28%)
  starting transfers between devices  17.9 us (27%)
  local copies, waits for them, and re-layouts  1.91 us (3%)
    pallas_call x5, Pallas kernels, stack(): pl.pallas_call(functools.partial(stack_kernel, distances, first), out_sha...  18.7 us
    ppermute x14, waiting for transfers between devices, send(): return lax.ppermute(x, ('chan', 'tm'), pairs)  18.3 us
    ppermute x14, starting transfers between devices, send(): return lax.ppermute(x, ('chan', 'tm'), pairs)  17.1 us
    pallas_call x1, Pallas kernels, receiver_weights(): pl.pallas_call(receiver_kernel, out_shape=jax.ShapeDtypeStruct((bins * 2...  4.19 us
    pallas_call x1, Pallas kernels, whiten(): pl.pallas_call(whiten_kernel, out_shape=(piece, piece), in_specs=[pl.Bloc...  4.01 us
    unnamed x12, local copies, waits for them, and re-layouts  1.91 us
  transfers between devices with their start and end apart: 16, of which 5 were waited for; matrix products, arithmetic and copies ran while one was open for 0% of the time, Pallas kernels for 28%

commit v1 on v0

--- a/solution.py
+++ b/solution.py
@@ -14,7 +14,8 @@
 LOW_BIN = 8
 LAG_STEP = 28
 WATER = 0.1
-BINS_TILE = 16
+BATCH = 8
+GROUP = 8
 
 VMEM = pltpu.VMEM
 SMEM = pltpu.SMEM
@@ -48,41 +49,72 @@
     return jnp.asarray(table, jnp.float32).astype(jnp.bfloat16)
 
 
+def interleave(first, second):
+    bins = first.shape[-1]
+    lane = lax.broadcasted_iota(jnp.int32, first.shape, 1)
+    even = lane // GROUP % 2 == 0
+    return (
+        jnp.where(even, first, pltpu.roll(second, GROUP, 1)),
+        jnp.where(even, pltpu.roll(first, bins - GROUP, 1), second),
+    )
+
+
 def whiten_kernel(chan_mask, win_mask, spectra, same, other):
     rows, bins = spectra.shape[1:]
     half = same.shape[0]
     mine = lax.axis_index("tm") * half
     theirs = half - mine
-    lane = lax.broadcasted_iota(jnp.int32, (rows, bins), 1)
     row = lax.broadcasted_iota(jnp.int32, (rows, bins), 0)
-    even = row % 2 == 0
     keep = jnp.zeros((rows, bins), jnp.float32)
     for w in range(rows // 2):
         keep = jnp.where(row // 2 == w, win_mask[w].astype(jnp.float32), keep)
 
-    def earlier(m):
-        return jnp.where(lane == 0, m, pltpu.roll(m, 1, 1))
-
-    def later(m):
-        return jnp.where(lane == bins - 1, m, pltpu.roll(m, bins - 1, 1))
-
-    def whitened(channel):
-        values = spectra[channel].astype(jnp.float32)
+    source = lax.broadcasted_iota(jnp.int32, (bins, bins), 0)
+    target = lax.broadcasted_iota(jnp.int32, (bins, bins), 1)
+    band = sum(
+        jnp.where(source == jnp.clip(target + d, 0, bins - 1), 1.0, 0.0) for d in range(-2, 3)
+    ).astype(jnp.bfloat16)
+    band = jnp.concatenate([band] * 3)
+
+    def with_partner(square):
+        even = lax.broadcasted_iota(jnp.int32, square.shape, 0) % 2 == 0
+        last = square.shape[0] - 1
+        return square + jnp.where(even, pltpu.roll(square, last, 0), pltpu.roll(square, 1, 0))
+
+    def whitened(channels):
+        values = jnp.concatenate([spectra[c].astype(jnp.float32) for c in channels])
         square = values * values
-        pair = jnp.where(even, pltpu.roll(square, rows - 1, 0), pltpu.roll(square, 1, 0))
-        magnitude = jnp.sqrt(square + pair)
-        e1 = earlier(magnitude)
-        l1 = later(magnitude)
-        smoothed = (earlier(e1) + e1 + magnitude + l1 + later(l1)) / 5.0
-        scaling = keep * chan_mask[channel].astype(jnp.float32) / (smoothed + WATER)
-        return (values * scaling).astype(jnp.bfloat16)
+        power = jnp.concatenate(
+            [with_partner(square[i : i + 8]) for i in range(0, square.shape[0], 8)]
+        )
+        magnitude = jnp.sqrt(power)
+        high = magnitude.astype(jnp.bfloat16)
+        rest = magnitude - high.astype(jnp.float32)
+        middle = rest.astype(jnp.bfloat16)
+        low = (rest - middle.astype(jnp.float32)).astype(jnp.bfloat16)
+        smoothed = (
+            jnp.dot(
+                jnp.concatenate((high, middle, low), axis=1),
+                band,
+                preferred_element_type=jnp.float32,
+            )
+            / 5.0
+        )
+        kept = jnp.concatenate([keep * chan_mask[c].astype(jnp.float32) for c in channels])
+        return values * (kept / (smoothed + WATER))
 
     def step(i, _):
-        same[i] = whitened(mine + i)
-        other[i] = whitened(theirs + i)
+        for start, piece in ((mine, same), (theirs, other)):
+            values = whitened([start + i * BATCH + j for j in range(BATCH)])
+            for j in range(0, BATCH, 2):
+                pair = interleave(
+                    values[j * rows : (j + 1) * rows], values[(j + 1) * rows : (j + 2) * rows]
+                )
+                piece[i * BATCH + j] = pair[0].astype(jnp.bfloat16)
+                piece[i * BATCH + j + 1] = pair[1].astype(jnp.bfloat16)
         return 0
 
-    lax.fori_loop(0, half, step, 0, unroll=4)
+    lax.fori_loop(0, half // BATCH, step, 0, unroll=2)
 
 
 def whiten(spectra, chan_mask, win_mask):
@@ -106,11 +138,13 @@
     mine = lax.axis_index("tm") * half
     theirs = half - mine
     deep = 2 * rows
-    for i in range(half):
-        for start, near, far in ((mine, same, far_other), (theirs, other, far_same)):
-            at = pl.multiple_of((start + i) * deep, deep)
-            flat[pl.ds(at, rows), :] = near[i].astype(jnp.float32)
-            flat[pl.ds(at + rows, rows), :] = far[i].astype(jnp.float32)
+    for i in range(0, half, 2):
+        for start, sides in ((mine, (same, far_other)), (theirs, (other, far_same))):
+            for h, piece in enumerate(sides):
+                pair = interleave(piece[i].astype(jnp.float32), piece[i + 1].astype(jnp.float32))
+                for j in range(2):
+                    at = pl.multiple_of((start + i + j) * deep + h * rows, rows)
+                    flat[pl.ds(at, rows), :] = pair[j]
     for w in range(rows):
         real = flat[pl.ds(2 * w, 2 * half, stride=deep), :]
         imag = flat[pl.ds(2 * w + 1, 2 * half, stride=deep), :]
@@ -136,7 +170,7 @@
     )(same, other, far_same, far_other)
 
 
-def stack_kernel(distances, first, tour, place, steps, weights, table, *refs):
+def stack_kernel(distances, first, tour, place, steps, table, weights, *refs):
     blocks = len(distances)
     pieces = refs[: 2 * blocks]
     out = refs[2 * blocks + (0 if first else 1)]
@@ -146,10 +180,11 @@
     ring = tour.shape[0]
     lanes = 2 * rows
     per_tile = 128 // lanes
-    tiles = BINS_TILE // per_tile
-    depth = BINS_TILE * lanes
-    row = lax.broadcasted_iota(jnp.int32, (BINS_TILE, 128), 0)
-    col = lax.broadcasted_iota(jnp.int32, (BINS_TILE, 128), 1)
+    tiles = GROUP // per_tile
+    depth = GROUP * lanes
+    pair_rows = 2 * GROUP
+    row = lax.broadcasted_iota(jnp.int32, (pair_rows, 128), 0) % GROUP
+    col = lax.broadcasted_iota(jnp.int32, (pair_rows, 128), 1) // lanes
     receivers = weights.shape[1] // 2
     me = place[lax.axis_index("chan")]
     owners = [tour[lax.rem(me + d + ring, ring)] for d in distances]
@@ -175,25 +210,27 @@
 
     def compute(b, owner):
         for s in range(sources):
-            turned[s] = jnp.concatenate([src[b, 0, s], src[b, 1, s]] * per_tile, axis=0).T
-        for g in range(bins // BINS_TILE):
-            at = g * BINS_TILE
-            mine = turned[:, at : at + BINS_TILE, :]
-            wide = jnp.concatenate(
-                [
-                    jnp.where(
-                        (row == q * per_tile + col // lanes)[None], mine, jnp.zeros_like(mine)
-                    ).reshape(sources * BINS_TILE, 128)
-                    for q in range(tiles)
-                ],
-                axis=1,
-            )
-            x = jnp.dot(
-                wide, weights[g * depth : (g + 1) * depth, :], preferred_element_type=jnp.float32
-            )
-            cross[:, at : at + BINS_TILE, :] = x.reshape(sources, BINS_TILE, 2 * receivers).astype(
-                jnp.bfloat16
-            )
+            turned[s // 2, s % 2] = jnp.concatenate([src[b, 0, s], src[b, 1, s]] * per_tile).T
+        for m in range(bins // pair_rows):
+            at = m * pair_rows
+            sums = []
+            for p in range(2):
+                mine = turned[:, p, at : at + pair_rows, :]
+                wide = jnp.concatenate(
+                    [
+                        jnp.where(
+                            (row == q * per_tile + col)[None], mine, jnp.zeros_like(mine)
+                        ).reshape(sources * GROUP, 128)
+                        for q in range(tiles)
+                    ],
+                    axis=1,
+                )
+                start = (2 * m + p) * depth
+                x = jnp.dot(
+                    wide, weights[start : start + depth, :], preferred_element_type=jnp.float32
+                )
+                sums.append(x.reshape(sources, GROUP, 2 * receivers))
+            cross[:, at : at + pair_rows, :] = jnp.concatenate(sums, axis=1).astype(jnp.bfloat16)
         for c in range(2):
             turns = [cross[c * part + i].T for i in range(part)]
             left = jnp.concatenate(
@@ -231,13 +268,13 @@
                     departure(b, k, c).wait()
 
 
-def stack(distances, tour, place, steps, weights, table, pieces, previous, out_shape):
+def stack(distances, tour, place, steps, table, weights, pieces, previous, out_shape):
     blocks = len(distances)
     sources, rows, bins = pieces[0].shape
     receivers = weights.shape[1] // 2
     count = steps.shape[0]
     first = previous is None
-    args = [tour, place, steps, weights, table, *pieces] + ([] if first else [previous])
+    args = [tour, place, steps, table, weights, *pieces] + ([] if first else [previous])
     return pl.pallas_call(
         functools.partial(stack_kernel, distances, first),
         out_shape=out_shape,
@@ -247,7 +284,7 @@
         out_specs=pl.BlockSpec(memory_space=pl.ANY),
         scratch_shapes=[
             VMEM((blocks, 2, sources, rows, bins), jnp.bfloat16),
-            VMEM((sources, bins, 128), jnp.bfloat16),
+            VMEM((sources // 2, 2, bins, 128), jnp.bfloat16),
             VMEM((sources, bins, 2 * receivers), jnp.bfloat16),
             VMEM((blocks, sources, receivers, LAGS), jnp.bfloat16),
             pltpu.SemaphoreType.DMA((blocks, 2)),
@@ -287,28 +324,38 @@
     place[list(ring)] = np.arange(count)
     where = (jnp.asarray(np.asarray(ring, np.int32)), jnp.asarray(place))
 
-    forward = (send(same, 1), send(other, 1, True))
-    backward = (send(same, -1), send(other, -1, True))
+    half = count // 2
+    tie = lax.optimization_barrier
+    early = (send(same, 1), send(same, -1))
+    far_same = across(same)
     far_other = across(other)
-    far_same = across(same)
+    late = (send(other, 1, True), send(other, -1, True))
     weights = receiver_weights(same, other, far_same, far_other)
     run = functools.partial(
         stack,
         out_shape=jax.ShapeDtypeStruct((steps, channels // 2, channels, LAGS), jnp.bfloat16),
     )
-    rest = (*where, source_block, weights, table)
-    out = run((0,), *rest, (same, far_other), None)
-    half = count // 2
+    rest = (*where, source_block, table)
+    out = held = None
     for hop in range(1, half):
-        pieces = forward + backward
-        if hop < half - 1:
-            forward = tuple(send(x, 1) for x in forward)
-            backward = tuple(send(x, -1) for x in backward)
+        closing = hop == half - 1
+        if hop == 1:
+            early, weights = tie((early, weights))
         else:
-            forward = (send(forward[0], 1),)
-            backward = (send(backward[1], -1),)
-        out = run((-hop, hop), *rest, pieces, out)
-    return run((half,), *rest, forward + backward, out)
+            early, out = tie((early, out))
+        coming = (send(early[0], 1), None if closing else send(early[1], -1))
+        if hop > 1:
+            out = run((1 - hop, hop - 1), *rest, weights, held, out)
+            late, out = tie((late, out))
+        else:
+            late, weights = tie((late, weights))
+        held = (early[0], late[0], early[1], late[1])
+        later = (None if closing else send(late[0], 1), send(late[1], -1))
+        if hop == 1:
+            out = run((0,), *rest, weights, (same, far_other), None)
+        early, late = coming, later
+    out = run((1 - half, half - 1), *rest, weights, held, out)
+    return run((half,), *rest, weights, (early[0], late[1]), out)
 
 
 def solution(mesh):

time: 65.5 us -> 58.7 us (0.90)
  Pallas kernels: 26.9 us -> 19.6 us
  waiting for transfers between devices: 18.3 us -> 20.9 us
  starting transfers between devices: 17.9 us -> 15.8 us
    pallas_call x5, Pallas kernels: 18.7 us -> 12.2 us  [stack(): pl.pallas_call(functools.partial(stack_kernel, distances, first), out_sha...]
    ppermute x14, waiting for transfers between devices: 18.3 us -> 20.9 us  [send(): return lax.ppermute(x, ('chan', 'tm'), pairs)]
    ppermute x14, starting transfers between devices: 17.1 us -> 15.3 us  [send(): return lax.ppermute(x, ('chan', 'tm'), pairs)]
    pallas_call x1, Pallas kernels: 4.01 us -> 3.08 us  [whiten(): pl.pallas_call(whiten_kernel, out_shape=(piece, piece), in_specs=[pl.Bloc...]
  transfers between devices with their start and end apart: 16 -> 16, of which waited for: 5 -> 13; matrix products, arithmetic and copies ran while one was open for 0% -> 0% of each run, Pallas kernels for 28% -> 23%
where the time goes in v1:
time: 58.7 us; the launch traced here: 58.4 us
  waiting for transfers between devices  20.9 us (36%)
  Pallas kernels  19.6 us (33%)
  starting transfers between devices  15.8 us (27%)
  local copies, waits for them, and re-layouts  1.91 us (3%)
    ppermute x14, waiting for transfers between devices, send(): return lax.ppermute(x, ('chan', 'tm'), pairs)  20.9 us
    ppermute x14, starting transfers between devices, send(): return lax.ppermute(x, ('chan', 'tm'), pairs)  15.3 us
    pallas_call x5, Pallas kernels, stack(): pl.pallas_call(functools.partial(stack_kernel, distances, first), out_sha...  12.2 us
    pallas_call x1, Pallas kernels, receiver_weights(): pl.pallas_call(receiver_kernel, out_shape=jax.ShapeDtypeStruct((bins * 2...  4.33 us
    pallas_call x1, Pallas kernels, whiten(): pl.pallas_call(whiten_kernel, out_shape=(piece, piece), in_specs=[pl.Bloc...  3.08 us
    unnamed x12, local copies, waits for them, and re-layouts  1.91 us
  transfers between devices with their start and end apart: 16, of which 13 were waited for; matrix products, arithmetic and copies ran while one was open for 0% of the time, Pallas kernels for 23%

profile of v1, /device:TPU:0, one launch (start us, length us, event | category | flops | bytes accessed | tf_op | source)
XLA Modules:
  0.0 58.4 jit_solution(15537832136265773416)
XLA Ops:
  0.0 3.1 %whiten.1 = (bf16[32,32,128]{2,1,0:T(8,128)(2,1)}, bf16[32,32,128]{2,1,0:T(8,128)(2,1)}) custom-call(s32[64]{0:T(128)} %chan_mask.1, s32[16]{0:T(128)} %win_mask.1, bf16[64,32,128]{2,1,0:T(8,128)(2,1)} %bitcast.1), custom_call_target="tpu_custom_call" | custom-call | tf_op jit(solution)/shard_map/whiten/pallas_call | solution.py:123
  3.1 0.5 collective-permute-start.4
  3.6 3.0 %collective-permute-start.2 = (bf16[32,32,128]{2,1,0:T(8,128)(2,1)}, bf16[32,32,128]{2,1,0:T(8,128)(2,1)S(1)}, u32[]{:S(2)}, u32[]{:S(2)}) collective-permute-start(bf16[32,32,128]{2,1,0:T(8,128)(2,1)} %get-tuple-element.26.same.refs_0_), channel_id=1, source_target_pairs={{0,4},{1,5},{4,8},{5,9},{8,12},{9,13},{12,14},{13,15},{14,10},{15,... | collective-permute-start | bytes 786440 | tf_op jit(solution)/shard_map/ppermute | solution.py:320
  6.6 1.2 %collective-permute-start = (bf16[32,32,128]{2,1,0:T(8,128)(2,1)}, bf16[32,32,128]{2,1,0:T(8,128)(2,1)S(1)}, u32[]{:S(2)}, u32[]{:S(2)}) collective-permute-start(bf16[32,32,128]{2,1,0:T(8,128)(2,1)} %get-tuple-element.25.other), channel_id=1, source_target_pairs={{0,5},{1,4},{4,9},{5,8},{8,13},{9,12},{12,15},{13,14},{14,11},{15,... | collective-permute-start | bytes 786440 | tf_op jit(solution)/shard_map/ppermute | solution.py:320
  7.8 0.6 %collective-permute-start.1 = (bf16[32,32,128]{2,1,0:T(8,128)(2,1)}, bf16[32,32,128]{2,1,0:T(8,128)(2,1)S(1)}, u32[]{:S(2)}, u32[]{:S(2)}) collective-permute-start(bf16[32,32,128]{2,1,0:T(8,128)(2,1)} %get-tuple-element.25.other), channel_id=1, source_target_pairs={{0,3},{1,2},{4,1},{5,0},{8,5},{9,4},{12,9},{13,8},{14,13},{15,12},... | collective-permute-start | bytes 786440 | tf_op jit(solution)/shard_map/ppermute | solution.py:320
  8.4 0.9 %copy-done = bf16[32,32,128]{2,1,0:T(8,128)(2,1)S(1)} copy-done((bf16[32,32,128]{2,1,0:T(8,128)(2,1)S(1)}, bf16[32,32,128]{2,1,0:T(8,128)(2,1)}, u32[]{:S(2)}) %copy-start) | copy-done | bytes 262168
  9.3 0.9 %copy-done.1 = bf16[32,32,128]{2,1,0:T(8,128)(2,1)S(1)} copy-done((bf16[32,32,128]{2,1,0:T(8,128)(2,1)S(1)}, bf16[32,32,128]{2,1,0:T(8,128)(2,1)}, u32[]{:S(2)}) %copy-start.1) | copy-done | bytes 262168
  10.3 4.3 %receiver_weights.1.weights = bf16[8192,128]{1,0:T(8,128)(2,1)S(1)} custom-call(bf16[32,32,128]{2,1,0:T(8,128)(2,1)S(1)} %copy-done, bf16[32,32,128]{2,1,0:T(8,128)(2,1)S(1)} %copy-done.1, bf16[32,32,128]{2,1,0:T(8,128)(2,1)S(1)} %collective-permute-done.4.far_same, bf16[32,32,128]{2,1,0:T(8,128)(2,1)S(1)} %collective-permute-done.5.far_other.refs_1_), custom_call_target="tpu_custom_call" | custom-call | flops 2147483648 | bytes 12582912 | tf_op jit(solution)/shard_map/receiver_weights/pallas_call | solution.py:158
  14.6 1.4 %collective-permute-done.3.refs_2_ = bf16[32,32,128]{2,1,0:T(8,128)(2,1)S(1)} collective-permute-done((bf16[32,32,128]{2,1,0:T(8,128)(2,1)}, bf16[32,32,128]{2,1,0:T(8,128)(2,1)S(1)}, u32[]{:S(2)}, u32[]{:S(2)}) %collective-permute-start.3) | collective-permute-done | bytes 262176 | tf_op jit(solution)/shard_map/ppermute | solution.py:320
  16.0 2.4 %collective-permute-done.refs_1_ = bf16[32,32,128]{2,1,0:T(8,128)(2,1)S(1)} collective-permute-done((bf16[32,32,128]{2,1,0:T(8,128)(2,1)}, bf16[32,32,128]{2,1,0:T(8,128)(2,1)S(1)}, u32[]{:S(2)}, u32[]{:S(2)}) %collective-permute-start) | collective-permute-done | bytes 262176 | tf_op jit(solution)/shard_map/ppermute | solution.py:320
  18.4 0.9 %collective-permute-done.1.refs_3_ = bf16[32,32,128]{2,1,0:T(8,128)(2,1)S(1)} collective-permute-done((bf16[32,32,128]{2,1,0:T(8,128)(2,1)}, bf16[32,32,128]{2,1,0:T(8,128)(2,1)S(1)}, u32[]{:S(2)}, u32[]{:S(2)}) %collective-permute-start.1) | collective-permute-done | bytes 262176 | tf_op jit(solution)/shard_map/ppermute | solution.py:320
  19.3 1.6 %collective-permute-start.6 = (bf16[32,32,128]{2,1,0:T(8,128)(2,1)S(1)}, bf16[32,32,128]{2,1,0:T(8,128)(2,1)S(1)}, u32[]{:S(2)}, u32[]{:S(2)}) collective-permute-start(bf16[32,32,128]{2,1,0:T(8,128)(2,1)S(1)} %collective-permute-done.2.refs_0_), channel_id=1, source_target_pairs={{0,4},{1,5},{4,8},{5,9},{8,12},{9,13},{12,14},{13,15},{14,10},{15,... | collective-permute-start | bytes 786440 | tf_op jit(solution)/shard_map/ppermute | solution.py:320
  20.9 0.4 collective-permute-start.7
  21.3 1.6 %collective-permute-start.10 = (bf16[32,32,128]{2,1,0:T(8,128)(2,1)S(1)}, bf16[32,32,128]{2,1,0:T(8,128)(2,1)S(1)}, u32[]{:S(2)}, u32[]{:S(2)}) collective-permute-start(bf16[32,32,128]{2,1,0:T(8,128)(2,1)S(1)} %collective-permute-done.refs_1_), channel_id=1, source_target_pairs={{0,4},{1,5},{4,8},{5,9},{8,12},{9,13},{12,14},{13,15},{14,10},{15,... | collective-permute-start | bytes 786440 | tf_op jit(solution)/shard_map/ppermute | solution.py:320
  23.3 3.4 %stack.5.refs_4_ = bf16[4,32,64,128]{3,2,1,0:T(8,128)(2,1)} custom-call(s32[8]{0:T(128)S(1)} %copy-done.4, s32[8]{0:T(128)S(1)} %copy-done.5, s32[4]{0:T(128)S(1)} %copy-done.2, bf16[256,128]{1,0:T(8,128)(2,1)S(1)} %copy-done.3, bf16[8192,128]{1,0:T(8,128)(2,1)S(1)} %receiver_weights.1.weights, bf16[32,32,128]{2,1,0:T(8,128)(2,1)S(1)} %copy-done, ...), custom_call_target="tpu_custom_call" | custom-call | flops 3221225472 | bytes 1048576 | tf_op jit(solution)/shard_map/stack/pallas_call | solution.py:278
  26.7 1.7 %collective-permute-done.6.refs_0_ = bf16[32,32,128]{2,1,0:T(8,128)(2,1)S(1)} collective-permute-done((bf16[32,32,128]{2,1,0:T(8,128)(2,1)S(1)}, bf16[32,32,128]{2,1,0:T(8,128)(2,1)S(1)}, u32[]{:S(2)}, u32[]{:S(2)}) %collective-permute-start.6) | collective-permute-done | bytes 262176 | tf_op jit(solution)/shard_map/ppermute | solution.py:320
  28.4 1.6 %collective-permute-done.7.refs_2_ = bf16[32,32,128]{2,1,0:T(8,128)(2,1)S(1)} collective-permute-done((bf16[32,32,128]{2,1,0:T(8,128)(2,1)S(1)}, bf16[32,32,128]{2,1,0:T(8,128)(2,1)S(1)}, u32[]{:S(2)}, u32[]{:S(2)}) %collective-permute-start.7) | collective-permute-done | bytes 262176 | tf_op jit(solution)/shard_map/ppermute | solution.py:320
  30.0 1.6 %collective-permute-start.8 = (bf16[32,32,128]{2,1,0:T(8,128)(2,1)S(1)}, bf16[32,32,128]{2,1,0:T(8,128)(2,1)S(1)}, u32[]{:S(2)}, u32[]{:S(2)}) collective-permute-start(bf16[32,32,128]{2,1,0:T(8,128)(2,1)S(1)} %collective-permute-done.6.refs_0_), channel_id=1, source_target_pairs={{0,4},{1,5},{4,8},{5,9},{8,12},{9,13},{12,14},{13,15},{14,10},{15,... | collective-permute-start | bytes 786440 | tf_op jit(solution)/shard_map/ppermute | solution.py:320
  31.6 0.4 collective-permute-start.9
  32.1 0.8 %stack.6.refs_4_ = bf16[4,32,64,128]{3,2,1,0:T(8,128)(2,1)} custom-call(s32[8]{0:T(128)S(1)} %copy-done.4, s32[8]{0:T(128)S(1)} %copy-done.5, s32[4]{0:T(128)S(1)} %copy-done.2, bf16[256,128]{1,0:T(8,128)(2,1)S(1)} %copy-done.3, bf16[8192,128]{1,0:T(8,128)(2,1)S(1)} %receiver_weights.1.weights, ...), custom_call_target="tpu_custom_call", output_to_operand_aliasing={{}: (9, {})} | custom-call | flops 6442450944 | bytes 2097152 | tf_op jit(solution)/shard_map/stack/pallas_call | solution.py:278
  32.9 1.1 %collective-permute-done.10.refs_1_ = bf16[32,32,128]{2,1,0:T(8,128)(2,1)S(1)} collective-permute-done((bf16[32,32,128]{2,1,0:T(8,128)(2,1)S(1)}, bf16[32,32,128]{2,1,0:T(8,128)(2,1)S(1)}, u32[]{:S(2)}, u32[]{:S(2)}) %collective-permute-start.10) | collective-permute-done | bytes 262176 | tf_op jit(solution)/shard_map/ppermute | solution.py:320
  34.0 1.6 %collective-permute-done.11.refs_3_ = bf16[32,32,128]{2,1,0:T(8,128)(2,1)S(1)} collective-permute-done((bf16[32,32,128]{2,1,0:T(8,128)(2,1)S(1)}, bf16[32,32,128]{2,1,0:T(8,128)(2,1)S(1)}, u32[]{:S(2)}, u32[]{:S(2)}) %collective-permute-start.11) | collective-permute-done | bytes 262176 | tf_op jit(solution)/shard_map/ppermute | solution.py:320
  35.7 1.6 %collective-permute-start.13 = (bf16[32,32,128]{2,1,0:T(8,128)(2,1)S(1)}, bf16[32,32,128]{2,1,0:T(8,128)(2,1)S(1)}, u32[]{:S(2)}, u32[]{:S(2)}) collective-permute-start(bf16[32,32,128]{2,1,0:T(8,128)(2,1)S(1)} %collective-permute-done.10.refs_1_), channel_id=1, source_target_pairs={{0,4},{1,5},{4,8},{5,9},{8,12},{9,13},{12,14},{13,15},{14,10},{15,... | collective-permute-start | bytes 786440 | tf_op jit(solution)/shard_map/ppermute | solution.py:320
  37.2 0.8 %collective-permute-start.14 = (bf16[32,32,128]{2,1,0:T(8,128)(2,1)S(1)}, bf16[32,32,128]{2,1,0:T(8,128)(2,1)S(1)}, u32[]{:S(2)}, u32[]{:S(2)}) collective-permute-start(bf16[32,32,128]{2,1,0:T(8,128)(2,1)S(1)} %collective-permute-done.11.refs_3_), channel_id=1, source_target_pairs={{0,2},{1,3},{4,0},{5,1},{8,4},{9,5},{12,8},{13,9},{14,12},{15,13},... | collective-permute-start | bytes 786440 | tf_op jit(solution)/shard_map/ppermute | solution.py:320
  38.1 1.6 %collective-permute-done.8.refs_0_ = bf16[32,32,128]{2,1,0:T(8,128)(2,1)S(1)} collective-permute-done((bf16[32,32,128]{2,1,0:T(8,128)(2,1)S(1)}, bf16[32,32,128]{2,1,0:T(8,128)(2,1)S(1)}, u32[]{:S(2)}, u32[]{:S(2)}) %collective-permute-start.8) | collective-permute-done | bytes 262176 | tf_op jit(solution)/shard_map/ppermute | solution.py:320
  39.7 1.6 %collective-permute-done.9.refs_2_ = bf16[32,32,128]{2,1,0:T(8,128)(2,1)S(1)} collective-permute-done((bf16[32,32,128]{2,1,0:T(8,128)(2,1)S(1)}, bf16[32,32,128]{2,1,0:T(8,128)(2,1)S(1)}, u32[]{:S(2)}, u32[]{:S(2)}) %collective-permute-start.9) | collective-permute-done | bytes 262176 | tf_op jit(solution)/shard_map/ppermute | solution.py:320
  41.3 3.8 %stack.7.refs_4_ = bf16[4,32,64,128]{3,2,1,0:T(8,128)(2,1)} custom-call(s32[8]{0:T(128)S(1)} %copy-done.4, s32[8]{0:T(128)S(1)} %copy-done.5, s32[4]{0:T(128)S(1)} %copy-done.2, bf16[256,128]{1,0:T(8,128)(2,1)S(1)} %copy-done.3, bf16[8192,128]{1,0:T(8,128)(2,1)S(1)} %receiver_weights.1.weights, ...), custom_call_target="tpu_custom_call", output_to_operand_aliasing={{}: (9, {})} | custom-call | flops 6442450944 | bytes 2097152 | tf_op jit(solution)/shard_map/stack/pallas_call | solution.py:278
  45.3 1.4 %collective-permute-done.14.refs_3_ = bf16[32,32,128]{2,1,0:T(8,128)(2,1)S(1)} collective-permute-done((bf16[32,32,128]{2,1,0:T(8,128)(2,1)S(1)}, bf16[32,32,128]{2,1,0:T(8,128)(2,1)S(1)}, u32[]{:S(2)}, u32[]{:S(2)}) %collective-permute-start.14) | collective-permute-done | bytes 262176 | tf_op jit(solution)/shard_map/ppermute | solution.py:320
  47.1 1.6 %collective-permute-start.12 = (bf16[32,32,128]{2,1,0:T(8,128)(2,1)S(1)}, bf16[32,32,128]{2,1,0:T(8,128)(2,1)S(1)}, u32[]{:S(2)}, u32[]{:S(2)}) collective-permute-start(bf16[32,32,128]{2,1,0:T(8,128)(2,1)S(1)} %collective-permute-done.8.refs_0_), channel_id=1, source_target_pairs={{0,4},{1,5},{4,8},{5,9},{8,12},{9,13},{12,14},{13,15},{14,10},{15,... | collective-permute-start | bytes 786440 | tf_op jit(solution)/shard_map/ppermute | solution.py:320
  48.7 0.8 %stack.8.refs_2_ = bf16[4,32,64,128]{3,2,1,0:T(8,128)(2,1)} custom-call(s32[8]{0:T(128)S(1)} %copy-done.4, s32[8]{0:T(128)S(1)} %copy-done.5, s32[4]{0:T(128)S(1)} %copy-done.2, bf16[256,128]{1,0:T(8,128)(2,1)S(1)} %copy-done.3, bf16[8192,128]{1,0:T(8,128)(2,1)S(1)} %receiver_weights.1.weights, ...), custom_call_target="tpu_custom_call", output_to_operand_aliasing={{}: (9, {})} | custom-call | flops 6442450944 | bytes 2097152 | tf_op jit(solution)/shard_map/stack/pallas_call | solution.py:278
  49.5 5.2 %collective-permute-done.15.refs_1_ = bf16[32,32,128]{2,1,0:T(8,128)(2,1)S(1)} collective-permute-done((bf16[32,32,128]{2,1,0:T(8,128)(2,1)S(1)}, bf16[32,32,128]{2,1,0:T(8,128)(2,1)S(1)}, u32[]{:S(2)}, u32[]{:S(2)}) %collective-permute-start.15) | collective-permute-done | bytes 262176 | tf_op jit(solution)/shard_map/ppermute | solution.py:320
  54.9 3.4 %stack.9 = bf16[4,32,64,128]{3,2,1,0:T(8,128)(2,1)} custom-call(s32[8]{0:T(128)S(1)} %copy-done.4, s32[8]{0:T(128)S(1)} %copy-done.5, s32[4]{0:T(128)S(1)} %copy-done.2, bf16[256,128]{1,0:T(8,128)(2,1)S(1)} %copy-done.3, bf16[8192,128]{1,0:T(8,128)(2,1)S(1)} %receiver_weights.1.weights, ...), custom_call_target="tpu_custom_call", output_to_operand_aliasing={{}: (7, {})} | custom-call | flops 3221225472 | bytes 1048576 | tf_op jit(solution)/shard_map/stack/pallas_call | solution.py:278
  (19 shorter events, 1.4 us)
Async XLA Ops:
  0.0 23.3 %copy-start.3 = (bf16[256,128]{1,0:T(8,128)(2,1)S(1)}, bf16[256,128]{1,0:T(8,128)(2,1)}, u32[]{:S(2)}) copy-start(bf16[256,128]{1,0:T(8,128)(2,1)} %constant.9.table) | copy-start | bytes 196612
  3.1 4.7 %collective-permute-start.4 = (bf16[32,32,128]{2,1,0:T(8,128)(2,1)}, bf16[32,32,128]{2,1,0:T(8,128)(2,1)S(1)}, u32[]{:S(2)}, u32[]{:S(2)}) collective-permute-start(bf16[32,32,128]{2,1,0:T(8,128)(2,1)} %get-tuple-element.26.same.refs_0_), channel_id=1, source_target_pairs={{0,1},{1,0},{2,3},{3,2},{4,5},{5,4},{6,7},{7,6},{8,9},{9,8},{10,11... | collective-permute-start | bytes 786440 | tf_op jit(solution)/shard_map/ppermute | solution.py:312
  3.5 19.8 %copy-start.2 = (s32[4]{0:T(128)S(1)}, s32[4]{0:T(128)}, u32[]{:S(2)}) copy-start(s32[4]{0:T(128)} %steps.9) | copy-start | bytes 52
  3.5 19.8 %copy-start.4 = (s32[8]{0:T(128)S(1)}, s32[8]{0:T(128)}, u32[]{:S(2)}) copy-start(s32[8]{0:T(128)} %constant.7.clone.tour) | copy-start | bytes 100
  3.5 19.8 %copy-start.5 = (s32[8]{0:T(128)S(1)}, s32[8]{0:T(128)}, u32[]{:S(2)}) copy-start(s32[8]{0:T(128)} %constant.8.clone.place) | copy-start | bytes 100
  3.5 4.8 %collective-permute-start.5 = (bf16[32,32,128]{2,1,0:T(8,128)(2,1)}, bf16[32,32,128]{2,1,0:T(8,128)(2,1)S(1)}, u32[]{:S(2)}, u32[]{:S(2)}) collective-permute-start(bf16[32,32,128]{2,1,0:T(8,128)(2,1)} %get-tuple-element.25.other), channel_id=1, source_target_pairs={{0,1},{1,0},{2,3},{3,2},{4,5},{5,4},{6,7},{7,6},{8,9},{9,8},{10,11... | collective-permute-start | bytes 786440 | tf_op jit(solution)/shard_map/ppermute | solution.py:312
  3.6 11.0 %collective-permute-start.2 = (bf16[32,32,128]{2,1,0:T(8,128)(2,1)}, bf16[32,32,128]{2,1,0:T(8,128)(2,1)S(1)}, u32[]{:S(2)}, u32[]{:S(2)}) collective-permute-start(bf16[32,32,128]{2,1,0:T(8,128)(2,1)} %get-tuple-element.26.same.refs_0_), channel_id=1, source_target_pairs={{0,4},{1,5},{4,8},{5,9},{8,12},{9,13},{12,14},{13,15},{14,10},{15,... | collective-permute-start | bytes 786440 | tf_op jit(solution)/shard_map/ppermute | solution.py:320
  6.6 9.4 %collective-permute-start.3 = (bf16[32,32,128]{2,1,0:T(8,128)(2,1)}, bf16[32,32,128]{2,1,0:T(8,128)(2,1)S(1)}, u32[]{:S(2)}, u32[]{:S(2)}) collective-permute-start(bf16[32,32,128]{2,1,0:T(8,128)(2,1)} %get-tuple-element.26.same.refs_0_), channel_id=1, source_target_pairs={{0,2},{1,3},{4,0},{5,1},{8,4},{9,5},{12,8},{13,9},{14,12},{15,13},... | collective-permute-start | bytes 786440 | tf_op jit(solution)/shard_map/ppermute | solution.py:320
  6.6 11.8 %collective-permute-start = (bf16[32,32,128]{2,1,0:T(8,128)(2,1)}, bf16[32,32,128]{2,1,0:T(8,128)(2,1)S(1)}, u32[]{:S(2)}, u32[]{:S(2)}) collective-permute-start(bf16[32,32,128]{2,1,0:T(8,128)(2,1)} %get-tuple-element.25.other), channel_id=1, source_target_pairs={{0,5},{1,4},{4,9},{5,8},{8,13},{9,12},{12,15},{13,14},{14,11},{15,... | collective-permute-start | bytes 786440 | tf_op jit(solution)/shard_map/ppermute | solution.py:320
  7.8 11.5 %collective-permute-start.1 = (bf16[32,32,128]{2,1,0:T(8,128)(2,1)}, bf16[32,32,128]{2,1,0:T(8,128)(2,1)S(1)}, u32[]{:S(2)}, u32[]{:S(2)}) collective-permute-start(bf16[32,32,128]{2,1,0:T(8,128)(2,1)} %get-tuple-element.25.other), channel_id=1, source_target_pairs={{0,3},{1,2},{4,1},{5,0},{8,5},{9,4},{12,9},{13,8},{14,13},{15,12},... | collective-permute-start | bytes 786440 | tf_op jit(solution)/shard_map/ppermute | solution.py:320
  8.4 1.0 %copy-start = (bf16[32,32,128]{2,1,0:T(8,128)(2,1)S(1)}, bf16[32,32,128]{2,1,0:T(8,128)(2,1)}, u32[]{:S(2)}) copy-start(bf16[32,32,128]{2,1,0:T(8,128)(2,1)} %get-tuple-element.26.same.refs_0_) | copy-start | bytes 786436
  9.3 0.9 %copy-start.1 = (bf16[32,32,128]{2,1,0:T(8,128)(2,1)S(1)}, bf16[32,32,128]{2,1,0:T(8,128)(2,1)}, u32[]{:S(2)}) copy-start(bf16[32,32,128]{2,1,0:T(8,128)(2,1)} %get-tuple-element.25.other) | copy-start | bytes 786436
  19.3 9.1 %collective-permute-start.6 = (bf16[32,32,128]{2,1,0:T(8,128)(2,1)S(1)}, bf16[32,32,128]{2,1,0:T(8,128)(2,1)S(1)}, u32[]{:S(2)}, u32[]{:S(2)}) collective-permute-start(bf16[32,32,128]{2,1,0:T(8,128)(2,1)S(1)} %collective-permute-done.2.refs_0_), channel_id=1, source_target_pairs={{0,4},{1,5},{4,8},{5,9},{8,12},{9,13},{12,14},{13,15},{14,10},{15,... | collective-permute-start | bytes 786440 | tf_op jit(solution)/shard_map/ppermute | solution.py:320
  20.9 9.2 %collective-permute-start.7 = (bf16[32,32,128]{2,1,0:T(8,128)(2,1)S(1)}, bf16[32,32,128]{2,1,0:T(8,128)(2,1)S(1)}, u32[]{:S(2)}, u32[]{:S(2)}) collective-permute-start(bf16[32,32,128]{2,1,0:T(8,128)(2,1)S(1)} %collective-permute-done.3.refs_2_), channel_id=1, source_target_pairs={{0,2},{1,3},{4,0},{5,1},{8,4},{9,5},{12,8},{13,9},{14,12},{15,13},... | collective-permute-start | bytes 786440 | tf_op jit(solution)/shard_map/ppermute | solution.py:320
  21.3 12.7 %collective-permute-start.10 = (bf16[32,32,128]{2,1,0:T(8,128)(2,1)S(1)}, bf16[32,32,128]{2,1,0:T(8,128)(2,1)S(1)}, u32[]{:S(2)}, u32[]{:S(2)}) collective-permute-start(bf16[32,32,128]{2,1,0:T(8,128)(2,1)S(1)} %collective-permute-done.refs_1_), channel_id=1, source_target_pairs={{0,4},{1,5},{4,8},{5,9},{8,12},{9,13},{12,14},{13,15},{14,10},{15,... | collective-permute-start | bytes 786440 | tf_op jit(solution)/shard_map/ppermute | solution.py:320
  22.9 12.8 %collective-permute-start.11 = (bf16[32,32,128]{2,1,0:T(8,128)(2,1)S(1)}, bf16[32,32,128]{2,1,0:T(8,128)(2,1)S(1)}, u32[]{:S(2)}, u32[]{:S(2)}) collective-permute-start(bf16[32,32,128]{2,1,0:T(8,128)(2,1)S(1)} %collective-permute-done.1.refs_3_), channel_id=1, source_target_pairs={{0,2},{1,3},{4,0},{5,1},{8,4},{9,5},{12,8},{13,9},{14,12},{15,13},... | collective-permute-start | bytes 786440 | tf_op jit(solution)/shard_map/ppermute | solution.py:320
  30.0 9.6 %collective-permute-start.8 = (bf16[32,32,128]{2,1,0:T(8,128)(2,1)S(1)}, bf16[32,32,128]{2,1,0:T(8,128)(2,1)S(1)}, u32[]{:S(2)}, u32[]{:S(2)}) collective-permute-start(bf16[32,32,128]{2,1,0:T(8,128)(2,1)S(1)} %collective-permute-done.6.refs_0_), channel_id=1, source_target_pairs={{0,4},{1,5},{4,8},{5,9},{8,12},{9,13},{12,14},{13,15},{14,10},{15,... | collective-permute-start | bytes 786440 | tf_op jit(solution)/shard_map/ppermute | solution.py:320
  31.6 9.7 %collective-permute-start.9 = (bf16[32,32,128]{2,1,0:T(8,128)(2,1)S(1)}, bf16[32,32,128]{2,1,0:T(8,128)(2,1)S(1)}, u32[]{:S(2)}, u32[]{:S(2)}) collective-permute-start(bf16[32,32,128]{2,1,0:T(8,128)(2,1)S(1)} %collective-permute-done.7.refs_2_), channel_id=1, source_target_pairs={{0,2},{1,3},{4,0},{5,1},{8,4},{9,5},{12,8},{13,9},{14,12},{15,13},... | collective-permute-start | bytes 786440 | tf_op jit(solution)/shard_map/ppermute | solution.py:320
  35.7 9.6 %collective-permute-start.13 = (bf16[32,32,128]{2,1,0:T(8,128)(2,1)S(1)}, bf16[32,32,128]{2,1,0:T(8,128)(2,1)S(1)}, u32[]{:S(2)}, u32[]{:S(2)}) collective-permute-start(bf16[32,32,128]{2,1,0:T(8,128)(2,1)S(1)} %collective-permute-done.10.refs_1_), channel_id=1, source_target_pairs={{0,4},{1,5},{4,8},{5,9},{8,12},{9,13},{12,14},{13,15},{14,10},{15,... | collective-permute-start | bytes 786440 | tf_op jit(solution)/shard_map/ppermute | solution.py:320
  37.2 9.4 %collective-permute-start.14 = (bf16[32,32,128]{2,1,0:T(8,128)(2,1)S(1)}, bf16[32,32,128]{2,1,0:T(8,128)(2,1)S(1)}, u32[]{:S(2)}, u32[]{:S(2)}) collective-permute-start(bf16[32,32,128]{2,1,0:T(8,128)(2,1)S(1)} %collective-permute-done.11.refs_3_), channel_id=1, source_target_pairs={{0,2},{1,3},{4,0},{5,1},{8,4},{9,5},{12,8},{13,9},{14,12},{15,13},... | collective-permute-start | bytes 786440 | tf_op jit(solution)/shard_map/ppermute | solution.py:320
  46.7 8.1 %collective-permute-start.15 = (bf16[32,32,128]{2,1,0:T(8,128)(2,1)S(1)}, bf16[32,32,128]{2,1,0:T(8,128)(2,1)S(1)}, u32[]{:S(2)}, u32[]{:S(2)}) collective-permute-start(bf16[32,32,128]{2,1,0:T(8,128)(2,1)S(1)} %collective-permute-done.14.refs_3_), channel_id=1, source_target_pairs={{0,2},{1,3},{4,0},{5,1},{8,4},{9,5},{12,8},{13,9},{14,12},{15,13},... | collective-permute-start | bytes 786440 | tf_op jit(solution)/shard_map/ppermute | solution.py:320
  47.1 7.8 %collective-permute-start.12 = (bf16[32,32,128]{2,1,0:T(8,128)(2,1)S(1)}, bf16[32,32,128]{2,1,0:T(8,128)(2,1)S(1)}, u32[]{:S(2)}, u32[]{:S(2)}) collective-permute-start(bf16[32,32,128]{2,1,0:T(8,128)(2,1)S(1)} %collective-permute-done.8.refs_0_), channel_id=1, source_target_pairs={{0,4},{1,5},{4,8},{5,9},{8,12},{9,13},{12,14},{13,15},{14,10},{15,... | collective-permute-start | bytes 786440 | tf_op jit(solution)/shard_map/ppermute | solution.py:320

commit v2 on v1

--- a/solution.py
+++ b/solution.py
@@ -19,6 +19,7 @@
 
 VMEM = pltpu.VMEM
 SMEM = pltpu.SMEM
+SMALL = pl.CostEstimate(flops=1 << 20, bytes_accessed=1 << 14, transcendentals=0)
 
 
 def ring_order(mesh):
@@ -59,11 +60,17 @@
     )
 
 
-def whiten_kernel(chan_mask, win_mask, spectra, same, other):
+def whiten_kernel(chan_mask, win_mask, spectra, same, other, held, sems):
     rows, bins = spectra.shape[1:]
     half = same.shape[0]
-    mine = lax.axis_index("tm") * half
-    theirs = half - mine
+    own = lax.axis_index("tm") * half
+    starts = (own, half - own)
+    copies = [
+        pltpu.make_async_copy(spectra.at[pl.ds(start, half)], held.at[i], sems.at[i])
+        for i, start in enumerate(starts)
+    ]
+    for copy in copies:
+        copy.start()
     row = lax.broadcasted_iota(jnp.int32, (rows, bins), 0)
     keep = jnp.zeros((rows, bins), jnp.float32)
     for w in range(rows // 2):
@@ -81,8 +88,8 @@
         last = square.shape[0] - 1
         return square + jnp.where(even, pltpu.roll(square, last, 0), pltpu.roll(square, 1, 0))
 
-    def whitened(channels):
-        values = jnp.concatenate([spectra[c].astype(jnp.float32) for c in channels])
+    def whitened(side, channels):
+        values = jnp.concatenate([held[side, c].astype(jnp.float32) for c in channels])
         square = values * values
         power = jnp.concatenate(
             [with_partner(square[i : i + 8]) for i in range(0, square.shape[0], 8)]
@@ -100,47 +107,58 @@
             )
             / 5.0
         )
-        kept = jnp.concatenate([keep * chan_mask[c].astype(jnp.float32) for c in channels])
+        kept = jnp.concatenate([keep * chan_mask[starts[side] + c].astype(jnp.float32) for c in channels])
         return values * (kept / (smoothed + WATER))
 
-    def step(i, _):
-        for start, piece in ((mine, same), (theirs, other)):
-            values = whitened([start + i * BATCH + j for j in range(BATCH)])
+    for side, piece in enumerate((same, other)):
+        copies[side].wait()
+        for i in range(0, half, BATCH):
+            values = whitened(side, range(i, i + BATCH))
             for j in range(0, BATCH, 2):
                 pair = interleave(
                     values[j * rows : (j + 1) * rows], values[(j + 1) * rows : (j + 2) * rows]
                 )
-                piece[i * BATCH + j] = pair[0].astype(jnp.bfloat16)
-                piece[i * BATCH + j + 1] = pair[1].astype(jnp.bfloat16)
-        return 0
-
-    lax.fori_loop(0, half // BATCH, step, 0, unroll=2)
+                piece[i + j] = pair[0].astype(jnp.bfloat16)
+                piece[i + j + 1] = pair[1].astype(jnp.bfloat16)
 
 
 def whiten(spectra, chan_mask, win_mask):
     channels, rows, bins = spectra.shape
-    piece = jax.ShapeDtypeStruct((channels // 2, rows, bins), jnp.bfloat16)
+    piece = VMEM((channels // 2, rows, bins), jnp.bfloat16)
     return pl.pallas_call(
         whiten_kernel,
         out_shape=(piece, piece),
         in_specs=[
             pl.BlockSpec(memory_space=SMEM),
             pl.BlockSpec(memory_space=SMEM),
-            pl.BlockSpec(memory_space=VMEM),
+            pl.BlockSpec(memory_space=pl.ANY),
         ],
         out_specs=(pl.BlockSpec(memory_space=VMEM),) * 2,
+        scratch_shapes=[
+            VMEM((2, channels // 2, rows, bins), jnp.bfloat16),
+            pltpu.SemaphoreType.DMA((2,)),
+        ],
+        cost_estimate=SMALL,
         name="whiten",
     )(chan_mask, win_mask, spectra)
 
 
-def receiver_kernel(same, other, far_same, far_other, weights, flat, wide):
+def receiver_kernel(same, other, far_same, far_other, weights, flat, wide, held, sems):
     half, rows, bins = same.shape
+    copies = [
+        pltpu.make_async_copy(piece, held.at[i], sems.at[i])
+        for i, piece in enumerate((same, far_other, other, far_same))
+    ]
+    for copy in copies:
+        copy.start()
     mine = lax.axis_index("tm") * half
     theirs = half - mine
     deep = 2 * rows
-    for i in range(0, half, 2):
-        for start, sides in ((mine, (same, far_other)), (theirs, (other, far_same))):
-            for h, piece in enumerate(sides):
+    for side, start in enumerate((mine, theirs)):
+        for h in range(2):
+            copies[2 * side + h].wait()
+            piece = held.at[2 * side + h]
+            for i in range(0, half, 2):
                 pair = interleave(piece[i].astype(jnp.float32), piece[i + 1].astype(jnp.float32))
                 for j in range(2):
                     at = pl.multiple_of((start + i + j) * deep + h * rows, rows)
@@ -158,26 +176,29 @@
     return pl.pallas_call(
         receiver_kernel,
         out_shape=jax.ShapeDtypeStruct((bins * 2 * rows, 4 * half), jnp.bfloat16),
-        in_specs=[pl.BlockSpec(memory_space=VMEM)] * 4,
+        in_specs=[pl.BlockSpec(memory_space=pl.ANY)] * 4,
         out_specs=pl.BlockSpec(memory_space=VMEM),
         scratch_shapes=[
             VMEM((2 * half * 2 * rows, bins), jnp.float32),
             VMEM((bins * 2 * rows, 4 * half), jnp.float32),
+            VMEM((4, half, rows, bins), jnp.bfloat16),
+            pltpu.SemaphoreType.DMA((4,)),
         ],
         compiler_params=pltpu.CompilerParams(vmem_limit_bytes=24 << 20),
-        cost_estimate=pl.CostEstimate(flops=2 << 30, bytes_accessed=12 << 20, transcendentals=0),
+        cost_estimate=SMALL,
         name="receiver_weights",
     )(same, other, far_same, far_other)
 
 
-def stack_kernel(distances, first, tour, place, steps, table, weights, *refs):
+def stack_kernel(tour, distances, first, steps, table, weights, *refs):
     blocks = len(distances)
     pieces = refs[: 2 * blocks]
     out = refs[2 * blocks + (0 if first else 1)]
     src, turned, cross, done, in_sem, out_sem = refs[2 * blocks + (1 if first else 2) :]
-    sources, rows, bins = src.shape[2:]
+    sources, rows, bins = pieces[0].shape
     count = steps.shape[0]
-    ring = tour.shape[0]
+    ring = len(tour)
+    staged = blocks > 1 or first
     lanes = 2 * rows
     per_tile = 128 // lanes
     tiles = GROUP // per_tile
@@ -186,8 +207,15 @@
     row = lax.broadcasted_iota(jnp.int32, (pair_rows, 128), 0) % GROUP
     col = lax.broadcasted_iota(jnp.int32, (pair_rows, 128), 1) // lanes
     receivers = weights.shape[1] // 2
-    me = place[lax.axis_index("chan")]
-    owners = [tour[lax.rem(me + d + ring, ring)] for d in distances]
+    me = lax.axis_index("chan")
+    folded = tour[1] == 2
+
+    def owner_at(distance):
+        at = jnp.where(me % 2 == 0, me // 2, ring - 1 - me // 2) if folded else me
+        at = lax.rem(at + distance + ring, ring)
+        return jnp.where(at < ring // 2, 2 * at, 2 * (ring - 1 - at) + 1) if folded else at
+
+    owners = [owner_at(d) for d in distances]
     needed = [
         functools.reduce(jnp.logical_or, [steps[k] == owner for k in range(count)])
         for owner in owners
@@ -197,7 +225,7 @@
     def arrival(b, h):
         return pltpu.make_async_copy(pieces[2 * b + h], src.at[b, h], in_sem.at[b, h])
 
-    for b in range(blocks):
+    for b in range(blocks if staged else 0):
         @pl.when(needed[b])
         def _(b=b):
             for h in range(2):
@@ -210,7 +238,8 @@
 
     def compute(b, owner):
         for s in range(sources):
-            turned[s // 2, s % 2] = jnp.concatenate([src[b, 0, s], src[b, 1, s]] * per_tile).T
+            parts = (src[b, 0, s], src[b, 1, s]) if staged else (pieces[0][s], pieces[1][s])
+            turned[s // 2, s % 2] = jnp.concatenate(parts * per_tile).T
         for m in range(bins // pair_rows):
             at = m * pair_rows
             sums = []
@@ -251,7 +280,7 @@
 
         @pl.when(jnp.where(later, needed[-1], needed[0]))
         def _():
-            for i in range(blocks):
+            for i in range(blocks if staged else 0):
                 @pl.when(b == i)
                 def _(i=i):
                     for h in range(2):
@@ -268,19 +297,23 @@
                     departure(b, k, c).wait()
 
 
-def stack(distances, tour, place, steps, table, weights, pieces, previous, out_shape):
+def stack(distances, tour, steps, table, weights, pieces, previous, out_shape):
     blocks = len(distances)
     sources, rows, bins = pieces[0].shape
     receivers = weights.shape[1] // 2
     count = steps.shape[0]
     first = previous is None
-    args = [tour, place, steps, table, weights, *pieces] + ([] if first else [previous])
+    if first:
+        kinds = [pl.ANY, pl.ANY]
+    else:
+        kinds = [VMEM if blocks == 1 else pl.ANY] * len(pieces) + [pl.ANY]
+    args = [steps, table, weights, *pieces] + ([] if first else [previous])
     return pl.pallas_call(
-        functools.partial(stack_kernel, distances, first),
+        functools.partial(stack_kernel, tour, distances, first),
         out_shape=out_shape,
-        in_specs=[pl.BlockSpec(memory_space=SMEM)] * 3
+        in_specs=[pl.BlockSpec(memory_space=SMEM)]
         + [pl.BlockSpec(memory_space=VMEM)] * 2
-        + [pl.BlockSpec(memory_space=pl.ANY)] * (len(args) - 5),
+        + [pl.BlockSpec(memory_space=kind) for kind in kinds],
         out_specs=pl.BlockSpec(memory_space=pl.ANY),
         scratch_shapes=[
             VMEM((blocks, 2, sources, rows, bins), jnp.bfloat16),
@@ -292,9 +325,7 @@
         ],
         input_output_aliases={} if first else {len(args) - 1: 0},
         compiler_params=pltpu.CompilerParams(vmem_limit_bytes=24 << 20),
-        cost_estimate=pl.CostEstimate(
-            flops=blocks * (3 << 30), bytes_accessed=blocks << 20, transcendentals=0
-        ),
+        cost_estimate=SMALL,
         name="stack",
     )(*args)
 
@@ -304,9 +335,8 @@
     channels, windows, parts, bins = spectra.shape
     steps = source_block.shape[0]
     halves = lax.axis_size("tm")
-    same, other = whiten(
-        spectra.reshape(channels, windows * parts, bins), channel_mask, window_mask
-    )
+    rows = spectra.reshape(channels, windows * parts, bins)
+    same, other = whiten(rows, channel_mask, window_mask)
 
     def across(x):
         return lax.ppermute(x, "tm", [(0, 1), (1, 0)])
@@ -320,9 +350,6 @@
         return lax.ppermute(x, ("chan", "tm"), pairs)
 
     table = lag_tables(windows * halves, bins)
-    place = np.zeros(count, np.int32)
-    place[list(ring)] = np.arange(count)
-    where = (jnp.asarray(np.asarray(ring, np.int32)), jnp.asarray(place))
 
     half = count // 2
     tie = lax.optimization_barrier
@@ -335,8 +362,9 @@
         stack,
         out_shape=jax.ShapeDtypeStruct((steps, channels // 2, channels, LAGS), jnp.bfloat16),
     )
-    rest = (*where, source_block, table)
-    out = held = None
+    rest = (tuple(ring), source_block, table)
+    out = None
+    held = []
     for hop in range(1, half):
         closing = hop == half - 1
         if hop == 1:
@@ -344,17 +372,18 @@
         else:
             early, out = tie((early, out))
         coming = (send(early[0], 1), None if closing else send(early[1], -1))
-        if hop > 1:
-            out = run((1 - hop, hop - 1), *rest, weights, held, out)
-            late, out = tie((late, out))
-        else:
+        if hop == 1:
             late, weights = tie((late, weights))
-        held = (early[0], late[0], early[1], late[1])
+        held.append((early[0], late[0], early[1], late[1]))
         later = (None if closing else send(late[0], 1), send(late[1], -1))
         if hop == 1:
             out = run((0,), *rest, weights, (same, far_other), None)
+        elif not closing:
+            late, out = tie((late, out))
+            out = run((1 - hop, hop - 1), *rest, weights, held[hop - 2], out)
         early, late = coming, later
-    out = run((1 - half, half - 1), *rest, weights, held, out)
+    for hop in range(half - 2, half):
+        out = run((-hop, hop), *rest, weights, held[hop - 1], out)
     return run((half,), *rest, weights, (early[0], late[1]), out)
 
 

time: 58.7 us -> 53.6 us (0.913)
  waiting for transfers between devices: 20.9 us -> 17.9 us
  local copies, waits for them, and re-layouts: 1.91 us -> 0.01 us
    ppermute x14, waiting for transfers between devices: 20.9 us -> 17.9 us  [send(): return lax.ppermute(x, ('chan', 'tm'), pairs)]
    unnamed x12 -> x4, local copies, waits for them, and re-layouts: 1.91 us -> 0.01 us
  transfers between devices with their start and end apart: 16 -> 16, of which waited for: 13 -> 10; matrix products, arithmetic and copies ran while one was open for 0% -> 0% of each run, Pallas kernels for 23% -> 25%
where the time goes in v2:
time: 53.6 us; the launch traced here: 53.3 us
  Pallas kernels  19.7 us (37%)
  waiting for transfers between devices  17.9 us (33%)
  starting transfers between devices  15.4 us (29%)
    ppermute x14, waiting for transfers between devices, send(): return lax.ppermute(x, ('chan', 'tm'), pairs)  17.9 us
    ppermute x14, starting transfers between devices, send(): return lax.ppermute(x, ('chan', 'tm'), pairs)  14.8 us
    pallas_call x5, Pallas kernels, stack(): pl.pallas_call(functools.partial(stack_kernel, tour, distances, first), o...  12.1 us
    pallas_call x1, Pallas kernels, receiver_weights(): pl.pallas_call(receiver_kernel, out_shape=jax.ShapeDtypeStruct((bins * 2...  4.65 us
    pallas_call x1, Pallas kernels, whiten(): pl.pallas_call(whiten_kernel, out_shape=(piece, piece), in_specs=[pl.Bloc...  2.99 us
  transfers between devices with their start and end apart: 16, of which 10 were waited for; matrix products, arithmetic and copies ran while one was open for 0% of the time, Pallas kernels for 25%

profile of v2, /device:TPU:0, one launch (start us, length us, event | category | flops | bytes accessed | tf_op | source)
XLA Modules:
  0.0 53.3 jit_solution(17531726104113055198)
XLA Ops:
  0.0 3.0 %whiten.1 = (bf16[32,32,128]{2,1,0:T(8,128)(2,1)S(1)}, bf16[32,32,128]{2,1,0:T(8,128)(2,1)S(1)}) custom-call(s32[64]{0:T(128)} %chan_mask.1, s32[16]{0:T(128)} %win_mask.1, bf16[64,32,128]{2,1,0:T(8,128)(2,1)} %bitcast.1), custom_call_target="tpu_custom_call" | custom-call | flops 1048576 | bytes 16384 | tf_op jit(solution)/shard_map/whiten/pallas_call | solution.py:128
  3.0 0.5 collective-permute-start.4
  3.5 0.1 collective-permute-start.5
  3.6 3.0 %collective-permute-start.2 = (bf16[32,32,128]{2,1,0:T(8,128)(2,1)S(1)}, bf16[32,32,128]{2,1,0:T(8,128)(2,1)S(1)}, u32[]{:S(2)}, u32[]{:S(2)}) collective-permute-start(bf16[32,32,128]{2,1,0:T(8,128)(2,1)S(1)} %get-tuple-element.21.same.refs_0_), channel_id=1, source_target_pairs={{0,4},{1,5},{4,8},{5,9},{8,12},{9,13},{12,14},{13,15},{14,10},{15,... | collective-permute-start | bytes 786440 | tf_op jit(solution)/shard_map/ppermute | solution.py:350
  6.6 0.0 collective-permute-start.3
  6.6 1.1 %collective-permute-start = (bf16[32,32,128]{2,1,0:T(8,128)(2,1)S(1)}, bf16[32,32,128]{2,1,0:T(8,128)(2,1)S(1)}, u32[]{:S(2)}, u32[]{:S(2)}) collective-permute-start(bf16[32,32,128]{2,1,0:T(8,128)(2,1)S(1)} %get-tuple-element.20.other), channel_id=1, source_target_pairs={{0,5},{1,4},{4,9},{5,8},{8,13},{9,12},{12,15},{13,14},{14,11},{15,... | collective-permute-start | bytes 786440 | tf_op jit(solution)/shard_map/ppermute | solution.py:350
  7.8 0.6 %collective-permute-start.1 = (bf16[32,32,128]{2,1,0:T(8,128)(2,1)S(1)}, bf16[32,32,128]{2,1,0:T(8,128)(2,1)S(1)}, u32[]{:S(2)}, u32[]{:S(2)}) collective-permute-start(bf16[32,32,128]{2,1,0:T(8,128)(2,1)S(1)} %get-tuple-element.20.other), channel_id=1, source_target_pairs={{0,3},{1,2},{4,1},{5,0},{8,5},{9,4},{12,9},{13,8},{14,13},{15,12},... | collective-permute-start | bytes 786440 | tf_op jit(solution)/shard_map/ppermute | solution.py:350
  8.4 4.6 %receiver_weights.1.weights = bf16[8192,128]{1,0:T(8,128)(2,1)S(1)} custom-call(bf16[32,32,128]{2,1,0:T(8,128)(2,1)S(1)} %get-tuple-element.21.same.refs_0_, bf16[32,32,128]{2,1,0:T(8,128)(2,1)S(1)} %get-tuple-element.20.other, bf16[32,32,128]{2,1,0:T(8,128)(2,1)S(1)} %collective-permute-done.4.far_same, ...), custom_call_target="tpu_custom_call" | custom-call | flops 1048576 | bytes 16384 | tf_op jit(solution)/shard_map/receiver_weights/pallas_call | solution.py:176
  13.0 0.6 %collective-permute-done.2.refs_0_ = bf16[32,32,128]{2,1,0:T(8,128)(2,1)S(1)} collective-permute-done((bf16[32,32,128]{2,1,0:T(8,128)(2,1)S(1)}, bf16[32,32,128]{2,1,0:T(8,128)(2,1)S(1)}, u32[]{:S(2)}, u32[]{:S(2)}) %collective-permute-start.2) | collective-permute-done | bytes 262176 | tf_op jit(solution)/shard_map/ppermute | solution.py:350
  13.6 2.2 %collective-permute-done.3.refs_2_ = bf16[32,32,128]{2,1,0:T(8,128)(2,1)S(1)} collective-permute-done((bf16[32,32,128]{2,1,0:T(8,128)(2,1)S(1)}, bf16[32,32,128]{2,1,0:T(8,128)(2,1)S(1)}, u32[]{:S(2)}, u32[]{:S(2)}) %collective-permute-start.3) | collective-permute-done | bytes 262176 | tf_op jit(solution)/shard_map/ppermute | solution.py:350
  15.8 1.6 %collective-permute-start.6 = (bf16[32,32,128]{2,1,0:T(8,128)(2,1)S(1)}, bf16[32,32,128]{2,1,0:T(8,128)(2,1)S(1)}, u32[]{:S(2)}, u32[]{:S(2)}) collective-permute-start(bf16[32,32,128]{2,1,0:T(8,128)(2,1)S(1)} %collective-permute-done.2.refs_0_), channel_id=1, source_target_pairs={{0,4},{1,5},{4,8},{5,9},{8,12},{9,13},{12,14},{13,15},{14,10},{15,... | collective-permute-start | bytes 786440 | tf_op jit(solution)/shard_map/ppermute | solution.py:350
  17.4 0.5 collective-permute-start.7
  17.8 1.1 %collective-permute-done.refs_1_ = bf16[32,32,128]{2,1,0:T(8,128)(2,1)S(1)} collective-permute-done((bf16[32,32,128]{2,1,0:T(8,128)(2,1)S(1)}, bf16[32,32,128]{2,1,0:T(8,128)(2,1)S(1)}, u32[]{:S(2)}, u32[]{:S(2)}) %collective-permute-start) | collective-permute-done | bytes 262176 | tf_op jit(solution)/shard_map/ppermute | solution.py:350
  18.9 0.1 collective-permute-done.1.refs_3_
  19.0 1.9 %collective-permute-start.11 = (bf16[32,32,128]{2,1,0:T(8,128)(2,1)S(1)}, bf16[32,32,128]{2,1,0:T(8,128)(2,1)S(1)}, u32[]{:S(2)}, u32[]{:S(2)}) collective-permute-start(bf16[32,32,128]{2,1,0:T(8,128)(2,1)S(1)} %collective-permute-done.1.refs_3_), channel_id=1, source_target_pairs={{0,2},{1,3},{4,0},{5,1},{8,4},{9,5},{12,8},{13,9},{14,12},{15,13},... | collective-permute-start | bytes 786440 | tf_op jit(solution)/shard_map/ppermute | solution.py:350
  20.9 0.2 collective-permute-start.10
  21.1 3.5 %stack.5.refs_4_ = bf16[4,32,64,128]{3,2,1,0:T(8,128)(2,1)} custom-call(s32[4]{0:T(128)S(1)} %copy-done.1, bf16[256,128]{1,0:T(8,128)(2,1)S(1)} %copy-done, bf16[8192,128]{1,0:T(8,128)(2,1)S(1)} %receiver_weights.1.weights, bf16[32,32,128]{2,1,0:T(8,128)(2,1)S(1)} %get-tuple-element.21.same.refs_0_, ...), custom_call_target="tpu_custom_call" | custom-call | flops 1048576 | bytes 16384 | tf_op jit(solution)/shard_map/stack/pallas_call | solution.py:311
  24.6 2.4 %collective-permute-done.7.refs_2_ = bf16[32,32,128]{2,1,0:T(8,128)(2,1)S(1)} collective-permute-done((bf16[32,32,128]{2,1,0:T(8,128)(2,1)S(1)}, bf16[32,32,128]{2,1,0:T(8,128)(2,1)S(1)}, u32[]{:S(2)}, u32[]{:S(2)}) %collective-permute-start.7) | collective-permute-done | bytes 262176 | tf_op jit(solution)/shard_map/ppermute | solution.py:350
  27.0 1.6 %collective-permute-start.8 = (bf16[32,32,128]{2,1,0:T(8,128)(2,1)S(1)}, bf16[32,32,128]{2,1,0:T(8,128)(2,1)S(1)}, u32[]{:S(2)}, u32[]{:S(2)}) collective-permute-start(bf16[32,32,128]{2,1,0:T(8,128)(2,1)S(1)} %collective-permute-done.6.refs_0_), channel_id=1, source_target_pairs={{0,4},{1,5},{4,8},{5,9},{8,12},{9,13},{12,14},{13,15},{14,10},{15,... | collective-permute-start | bytes 786440 | tf_op jit(solution)/shard_map/ppermute | solution.py:350
  28.6 0.5 collective-permute-start.9
  29.1 3.6 %collective-permute-done.11.refs_3_ = bf16[32,32,128]{2,1,0:T(8,128)(2,1)S(1)} collective-permute-done((bf16[32,32,128]{2,1,0:T(8,128)(2,1)S(1)}, bf16[32,32,128]{2,1,0:T(8,128)(2,1)S(1)}, u32[]{:S(2)}, u32[]{:S(2)}) %collective-permute-start.11) | collective-permute-done | bytes 262176 | tf_op jit(solution)/shard_map/ppermute | solution.py:350
  32.7 2.0 %collective-permute-start.15 = (bf16[32,32,128]{2,1,0:T(8,128)(2,1)S(1)}, bf16[32,32,128]{2,1,0:T(8,128)(2,1)S(1)}, u32[]{:S(2)}, u32[]{:S(2)}) collective-permute-start(bf16[32,32,128]{2,1,0:T(8,128)(2,1)S(1)} %collective-permute-done.10.refs_1_), channel_id=1, source_target_pairs={{0,4},{1,5},{4,8},{5,9},{8,12},{9,13},{12,14},{13,15},{14,10},{15,... | collective-permute-start | bytes 786440 | tf_op jit(solution)/shard_map/ppermute | solution.py:350
  34.7 0.8 %stack.6.refs_4_ = bf16[4,32,64,128]{3,2,1,0:T(8,128)(2,1)} custom-call(s32[4]{0:T(128)S(1)} %copy-done.1, bf16[256,128]{1,0:T(8,128)(2,1)S(1)} %copy-done, bf16[8192,128]{1,0:T(8,128)(2,1)S(1)} %receiver_weights.1.weights, bf16[32,32,128]{2,1,0:T(8,128)(2,1)S(1)} %collective-permute-done.2.refs_0_, ...), custom_call_target="tpu_custom_call", output_to_operand_aliasing={{}: (7, {})} | custom-call | flops 1048576 | bytes 16384 | tf_op jit(solution)/shard_map/stack/pallas_call | solution.py:311
  35.5 0.8 %collective-permute-done.8.refs_0_ = bf16[32,32,128]{2,1,0:T(8,128)(2,1)S(1)} collective-permute-done((bf16[32,32,128]{2,1,0:T(8,128)(2,1)S(1)}, bf16[32,32,128]{2,1,0:T(8,128)(2,1)S(1)}, u32[]{:S(2)}, u32[]{:S(2)}) %collective-permute-start.8) | collective-permute-done | bytes 262176 | tf_op jit(solution)/shard_map/ppermute | solution.py:350
  36.3 2.0 %collective-permute-done.9.refs_2_ = bf16[32,32,128]{2,1,0:T(8,128)(2,1)S(1)} collective-permute-done((bf16[32,32,128]{2,1,0:T(8,128)(2,1)S(1)}, bf16[32,32,128]{2,1,0:T(8,128)(2,1)S(1)}, u32[]{:S(2)}, u32[]{:S(2)}) %collective-permute-start.9) | collective-permute-done | bytes 262176 | tf_op jit(solution)/shard_map/ppermute | solution.py:350
  38.3 1.7 %collective-permute-start.12 = (bf16[32,32,128]{2,1,0:T(8,128)(2,1)S(1)}, bf16[32,32,128]{2,1,0:T(8,128)(2,1)S(1)}, u32[]{:S(2)}, u32[]{:S(2)}) collective-permute-start(bf16[32,32,128]{2,1,0:T(8,128)(2,1)S(1)} %collective-permute-done.8.refs_0_), channel_id=1, source_target_pairs={{0,4},{1,5},{4,8},{5,9},{8,12},{9,13},{12,14},{13,15},{14,10},{15,... | collective-permute-start | bytes 786440 | tf_op jit(solution)/shard_map/ppermute | solution.py:350
  40.0 2.7 %collective-permute-done.13.refs_3_ = bf16[32,32,128]{2,1,0:T(8,128)(2,1)S(1)} collective-permute-done((bf16[32,32,128]{2,1,0:T(8,128)(2,1)S(1)}, bf16[32,32,128]{2,1,0:T(8,128)(2,1)S(1)}, u32[]{:S(2)}, u32[]{:S(2)}) %collective-permute-start.13) | collective-permute-done | bytes 262176 | tf_op jit(solution)/shard_map/ppermute | solution.py:350
  42.7 0.3 collective-permute-start.14
  43.0 1.0 %stack.7.refs_4_ = bf16[4,32,64,128]{3,2,1,0:T(8,128)(2,1)} custom-call(s32[4]{0:T(128)S(1)} %copy-done.1, bf16[256,128]{1,0:T(8,128)(2,1)S(1)} %copy-done, bf16[8192,128]{1,0:T(8,128)(2,1)S(1)} %receiver_weights.1.weights, bf16[32,32,128]{2,1,0:T(8,128)(2,1)S(1)} %collective-permute-done.6.refs_0_, ...), custom_call_target="tpu_custom_call", output_to_operand_aliasing={{}: (7, {})} | custom-call | flops 1048576 | bytes 16384 | tf_op jit(solution)/shard_map/stack/pallas_call | solution.py:311
  44.0 3.5 %stack.8.refs_2_ = bf16[4,32,64,128]{3,2,1,0:T(8,128)(2,1)} custom-call(s32[4]{0:T(128)S(1)} %copy-done.1, bf16[256,128]{1,0:T(8,128)(2,1)S(1)} %copy-done, bf16[8192,128]{1,0:T(8,128)(2,1)S(1)} %receiver_weights.1.weights, bf16[32,32,128]{2,1,0:T(8,128)(2,1)S(1)} %collective-permute-done.8.refs_0_, ...), custom_call_target="tpu_custom_call", output_to_operand_aliasing={{}: (7, {})} | custom-call | flops 1048576 | bytes 16384 | tf_op jit(solution)/shard_map/stack/pallas_call | solution.py:311
  47.5 2.4 %collective-permute-done.14.refs_1_ = bf16[32,32,128]{2,1,0:T(8,128)(2,1)S(1)} collective-permute-done((bf16[32,32,128]{2,1,0:T(8,128)(2,1)S(1)}, bf16[32,32,128]{2,1,0:T(8,128)(2,1)S(1)}, u32[]{:S(2)}, u32[]{:S(2)}) %collective-permute-start.14) | collective-permute-done | bytes 262176 | tf_op jit(solution)/shard_map/ppermute | solution.py:350
  49.8 3.3 %stack.9 = bf16[4,32,64,128]{3,2,1,0:T(8,128)(2,1)} custom-call(s32[4]{0:T(128)S(1)} %copy-done.1, bf16[256,128]{1,0:T(8,128)(2,1)S(1)} %copy-done, bf16[8192,128]{1,0:T(8,128)(2,1)S(1)} %receiver_weights.1.weights, bf16[32,32,128]{2,1,0:T(8,128)(2,1)S(1)} %collective-permute-done.12.refs_0_, ...), custom_call_target="tpu_custom_call", output_to_operand_aliasing={{}: (5, {})} | custom-call | flops 1048576 | bytes 16384 | tf_op jit(solution)/shard_map/stack/pallas_call | solution.py:311
  (11 shorter events, 0.0 us)
Async XLA Ops:
  0.0 21.1 %copy-start = (bf16[256,128]{1,0:T(8,128)(2,1)S(1)}, bf16[256,128]{1,0:T(8,128)(2,1)}, u32[]{:S(2)}) copy-start(bf16[256,128]{1,0:T(8,128)(2,1)} %constant.3.table) | copy-start | bytes 196612
  0.0 21.1 %copy-start.1 = (s32[4]{0:T(128)S(1)}, s32[4]{0:T(128)}, u32[]{:S(2)}) copy-start(s32[4]{0:T(128)} %steps.9) | copy-start | bytes 52
  3.0 4.8 %collective-permute-start.4 = (bf16[32,32,128]{2,1,0:T(8,128)(2,1)S(1)}, bf16[32,32,128]{2,1,0:T(8,128)(2,1)S(1)}, u32[]{:S(2)}, u32[]{:S(2)}) collective-permute-start(bf16[32,32,128]{2,1,0:T(8,128)(2,1)S(1)} %get-tuple-element.21.same.refs_0_), channel_id=1, source_target_pairs={{0,1},{1,0},{2,3},{3,2},{4,5},{5,4},{6,7},{7,6},{8,9},{9,8},{10,11... | collective-permute-start | bytes 786440 | tf_op jit(solution)/shard_map/ppermute | solution.py:342
  3.5 4.8 %collective-permute-start.5 = (bf16[32,32,128]{2,1,0:T(8,128)(2,1)S(1)}, bf16[32,32,128]{2,1,0:T(8,128)(2,1)S(1)}, u32[]{:S(2)}, u32[]{:S(2)}) collective-permute-start(bf16[32,32,128]{2,1,0:T(8,128)(2,1)S(1)} %get-tuple-element.20.other), channel_id=1, source_target_pairs={{0,1},{1,0},{2,3},{3,2},{4,5},{5,4},{6,7},{7,6},{8,9},{9,8},{10,11... | collective-permute-start | bytes 786440 | tf_op jit(solution)/shard_map/ppermute | solution.py:342
  3.6 10.0 %collective-permute-start.2 = (bf16[32,32,128]{2,1,0:T(8,128)(2,1)S(1)}, bf16[32,32,128]{2,1,0:T(8,128)(2,1)S(1)}, u32[]{:S(2)}, u32[]{:S(2)}) collective-permute-start(bf16[32,32,128]{2,1,0:T(8,128)(2,1)S(1)} %get-tuple-element.21.same.refs_0_), channel_id=1, source_target_pairs={{0,4},{1,5},{4,8},{5,9},{8,12},{9,13},{12,14},{13,15},{14,10},{15,... | collective-permute-start | bytes 786440 | tf_op jit(solution)/shard_map/ppermute | solution.py:350
  6.6 9.2 %collective-permute-start.3 = (bf16[32,32,128]{2,1,0:T(8,128)(2,1)S(1)}, bf16[32,32,128]{2,1,0:T(8,128)(2,1)S(1)}, u32[]{:S(2)}, u32[]{:S(2)}) collective-permute-start(bf16[32,32,128]{2,1,0:T(8,128)(2,1)S(1)} %get-tuple-element.21.same.refs_0_), channel_id=1, source_target_pairs={{0,2},{1,3},{4,0},{5,1},{8,4},{9,5},{12,8},{13,9},{14,12},{15,13},... | collective-permute-start | bytes 786440 | tf_op jit(solution)/shard_map/ppermute | solution.py:350
  6.6 12.3 %collective-permute-start = (bf16[32,32,128]{2,1,0:T(8,128)(2,1)S(1)}, bf16[32,32,128]{2,1,0:T(8,128)(2,1)S(1)}, u32[]{:S(2)}, u32[]{:S(2)}) collective-permute-start(bf16[32,32,128]{2,1,0:T(8,128)(2,1)S(1)} %get-tuple-element.20.other), channel_id=1, source_target_pairs={{0,5},{1,4},{4,9},{5,8},{8,13},{9,12},{12,15},{13,14},{14,11},{15,... | collective-permute-start | bytes 786440 | tf_op jit(solution)/shard_map/ppermute | solution.py:350
  7.8 11.3 %collective-permute-start.1 = (bf16[32,32,128]{2,1,0:T(8,128)(2,1)S(1)}, bf16[32,32,128]{2,1,0:T(8,128)(2,1)S(1)}, u32[]{:S(2)}, u32[]{:S(2)}) collective-permute-start(bf16[32,32,128]{2,1,0:T(8,128)(2,1)S(1)} %get-tuple-element.20.other), channel_id=1, source_target_pairs={{0,3},{1,2},{4,1},{5,0},{8,5},{9,4},{12,9},{13,8},{14,13},{15,12},... | collective-permute-start | bytes 786440 | tf_op jit(solution)/shard_map/ppermute | solution.py:350
  15.8 8.8 %collective-permute-start.6 = (bf16[32,32,128]{2,1,0:T(8,128)(2,1)S(1)}, bf16[32,32,128]{2,1,0:T(8,128)(2,1)S(1)}, u32[]{:S(2)}, u32[]{:S(2)}) collective-permute-start(bf16[32,32,128]{2,1,0:T(8,128)(2,1)S(1)} %collective-permute-done.2.refs_0_), channel_id=1, source_target_pairs={{0,4},{1,5},{4,8},{5,9},{8,12},{9,13},{12,14},{13,15},{14,10},{15,... | collective-permute-start | bytes 786440 | tf_op jit(solution)/shard_map/ppermute | solution.py:350
  17.4 9.7 %collective-permute-start.7 = (bf16[32,32,128]{2,1,0:T(8,128)(2,1)S(1)}, bf16[32,32,128]{2,1,0:T(8,128)(2,1)S(1)}, u32[]{:S(2)}, u32[]{:S(2)}) collective-permute-start(bf16[32,32,128]{2,1,0:T(8,128)(2,1)S(1)} %collective-permute-done.3.refs_2_), channel_id=1, source_target_pairs={{0,2},{1,3},{4,0},{5,1},{8,4},{9,5},{12,8},{13,9},{14,12},{15,13},... | collective-permute-start | bytes 786440 | tf_op jit(solution)/shard_map/ppermute | solution.py:350
  19.0 13.6 %collective-permute-start.11 = (bf16[32,32,128]{2,1,0:T(8,128)(2,1)S(1)}, bf16[32,32,128]{2,1,0:T(8,128)(2,1)S(1)}, u32[]{:S(2)}, u32[]{:S(2)}) collective-permute-start(bf16[32,32,128]{2,1,0:T(8,128)(2,1)S(1)} %collective-permute-done.1.refs_3_), channel_id=1, source_target_pairs={{0,2},{1,3},{4,0},{5,1},{8,4},{9,5},{12,8},{13,9},{14,12},{15,13},... | collective-permute-start | bytes 786440 | tf_op jit(solution)/shard_map/ppermute | solution.py:350
  20.9 11.8 %collective-permute-start.10 = (bf16[32,32,128]{2,1,0:T(8,128)(2,1)S(1)}, bf16[32,32,128]{2,1,0:T(8,128)(2,1)S(1)}, u32[]{:S(2)}, u32[]{:S(2)}) collective-permute-start(bf16[32,32,128]{2,1,0:T(8,128)(2,1)S(1)} %collective-permute-done.refs_1_), channel_id=1, source_target_pairs={{0,4},{1,5},{4,8},{5,9},{8,12},{9,13},{12,14},{13,15},{14,10},{15,... | collective-permute-start | bytes 786440 | tf_op jit(solution)/shard_map/ppermute | solution.py:350
  27.0 9.2 %collective-permute-start.8 = (bf16[32,32,128]{2,1,0:T(8,128)(2,1)S(1)}, bf16[32,32,128]{2,1,0:T(8,128)(2,1)S(1)}, u32[]{:S(2)}, u32[]{:S(2)}) collective-permute-start(bf16[32,32,128]{2,1,0:T(8,128)(2,1)S(1)} %collective-permute-done.6.refs_0_), channel_id=1, source_target_pairs={{0,4},{1,5},{4,8},{5,9},{8,12},{9,13},{12,14},{13,15},{14,10},{15,... | collective-permute-start | bytes 786440 | tf_op jit(solution)/shard_map/ppermute | solution.py:350
  28.6 9.7 %collective-permute-start.9 = (bf16[32,32,128]{2,1,0:T(8,128)(2,1)S(1)}, bf16[32,32,128]{2,1,0:T(8,128)(2,1)S(1)}, u32[]{:S(2)}, u32[]{:S(2)}) collective-permute-start(bf16[32,32,128]{2,1,0:T(8,128)(2,1)S(1)} %collective-permute-done.7.refs_2_), channel_id=1, source_target_pairs={{0,2},{1,3},{4,0},{5,1},{8,4},{9,5},{12,8},{13,9},{14,12},{15,13},... | collective-permute-start | bytes 786440 | tf_op jit(solution)/shard_map/ppermute | solution.py:350
  32.7 10.0 %collective-permute-start.13 = (bf16[32,32,128]{2,1,0:T(8,128)(2,1)S(1)}, bf16[32,32,128]{2,1,0:T(8,128)(2,1)S(1)}, u32[]{:S(2)}, u32[]{:S(2)}) collective-permute-start(bf16[32,32,128]{2,1,0:T(8,128)(2,1)S(1)} %collective-permute-done.11.refs_3_), channel_id=1, source_target_pairs={{0,2},{1,3},{4,0},{5,1},{8,4},{9,5},{12,8},{13,9},{14,12},{15,13},... | collective-permute-start | bytes 786440 | tf_op jit(solution)/shard_map/ppermute | solution.py:350
  32.7 11.3 %collective-permute-start.15 = (bf16[32,32,128]{2,1,0:T(8,128)(2,1)S(1)}, bf16[32,32,128]{2,1,0:T(8,128)(2,1)S(1)}, u32[]{:S(2)}, u32[]{:S(2)}) collective-permute-start(bf16[32,32,128]{2,1,0:T(8,128)(2,1)S(1)} %collective-permute-done.10.refs_1_), channel_id=1, source_target_pairs={{0,4},{1,5},{4,8},{5,9},{8,12},{9,13},{12,14},{13,15},{14,10},{15,... | collective-permute-start | bytes 786440 | tf_op jit(solution)/shard_map/ppermute | solution.py:350
  38.3 9.2 %collective-permute-start.12 = (bf16[32,32,128]{2,1,0:T(8,128)(2,1)S(1)}, bf16[32,32,128]{2,1,0:T(8,128)(2,1)S(1)}, u32[]{:S(2)}, u32[]{:S(2)}) collective-permute-start(bf16[32,32,128]{2,1,0:T(8,128)(2,1)S(1)} %collective-permute-done.8.refs_0_), channel_id=1, source_target_pairs={{0,4},{1,5},{4,8},{5,9},{8,12},{9,13},{12,14},{13,15},{14,10},{15,... | collective-permute-start | bytes 786440 | tf_op jit(solution)/shard_map/ppermute | solution.py:350
  42.7 7.1 %collective-permute-start.14 = (bf16[32,32,128]{2,1,0:T(8,128)(2,1)S(1)}, bf16[32,32,128]{2,1,0:T(8,128)(2,1)S(1)}, u32[]{:S(2)}, u32[]{:S(2)}) collective-permute-start(bf16[32,32,128]{2,1,0:T(8,128)(2,1)S(1)} %collective-permute-done.13.refs_3_), channel_id=1, source_target_pairs={{0,2},{1,3},{4,0},{5,1},{8,4},{9,5},{12,8},{13,9},{14,12},{15,13},... | collective-permute-start | bytes 786440 | tf_op jit(solution)/shard_map/ppermute | solution.py:350

commit v3 on v2

--- a/solution.py
+++ b/solution.py
@@ -15,7 +15,7 @@
 LAG_STEP = 28
 WATER = 0.1
 BATCH = 8
-GROUP = 8
+GROUP = 4
 
 VMEM = pltpu.VMEM
 SMEM = pltpu.SMEM
@@ -50,17 +50,23 @@
     return jnp.asarray(table, jnp.float32).astype(jnp.bfloat16)
 
 
-def interleave(first, second):
+def exchange(first, second, size):
     bins = first.shape[-1]
     lane = lax.broadcasted_iota(jnp.int32, first.shape, 1)
-    even = lane // GROUP % 2 == 0
+    even = lane // size % 2 == 0
     return (
-        jnp.where(even, first, pltpu.roll(second, GROUP, 1)),
-        jnp.where(even, pltpu.roll(first, bins - GROUP, 1), second),
+        jnp.where(even, first, pltpu.roll(second, size, 1)),
+        jnp.where(even, pltpu.roll(first, bins - size, 1), second),
     )
 
 
-def whiten_kernel(chan_mask, win_mask, spectra, same, other, held, sems):
+def interleave(a, b, c, d):
+    a, c = exchange(a, c, 2 * GROUP)
+    b, d = exchange(b, d, 2 * GROUP)
+    return exchange(a, b, GROUP) + exchange(c, d, GROUP)
+
+
+def whiten_kernel(chan_in, win_in, spectra, same, other, held, chan_mask, win_mask, sems):
     rows, bins = spectra.shape[1:]
     half = same.shape[0]
     own = lax.axis_index("tm") * half
@@ -69,8 +75,14 @@
         pltpu.make_async_copy(spectra.at[pl.ds(start, half)], held.at[i], sems.at[i])
         for i, start in enumerate(starts)
     ]
-    for copy in copies:
+    masks = [
+        pltpu.make_async_copy(win_in, win_mask, sems.at[2]),
+        pltpu.make_async_copy(chan_in, chan_mask, sems.at[3]),
+    ]
+    for copy in copies + masks:
         copy.start()
+    for copy in masks:
+        copy.wait()
     row = lax.broadcasted_iota(jnp.int32, (rows, bins), 0)
     keep = jnp.zeros((rows, bins), jnp.float32)
     for w in range(rows // 2):
@@ -114,12 +126,12 @@
         copies[side].wait()
         for i in range(0, half, BATCH):
             values = whitened(side, range(i, i + BATCH))
-            for j in range(0, BATCH, 2):
-                pair = interleave(
-                    values[j * rows : (j + 1) * rows], values[(j + 1) * rows : (j + 2) * rows]
+            for j in range(0, BATCH, GROUP):
+                mixed = interleave(
+                    *(values[n * rows : (n + 1) * rows] for n in range(j, j + GROUP))
                 )
-                piece[i + j] = pair[0].astype(jnp.bfloat16)
-                piece[i + j + 1] = pair[1].astype(jnp.bfloat16)
+                for n, one in enumerate(mixed):
+                    piece[i + j + n] = one.astype(jnp.bfloat16)
 
 
 def whiten(spectra, chan_mask, win_mask):
@@ -128,15 +140,13 @@
     return pl.pallas_call(
         whiten_kernel,
         out_shape=(piece, piece),
-        in_specs=[
-            pl.BlockSpec(memory_space=SMEM),
-            pl.BlockSpec(memory_space=SMEM),
-            pl.BlockSpec(memory_space=pl.ANY),
-        ],
+        in_specs=[pl.BlockSpec(memory_space=pl.ANY)] * 3,
         out_specs=(pl.BlockSpec(memory_space=VMEM),) * 2,
         scratch_shapes=[
             VMEM((2, channels // 2, rows, bins), jnp.bfloat16),
-            pltpu.SemaphoreType.DMA((2,)),
+            SMEM(chan_mask.shape, chan_mask.dtype),
+            SMEM(win_mask.shape, win_mask.dtype),
+            pltpu.SemaphoreType.DMA((4,)),
         ],
         cost_estimate=SMALL,
         name="whiten",
@@ -158,11 +168,11 @@
         for h in range(2):
             copies[2 * side + h].wait()
             piece = held.at[2 * side + h]
-            for i in range(0, half, 2):
-                pair = interleave(piece[i].astype(jnp.float32), piece[i + 1].astype(jnp.float32))
-                for j in range(2):
+            for i in range(0, half, GROUP):
+                apart = interleave(*(piece[i + j].astype(jnp.float32) for j in range(GROUP)))
+                for j, one in enumerate(apart):
                     at = pl.multiple_of((start + i + j) * deep + h * rows, rows)
-                    flat[pl.ds(at, rows), :] = pair[j]
+                    flat[pl.ds(at, rows), :] = one
     for w in range(rows):
         real = flat[pl.ds(2 * w, 2 * half, stride=deep), :]
         imag = flat[pl.ds(2 * w + 1, 2 * half, stride=deep), :]
@@ -190,11 +200,13 @@
     )(same, other, far_same, far_other)
 
 
-def stack_kernel(tour, distances, first, steps, table, weights, *refs):
+def stack_kernel(tour, distances, first, steps_in, table, weights, *refs):
     blocks = len(distances)
     pieces = refs[: 2 * blocks]
     out = refs[2 * blocks + (0 if first else 1)]
-    src, turned, cross, done, in_sem, out_sem = refs[2 * blocks + (1 if first else 2) :]
+    steps, src, turned, cross, done, in_sem, out_sem, step_sem = refs[
+        2 * blocks + (1 if first else 2) :
+    ]
     sources, rows, bins = pieces[0].shape
     count = steps.shape[0]
     ring = len(tour)
@@ -203,9 +215,9 @@
     per_tile = 128 // lanes
     tiles = GROUP // per_tile
     depth = GROUP * lanes
-    pair_rows = 2 * GROUP
-    row = lax.broadcasted_iota(jnp.int32, (pair_rows, 128), 0) % GROUP
-    col = lax.broadcasted_iota(jnp.int32, (pair_rows, 128), 1) // lanes
+    span = GROUP * GROUP
+    row = lax.broadcasted_iota(jnp.int32, (span, 128), 0) % GROUP
+    col = lax.broadcasted_iota(jnp.int32, (span, 128), 1) // lanes
     receivers = weights.shape[1] // 2
     me = lax.axis_index("chan")
     folded = tour[1] == 2
@@ -216,11 +228,16 @@
         return jnp.where(at < ring // 2, 2 * at, 2 * (ring - 1 - at) + 1) if folded else at
 
     owners = [owner_at(d) for d in distances]
-    needed = [
-        functools.reduce(jnp.logical_or, [steps[k] == owner for k in range(count)])
-        for owner in owners
-    ]
-    part = sources // 2
+    parts_out = out_sem.shape[2]
+    part = sources // parts_out
+    asked = pltpu.make_async_copy(steps_in, steps, step_sem)
+    asked.start()
+    if staged:
+        asked.wait()
+        needed = [
+            functools.reduce(jnp.logical_or, [steps[k] == owner for k in range(count)])
+            for owner in owners
+        ]
 
     def arrival(b, h):
         return pltpu.make_async_copy(pieces[2 * b + h], src.at[b, h], in_sem.at[b, h])
@@ -239,12 +256,12 @@
     def compute(b, owner):
         for s in range(sources):
             parts = (src[b, 0, s], src[b, 1, s]) if staged else (pieces[0][s], pieces[1][s])
-            turned[s // 2, s % 2] = jnp.concatenate(parts * per_tile).T
-        for m in range(bins // pair_rows):
-            at = m * pair_rows
+            turned[s // GROUP, s % GROUP] = jnp.concatenate(parts * per_tile).T
+        for m in range(bins // span):
+            at = m * span
             sums = []
-            for p in range(2):
-                mine = turned[:, p, at : at + pair_rows, :]
+            for p in range(GROUP):
+                mine = turned[:, p, at : at + span, :]
                 wide = jnp.concatenate(
                     [
                         jnp.where(
@@ -254,13 +271,24 @@
                     ],
                     axis=1,
                 )
-                start = (2 * m + p) * depth
+                start = (GROUP * m + p) * depth
                 x = jnp.dot(
                     wide, weights[start : start + depth, :], preferred_element_type=jnp.float32
                 )
-                sums.append(x.reshape(sources, GROUP, 2 * receivers))
-            cross[:, at : at + pair_rows, :] = jnp.concatenate(sums, axis=1).astype(jnp.bfloat16)
-        for c in range(2):
+                sums.append(x.reshape(sources // 2, 2 * GROUP, 2 * receivers))
+            eights = []
+            for p in range(0, GROUP, 2):
+                low, high = sums[p], sums[p + 1]
+                upper = lax.broadcasted_iota(jnp.int32, low.shape, 1) < GROUP
+                one = jnp.where(upper, low, pltpu.roll(high, GROUP, 1))
+                two = jnp.where(upper, pltpu.roll(low, GROUP, 1), high)
+                eights.append(
+                    jnp.stack((one, two), axis=1).reshape(sources, 2 * GROUP, 2 * receivers)
+                )
+            cross[:, at : at + span, :] = jnp.concatenate(eights, axis=1).astype(jnp.bfloat16)
+        if not staged:
+            asked.wait()
+        for c in range(parts_out):
             turns = [cross[c * part + i].T for i in range(part)]
             left = jnp.concatenate(
                 [jnp.concatenate([x[:receivers], x[receivers:]], axis=1) for x in turns]
@@ -288,12 +316,15 @@
             compute(b, owner)
         return 0
 
-    lax.fori_loop(0, blocks, turn, 0)
+    if staged:
+        lax.fori_loop(0, blocks, turn, 0)
+    else:
+        compute(0, owners[0])
     for b in range(blocks):
         for k in range(count):
             @pl.when(steps[k] == owners[b])
             def _(b=b, k=k):
-                for c in range(2):
+                for c in range(parts_out):
                     departure(b, k, c).wait()
 
 
@@ -311,17 +342,19 @@
     return pl.pallas_call(
         functools.partial(stack_kernel, tour, distances, first),
         out_shape=out_shape,
-        in_specs=[pl.BlockSpec(memory_space=SMEM)]
+        in_specs=[pl.BlockSpec(memory_space=pl.ANY)]
         + [pl.BlockSpec(memory_space=VMEM)] * 2
         + [pl.BlockSpec(memory_space=kind) for kind in kinds],
         out_specs=pl.BlockSpec(memory_space=pl.ANY),
         scratch_shapes=[
+            SMEM(steps.shape, steps.dtype),
             VMEM((blocks, 2, sources, rows, bins), jnp.bfloat16),
-            VMEM((sources // 2, 2, bins, 128), jnp.bfloat16),
+            VMEM((sources // GROUP, GROUP, bins, 128), jnp.bfloat16),
             VMEM((sources, bins, 2 * receivers), jnp.bfloat16),
             VMEM((blocks, sources, receivers, LAGS), jnp.bfloat16),
             pltpu.SemaphoreType.DMA((blocks, 2)),
-            pltpu.SemaphoreType.DMA((blocks, count, 2)),
+            pltpu.SemaphoreType.DMA((blocks, count, 4 if blocks == 1 else 2)),
+            pltpu.SemaphoreType.DMA,
         ],
         input_output_aliases={} if first else {len(args) - 1: 0},
         compiler_params=pltpu.CompilerParams(vmem_limit_bytes=24 << 20),

time: 53.6 us -> 52 us (0.970)
  waiting for transfers between devices: 17.9 us -> 15.7 us
  Pallas kernels: 19.7 us -> 20.4 us
    ppermute x14, waiting for transfers between devices: 17.9 us -> 15.7 us  [send(): return lax.ppermute(x, ('chan', 'tm'), pairs)]
    pallas_call x1, Pallas kernels: 4.65 us -> 5.79 us  [receiver_weights(): pl.pallas_call(receiver_kernel, out_shape=jax.ShapeDtypeStruct((bins * 2...]
    pallas_call x1, Pallas kernels: 2.99 us -> 2.37 us  [whiten(): pl.pallas_call(whiten_kernel, out_shape=(piece, piece), in_specs=[pl.Bloc...]
  transfers between devices with their start and end apart: 16 -> 16, of which waited for: 10 -> 9; matrix products, arithmetic and copies ran while one was open for 0% -> 0% of each run, Pallas kernels for 25% -> 30%
where the time goes in v3:
time: 52 us; the launch traced here: 51.7 us
  Pallas kernels  20.4 us (39%)
  waiting for transfers between devices  15.7 us (30%)
  starting transfers between devices  15.3 us (29%)
    ppermute x14, waiting for transfers between devices, send(): return lax.ppermute(x, ('chan', 'tm'), pairs)  15.7 us
    ppermute x14, starting transfers between devices, send(): return lax.ppermute(x, ('chan', 'tm'), pairs)  14.7 us
    pallas_call x5, Pallas kernels, stack(): pl.pallas_call(functools.partial(stack_kernel, tour, distances, first), o...  12.3 us
    pallas_call x1, Pallas kernels, receiver_weights(): pl.pallas_call(receiver_kernel, out_shape=jax.ShapeDtypeStruct((bins * 2...  5.79 us
    pallas_call x1, Pallas kernels, whiten(): pl.pallas_call(whiten_kernel, out_shape=(piece, piece), in_specs=[pl.Bloc...  2.37 us
  transfers between devices with their start and end apart: 16, of which 9 were waited for; matrix products, arithmetic and copies ran while one was open for 0% of the time, Pallas kernels for 30%

profile of v3, /device:TPU:0, one launch (start us, length us, event | category | flops | bytes accessed | tf_op | source)
XLA Modules:
  0.0 51.7 jit_solution(707165796713868672)
XLA Ops:
  0.0 2.4 %whiten.1 = (bf16[32,32,128]{2,1,0:T(8,128)(2,1)S(1)}, bf16[32,32,128]{2,1,0:T(8,128)(2,1)S(1)}) custom-call(s32[64]{0:T(128)} %chan_in.1, s32[16]{0:T(128)} %win_in.1, bf16[64,32,128]{2,1,0:T(8,128)(2,1)} %bitcast.1), custom_call_target="tpu_custom_call" | custom-call | flops 1048576 | bytes 16384 | tf_op jit(solution)/shard_map/whiten/pallas_call | solution.py:140
  2.4 0.5 %collective-permute-start.4 = (bf16[32,32,128]{2,1,0:T(8,128)(2,1)S(1)}, bf16[32,32,128]{2,1,0:T(8,128)(2,1)S(1)}, u32[]{:S(2)}, u32[]{:S(2)}) collective-permute-start(bf16[32,32,128]{2,1,0:T(8,128)(2,1)S(1)} %get-tuple-element.21.same.refs_0_), channel_id=1, source_target_pairs={{0,1},{1,0},{2,3},{3,2},{4,5},{5,4},{6,7},{7,6},{8,9},{9,8},{10,11... | collective-permute-start | bytes 786440 | tf_op jit(solution)/shard_map/ppermute | solution.py:375
  2.9 0.1 collective-permute-start.5
  3.0 3.0 %collective-permute-start.2 = (bf16[32,32,128]{2,1,0:T(8,128)(2,1)S(1)}, bf16[32,32,128]{2,1,0:T(8,128)(2,1)S(1)}, u32[]{:S(2)}, u32[]{:S(2)}) collective-permute-start(bf16[32,32,128]{2,1,0:T(8,128)(2,1)S(1)} %get-tuple-element.21.same.refs_0_), channel_id=1, source_target_pairs={{0,4},{1,5},{4,8},{5,9},{8,12},{9,13},{12,14},{13,15},{14,10},{15,... | collective-permute-start | bytes 786440 | tf_op jit(solution)/shard_map/ppermute | solution.py:383
  6.0 0.0 collective-permute-start.3
  6.0 1.1 %collective-permute-start = (bf16[32,32,128]{2,1,0:T(8,128)(2,1)S(1)}, bf16[32,32,128]{2,1,0:T(8,128)(2,1)S(1)}, u32[]{:S(2)}, u32[]{:S(2)}) collective-permute-start(bf16[32,32,128]{2,1,0:T(8,128)(2,1)S(1)} %get-tuple-element.20.other), channel_id=1, source_target_pairs={{0,5},{1,4},{4,9},{5,8},{8,13},{9,12},{12,15},{13,14},{14,11},{15,... | collective-permute-start | bytes 786440 | tf_op jit(solution)/shard_map/ppermute | solution.py:383
  7.1 0.6 %collective-permute-start.1 = (bf16[32,32,128]{2,1,0:T(8,128)(2,1)S(1)}, bf16[32,32,128]{2,1,0:T(8,128)(2,1)S(1)}, u32[]{:S(2)}, u32[]{:S(2)}) collective-permute-start(bf16[32,32,128]{2,1,0:T(8,128)(2,1)S(1)} %get-tuple-element.20.other), channel_id=1, source_target_pairs={{0,3},{1,2},{4,1},{5,0},{8,5},{9,4},{12,9},{13,8},{14,13},{15,12},... | collective-permute-start | bytes 786440 | tf_op jit(solution)/shard_map/ppermute | solution.py:383
  7.7 5.8 %receiver_weights.1.weights = bf16[8192,128]{1,0:T(8,128)(2,1)S(1)} custom-call(bf16[32,32,128]{2,1,0:T(8,128)(2,1)S(1)} %get-tuple-element.21.same.refs_0_, bf16[32,32,128]{2,1,0:T(8,128)(2,1)S(1)} %get-tuple-element.20.other, bf16[32,32,128]{2,1,0:T(8,128)(2,1)S(1)} %collective-permute-done.4.far_same, ...), custom_call_target="tpu_custom_call" | custom-call | flops 1048576 | bytes 16384 | tf_op jit(solution)/shard_map/receiver_weights/pallas_call | solution.py:186
  13.5 1.6 %collective-permute-done.3.refs_2_ = bf16[32,32,128]{2,1,0:T(8,128)(2,1)S(1)} collective-permute-done((bf16[32,32,128]{2,1,0:T(8,128)(2,1)S(1)}, bf16[32,32,128]{2,1,0:T(8,128)(2,1)S(1)}, u32[]{:S(2)}, u32[]{:S(2)}) %collective-permute-start.3) | collective-permute-done | bytes 262176 | tf_op jit(solution)/shard_map/ppermute | solution.py:383
  15.2 1.6 %collective-permute-start.6 = (bf16[32,32,128]{2,1,0:T(8,128)(2,1)S(1)}, bf16[32,32,128]{2,1,0:T(8,128)(2,1)S(1)}, u32[]{:S(2)}, u32[]{:S(2)}) collective-permute-start(bf16[32,32,128]{2,1,0:T(8,128)(2,1)S(1)} %collective-permute-done.2.refs_0_), channel_id=1, source_target_pairs={{0,4},{1,5},{4,8},{5,9},{8,12},{9,13},{12,14},{13,15},{14,10},{15,... | collective-permute-start | bytes 786440 | tf_op jit(solution)/shard_map/ppermute | solution.py:383
  16.8 0.4 collective-permute-start.7
  17.2 1.1 %collective-permute-done.refs_1_ = bf16[32,32,128]{2,1,0:T(8,128)(2,1)S(1)} collective-permute-done((bf16[32,32,128]{2,1,0:T(8,128)(2,1)S(1)}, bf16[32,32,128]{2,1,0:T(8,128)(2,1)S(1)}, u32[]{:S(2)}, u32[]{:S(2)}) %collective-permute-start) | collective-permute-done | bytes 262176 | tf_op jit(solution)/shard_map/ppermute | solution.py:383
  18.3 0.1 collective-permute-done.1.refs_3_
  18.4 1.9 %collective-permute-start.11 = (bf16[32,32,128]{2,1,0:T(8,128)(2,1)S(1)}, bf16[32,32,128]{2,1,0:T(8,128)(2,1)S(1)}, u32[]{:S(2)}, u32[]{:S(2)}) collective-permute-start(bf16[32,32,128]{2,1,0:T(8,128)(2,1)S(1)} %collective-permute-done.1.refs_3_), channel_id=1, source_target_pairs={{0,2},{1,3},{4,0},{5,1},{8,4},{9,5},{12,8},{13,9},{14,12},{15,13},... | collective-permute-start | bytes 786440 | tf_op jit(solution)/shard_map/ppermute | solution.py:383
  20.3 0.1 collective-permute-start.10
  20.4 2.9 %stack.5.refs_4_ = bf16[4,32,64,128]{3,2,1,0:T(8,128)(2,1)} custom-call(s32[4]{0:T(128)S(1)} %copy-done.1, bf16[256,128]{1,0:T(8,128)(2,1)S(1)} %copy-done, bf16[8192,128]{1,0:T(8,128)(2,1)S(1)} %receiver_weights.1.weights, bf16[32,32,128]{2,1,0:T(8,128)(2,1)S(1)} %get-tuple-element.21.same.refs_0_, ...), custom_call_target="tpu_custom_call" | custom-call | flops 1048576 | bytes 16384 | tf_op jit(solution)/shard_map/stack/pallas_call | solution.py:342
  23.4 0.5 collective-permute-done.6.refs_0_
  23.8 2.6 %collective-permute-done.7.refs_2_ = bf16[32,32,128]{2,1,0:T(8,128)(2,1)S(1)} collective-permute-done((bf16[32,32,128]{2,1,0:T(8,128)(2,1)S(1)}, bf16[32,32,128]{2,1,0:T(8,128)(2,1)S(1)}, u32[]{:S(2)}, u32[]{:S(2)}) %collective-permute-start.7) | collective-permute-done | bytes 262176 | tf_op jit(solution)/shard_map/ppermute | solution.py:383
  26.4 1.6 %collective-permute-start.8 = (bf16[32,32,128]{2,1,0:T(8,128)(2,1)S(1)}, bf16[32,32,128]{2,1,0:T(8,128)(2,1)S(1)}, u32[]{:S(2)}, u32[]{:S(2)}) collective-permute-start(bf16[32,32,128]{2,1,0:T(8,128)(2,1)S(1)} %collective-permute-done.6.refs_0_), channel_id=1, source_target_pairs={{0,4},{1,5},{4,8},{5,9},{8,12},{9,13},{12,14},{13,15},{14,10},{15,... | collective-permute-start | bytes 786440 | tf_op jit(solution)/shard_map/ppermute | solution.py:383
  28.0 0.4 collective-permute-start.9
  28.4 3.6 %collective-permute-done.11.refs_3_ = bf16[32,32,128]{2,1,0:T(8,128)(2,1)S(1)} collective-permute-done((bf16[32,32,128]{2,1,0:T(8,128)(2,1)S(1)}, bf16[32,32,128]{2,1,0:T(8,128)(2,1)S(1)}, u32[]{:S(2)}, u32[]{:S(2)}) %collective-permute-start.11) | collective-permute-done | bytes 262176 | tf_op jit(solution)/shard_map/ppermute | solution.py:383
  32.0 0.0 collective-permute-start.13
  32.1 2.0 %collective-permute-start.15 = (bf16[32,32,128]{2,1,0:T(8,128)(2,1)S(1)}, bf16[32,32,128]{2,1,0:T(8,128)(2,1)S(1)}, u32[]{:S(2)}, u32[]{:S(2)}) collective-permute-start(bf16[32,32,128]{2,1,0:T(8,128)(2,1)S(1)} %collective-permute-done.10.refs_1_), channel_id=1, source_target_pairs={{0,4},{1,5},{4,8},{5,9},{8,12},{9,13},{12,14},{13,15},{14,10},{15,... | collective-permute-start | bytes 786440 | tf_op jit(solution)/shard_map/ppermute | solution.py:383
  34.1 3.0 %stack.6.refs_4_ = bf16[4,32,64,128]{3,2,1,0:T(8,128)(2,1)} custom-call(s32[4]{0:T(128)S(1)} %copy-done.1, bf16[256,128]{1,0:T(8,128)(2,1)S(1)} %copy-done, bf16[8192,128]{1,0:T(8,128)(2,1)S(1)} %receiver_weights.1.weights, bf16[32,32,128]{2,1,0:T(8,128)(2,1)S(1)} %collective-permute-done.2.refs_0_, ...), custom_call_target="tpu_custom_call", output_to_operand_aliasing={{}: (7, {})} | custom-call | flops 1048576 | bytes 16384 | tf_op jit(solution)/shard_map/stack/pallas_call | solution.py:342
  37.1 0.6 %collective-permute-done.9.refs_2_ = bf16[32,32,128]{2,1,0:T(8,128)(2,1)S(1)} collective-permute-done((bf16[32,32,128]{2,1,0:T(8,128)(2,1)S(1)}, bf16[32,32,128]{2,1,0:T(8,128)(2,1)S(1)}, u32[]{:S(2)}, u32[]{:S(2)}) %collective-permute-start.9) | collective-permute-done | bytes 262176 | tf_op jit(solution)/shard_map/ppermute | solution.py:383
  37.7 1.6 %collective-permute-start.12 = (bf16[32,32,128]{2,1,0:T(8,128)(2,1)S(1)}, bf16[32,32,128]{2,1,0:T(8,128)(2,1)S(1)}, u32[]{:S(2)}, u32[]{:S(2)}) collective-permute-start(bf16[32,32,128]{2,1,0:T(8,128)(2,1)S(1)} %collective-permute-done.8.refs_0_), channel_id=1, source_target_pairs={{0,4},{1,5},{4,8},{5,9},{8,12},{9,13},{12,14},{13,15},{14,10},{15,... | collective-permute-start | bytes 786440 | tf_op jit(solution)/shard_map/ppermute | solution.py:383
  39.2 2.9 %collective-permute-done.13.refs_3_ = bf16[32,32,128]{2,1,0:T(8,128)(2,1)S(1)} collective-permute-done((bf16[32,32,128]{2,1,0:T(8,128)(2,1)S(1)}, bf16[32,32,128]{2,1,0:T(8,128)(2,1)S(1)}, u32[]{:S(2)}, u32[]{:S(2)}) %collective-permute-start.13) | collective-permute-done | bytes 262176 | tf_op jit(solution)/shard_map/ppermute | solution.py:383
  42.1 0.3 collective-permute-start.14
  42.4 1.0 %stack.7.refs_4_ = bf16[4,32,64,128]{3,2,1,0:T(8,128)(2,1)} custom-call(s32[4]{0:T(128)S(1)} %copy-done.1, bf16[256,128]{1,0:T(8,128)(2,1)S(1)} %copy-done, bf16[8192,128]{1,0:T(8,128)(2,1)S(1)} %receiver_weights.1.weights, bf16[32,32,128]{2,1,0:T(8,128)(2,1)S(1)} %collective-permute-done.6.refs_0_, ...), custom_call_target="tpu_custom_call", output_to_operand_aliasing={{}: (7, {})} | custom-call | flops 1048576 | bytes 16384 | tf_op jit(solution)/shard_map/stack/pallas_call | solution.py:342
  43.4 3.0 %stack.8.refs_2_ = bf16[4,32,64,128]{3,2,1,0:T(8,128)(2,1)} custom-call(s32[4]{0:T(128)S(1)} %copy-done.1, bf16[256,128]{1,0:T(8,128)(2,1)S(1)} %copy-done, bf16[8192,128]{1,0:T(8,128)(2,1)S(1)} %receiver_weights.1.weights, bf16[32,32,128]{2,1,0:T(8,128)(2,1)S(1)} %collective-permute-done.8.refs_0_, ...), custom_call_target="tpu_custom_call", output_to_operand_aliasing={{}: (7, {})} | custom-call | flops 1048576 | bytes 16384 | tf_op jit(solution)/shard_map/stack/pallas_call | solution.py:342
  46.4 2.8 %collective-permute-done.14.refs_1_ = bf16[32,32,128]{2,1,0:T(8,128)(2,1)S(1)} collective-permute-done((bf16[32,32,128]{2,1,0:T(8,128)(2,1)S(1)}, bf16[32,32,128]{2,1,0:T(8,128)(2,1)S(1)}, u32[]{:S(2)}, u32[]{:S(2)}) %collective-permute-start.14) | collective-permute-done | bytes 262176 | tf_op jit(solution)/shard_map/ppermute | solution.py:383
  49.2 2.4 %stack.9 = bf16[4,32,64,128]{3,2,1,0:T(8,128)(2,1)} custom-call(s32[4]{0:T(128)S(1)} %copy-done.1, bf16[256,128]{1,0:T(8,128)(2,1)S(1)} %copy-done, bf16[8192,128]{1,0:T(8,128)(2,1)S(1)} %receiver_weights.1.weights, bf16[32,32,128]{2,1,0:T(8,128)(2,1)S(1)} %collective-permute-done.12.refs_0_, ...), custom_call_target="tpu_custom_call", output_to_operand_aliasing={{}: (5, {})} | custom-call | flops 1048576 | bytes 16384 | tf_op jit(solution)/shard_map/stack/pallas_call | solution.py:342
  (11 shorter events, 0.0 us)
Async XLA Ops:
  0.0 20.4 %copy-start = (bf16[256,128]{1,0:T(8,128)(2,1)S(1)}, bf16[256,128]{1,0:T(8,128)(2,1)}, u32[]{:S(2)}) copy-start(bf16[256,128]{1,0:T(8,128)(2,1)} %constant.3.table) | copy-start | bytes 196612
  0.0 20.4 %copy-start.1 = (s32[4]{0:T(128)S(1)}, s32[4]{0:T(128)}, u32[]{:S(2)}) copy-start(s32[4]{0:T(128)} %steps_in.9) | copy-start | bytes 52
  2.4 4.8 %collective-permute-start.4 = (bf16[32,32,128]{2,1,0:T(8,128)(2,1)S(1)}, bf16[32,32,128]{2,1,0:T(8,128)(2,1)S(1)}, u32[]{:S(2)}, u32[]{:S(2)}) collective-permute-start(bf16[32,32,128]{2,1,0:T(8,128)(2,1)S(1)} %get-tuple-element.21.same.refs_0_), channel_id=1, source_target_pairs={{0,1},{1,0},{2,3},{3,2},{4,5},{5,4},{6,7},{7,6},{8,9},{9,8},{10,11... | collective-permute-start | bytes 786440 | tf_op jit(solution)/shard_map/ppermute | solution.py:375
  2.9 4.8 %collective-permute-start.5 = (bf16[32,32,128]{2,1,0:T(8,128)(2,1)S(1)}, bf16[32,32,128]{2,1,0:T(8,128)(2,1)S(1)}, u32[]{:S(2)}, u32[]{:S(2)}) collective-permute-start(bf16[32,32,128]{2,1,0:T(8,128)(2,1)S(1)} %get-tuple-element.20.other), channel_id=1, source_target_pairs={{0,1},{1,0},{2,3},{3,2},{4,5},{5,4},{6,7},{7,6},{8,9},{9,8},{10,11... | collective-permute-start | bytes 786440 | tf_op jit(solution)/shard_map/ppermute | solution.py:375
  3.0 10.6 %collective-permute-start.2 = (bf16[32,32,128]{2,1,0:T(8,128)(2,1)S(1)}, bf16[32,32,128]{2,1,0:T(8,128)(2,1)S(1)}, u32[]{:S(2)}, u32[]{:S(2)}) collective-permute-start(bf16[32,32,128]{2,1,0:T(8,128)(2,1)S(1)} %get-tuple-element.21.same.refs_0_), channel_id=1, source_target_pairs={{0,4},{1,5},{4,8},{5,9},{8,12},{9,13},{12,14},{13,15},{14,10},{15,... | collective-permute-start | bytes 786440 | tf_op jit(solution)/shard_map/ppermute | solution.py:383
  6.0 9.2 %collective-permute-start.3 = (bf16[32,32,128]{2,1,0:T(8,128)(2,1)S(1)}, bf16[32,32,128]{2,1,0:T(8,128)(2,1)S(1)}, u32[]{:S(2)}, u32[]{:S(2)}) collective-permute-start(bf16[32,32,128]{2,1,0:T(8,128)(2,1)S(1)} %get-tuple-element.21.same.refs_0_), channel_id=1, source_target_pairs={{0,2},{1,3},{4,0},{5,1},{8,4},{9,5},{12,8},{13,9},{14,12},{15,13},... | collective-permute-start | bytes 786440 | tf_op jit(solution)/shard_map/ppermute | solution.py:383
  6.0 12.3 %collective-permute-start = (bf16[32,32,128]{2,1,0:T(8,128)(2,1)S(1)}, bf16[32,32,128]{2,1,0:T(8,128)(2,1)S(1)}, u32[]{:S(2)}, u32[]{:S(2)}) collective-permute-start(bf16[32,32,128]{2,1,0:T(8,128)(2,1)S(1)} %get-tuple-element.20.other), channel_id=1, source_target_pairs={{0,5},{1,4},{4,9},{5,8},{8,13},{9,12},{12,15},{13,14},{14,11},{15,... | collective-permute-start | bytes 786440 | tf_op jit(solution)/shard_map/ppermute | solution.py:383
  7.1 11.3 %collective-permute-start.1 = (bf16[32,32,128]{2,1,0:T(8,128)(2,1)S(1)}, bf16[32,32,128]{2,1,0:T(8,128)(2,1)S(1)}, u32[]{:S(2)}, u32[]{:S(2)}) collective-permute-start(bf16[32,32,128]{2,1,0:T(8,128)(2,1)S(1)} %get-tuple-element.20.other), channel_id=1, source_target_pairs={{0,3},{1,2},{4,1},{5,0},{8,5},{9,4},{12,9},{13,8},{14,13},{15,12},... | collective-permute-start | bytes 786440 | tf_op jit(solution)/shard_map/ppermute | solution.py:383
  15.2 8.7 %collective-permute-start.6 = (bf16[32,32,128]{2,1,0:T(8,128)(2,1)S(1)}, bf16[32,32,128]{2,1,0:T(8,128)(2,1)S(1)}, u32[]{:S(2)}, u32[]{:S(2)}) collective-permute-start(bf16[32,32,128]{2,1,0:T(8,128)(2,1)S(1)} %collective-permute-done.2.refs_0_), channel_id=1, source_target_pairs={{0,4},{1,5},{4,8},{5,9},{8,12},{9,13},{12,14},{13,15},{14,10},{15,... | collective-permute-start | bytes 786440 | tf_op jit(solution)/shard_map/ppermute | solution.py:383
  16.8 9.7 %collective-permute-start.7 = (bf16[32,32,128]{2,1,0:T(8,128)(2,1)S(1)}, bf16[32,32,128]{2,1,0:T(8,128)(2,1)S(1)}, u32[]{:S(2)}, u32[]{:S(2)}) collective-permute-start(bf16[32,32,128]{2,1,0:T(8,128)(2,1)S(1)} %collective-permute-done.3.refs_2_), channel_id=1, source_target_pairs={{0,2},{1,3},{4,0},{5,1},{8,4},{9,5},{12,8},{13,9},{14,12},{15,13},... | collective-permute-start | bytes 786440 | tf_op jit(solution)/shard_map/ppermute | solution.py:383
  18.4 13.6 %collective-permute-start.11 = (bf16[32,32,128]{2,1,0:T(8,128)(2,1)S(1)}, bf16[32,32,128]{2,1,0:T(8,128)(2,1)S(1)}, u32[]{:S(2)}, u32[]{:S(2)}) collective-permute-start(bf16[32,32,128]{2,1,0:T(8,128)(2,1)S(1)} %collective-permute-done.1.refs_3_), channel_id=1, source_target_pairs={{0,2},{1,3},{4,0},{5,1},{8,4},{9,5},{12,8},{13,9},{14,12},{15,13},... | collective-permute-start | bytes 786440 | tf_op jit(solution)/shard_map/ppermute | solution.py:383
  20.3 11.8 %collective-permute-start.10 = (bf16[32,32,128]{2,1,0:T(8,128)(2,1)S(1)}, bf16[32,32,128]{2,1,0:T(8,128)(2,1)S(1)}, u32[]{:S(2)}, u32[]{:S(2)}) collective-permute-start(bf16[32,32,128]{2,1,0:T(8,128)(2,1)S(1)} %collective-permute-done.refs_1_), channel_id=1, source_target_pairs={{0,4},{1,5},{4,8},{5,9},{8,12},{9,13},{12,14},{13,15},{14,10},{15,... | collective-permute-start | bytes 786440 | tf_op jit(solution)/shard_map/ppermute | solution.py:383
  26.4 10.7 %collective-permute-start.8 = (bf16[32,32,128]{2,1,0:T(8,128)(2,1)S(1)}, bf16[32,32,128]{2,1,0:T(8,128)(2,1)S(1)}, u32[]{:S(2)}, u32[]{:S(2)}) collective-permute-start(bf16[32,32,128]{2,1,0:T(8,128)(2,1)S(1)} %collective-permute-done.6.refs_0_), channel_id=1, source_target_pairs={{0,4},{1,5},{4,8},{5,9},{8,12},{9,13},{12,14},{13,15},{14,10},{15,... | collective-permute-start | bytes 786440 | tf_op jit(solution)/shard_map/ppermute | solution.py:383
  28.0 9.7 %collective-permute-start.9 = (bf16[32,32,128]{2,1,0:T(8,128)(2,1)S(1)}, bf16[32,32,128]{2,1,0:T(8,128)(2,1)S(1)}, u32[]{:S(2)}, u32[]{:S(2)}) collective-permute-start(bf16[32,32,128]{2,1,0:T(8,128)(2,1)S(1)} %collective-permute-done.7.refs_2_), channel_id=1, source_target_pairs={{0,2},{1,3},{4,0},{5,1},{8,4},{9,5},{12,8},{13,9},{14,12},{15,13},... | collective-permute-start | bytes 786440 | tf_op jit(solution)/shard_map/ppermute | solution.py:383
  32.0 10.0 %collective-permute-start.13 = (bf16[32,32,128]{2,1,0:T(8,128)(2,1)S(1)}, bf16[32,32,128]{2,1,0:T(8,128)(2,1)S(1)}, u32[]{:S(2)}, u32[]{:S(2)}) collective-permute-start(bf16[32,32,128]{2,1,0:T(8,128)(2,1)S(1)} %collective-permute-done.11.refs_3_), channel_id=1, source_target_pairs={{0,2},{1,3},{4,0},{5,1},{8,4},{9,5},{12,8},{13,9},{14,12},{15,13},... | collective-permute-start | bytes 786440 | tf_op jit(solution)/shard_map/ppermute | solution.py:383
  32.1 11.3 %collective-permute-start.15 = (bf16[32,32,128]{2,1,0:T(8,128)(2,1)S(1)}, bf16[32,32,128]{2,1,0:T(8,128)(2,1)S(1)}, u32[]{:S(2)}, u32[]{:S(2)}) collective-permute-start(bf16[32,32,128]{2,1,0:T(8,128)(2,1)S(1)} %collective-permute-done.10.refs_1_), channel_id=1, source_target_pairs={{0,4},{1,5},{4,8},{5,9},{8,12},{9,13},{12,14},{13,15},{14,10},{15,... | collective-permute-start | bytes 786440 | tf_op jit(solution)/shard_map/ppermute | solution.py:383
  37.7 8.7 %collective-permute-start.12 = (bf16[32,32,128]{2,1,0:T(8,128)(2,1)S(1)}, bf16[32,32,128]{2,1,0:T(8,128)(2,1)S(1)}, u32[]{:S(2)}, u32[]{:S(2)}) collective-permute-start(bf16[32,32,128]{2,1,0:T(8,128)(2,1)S(1)} %collective-permute-done.8.refs_0_), channel_id=1, source_target_pairs={{0,4},{1,5},{4,8},{5,9},{8,12},{9,13},{12,14},{13,15},{14,10},{15,... | collective-permute-start | bytes 786440 | tf_op jit(solution)/shard_map/ppermute | solution.py:383
  42.1 7.1 %collective-permute-start.14 = (bf16[32,32,128]{2,1,0:T(8,128)(2,1)S(1)}, bf16[32,32,128]{2,1,0:T(8,128)(2,1)S(1)}, u32[]{:S(2)}, u32[]{:S(2)}) collective-permute-start(bf16[32,32,128]{2,1,0:T(8,128)(2,1)S(1)} %collective-permute-done.13.refs_3_), channel_id=1, source_target_pairs={{0,2},{1,3},{4,0},{5,1},{8,4},{9,5},{12,8},{13,9},{14,12},{15,13},... | collective-permute-start | bytes 786440 | tf_op jit(solution)/shard_map/ppermute | solution.py:383

commit v4 on v3

--- a/solution.py
+++ b/solution.py
@@ -385,39 +385,47 @@
     table = lag_tables(windows * halves, bins)
 
     half = count // 2
-    tie = lax.optimization_barrier
-    early = (send(same, 1), send(same, -1))
+    early = [send(same, 1), send(other, -1, True)]
     far_same = across(same)
     far_other = across(other)
-    late = (send(other, 1, True), send(other, -1, True))
+    late = [send(other, 1, True), send(same, -1)]
     weights = receiver_weights(same, other, far_same, far_other)
     run = functools.partial(
         stack,
         out_shape=jax.ShapeDtypeStruct((steps, channels // 2, channels, LAGS), jnp.bfloat16),
     )
     rest = (tuple(ring), source_block, table)
+
+    def tie(pieces, token):
+        tied = []
+        for piece in pieces:
+            piece, token = lax.optimization_barrier((piece, token))
+            tied.append(piece)
+        return tied, token
+
     out = None
     held = []
     for hop in range(1, half):
         closing = hop == half - 1
         if hop == 1:
-            early, weights = tie((early, weights))
+            early, weights = tie(early, weights)
         else:
-            early, out = tie((early, out))
-        coming = (send(early[0], 1), None if closing else send(early[1], -1))
+            early, out = tie(early, out)
+        coming = [send(early[0], 1), send(early[1], -1)]
         if hop == 1:
-            late, weights = tie((late, weights))
-        held.append((early[0], late[0], early[1], late[1]))
-        later = (None if closing else send(late[0], 1), send(late[1], -1))
+            late, weights = tie(late, weights)
+        held.append((early[0], late[0], late[1], early[1]))
+        if not closing:
+            later = [send(late[0], 1), send(late[1], -1)]
         if hop == 1:
             out = run((0,), *rest, weights, (same, far_other), None)
         elif not closing:
-            late, out = tie((late, out))
+            late, out = tie(late, out)
             out = run((1 - hop, hop - 1), *rest, weights, held[hop - 2], out)
         early, late = coming, later
     for hop in range(half - 2, half):
         out = run((-hop, hop), *rest, weights, held[hop - 1], out)
-    return run((half,), *rest, weights, (early[0], late[1]), out)
+    return run((half,), *rest, weights, early, out)
 
 
 def solution(mesh):

time: 52 us -> 50.9 us (0.979)
  waiting for transfers between devices: 15.7 us -> 14.6 us
    ppermute x14, waiting for transfers between devices: 15.7 us -> 14.6 us  [send(): return lax.ppermute(x, ('chan', 'tm'), pairs)]
  transfers between devices with their start and end apart: 16 -> 16, of which waited for: 9 -> 7; matrix products, arithmetic and copies ran while one was open for 0% -> 0% of each run, Pallas kernels for 30% -> 31%
where the time goes in v4:
time: 50.9 us; the launch traced here: 50.8 us
  Pallas kernels  20.4 us (40%)
  starting transfers between devices  15.6 us (31%)
  waiting for transfers between devices  14.6 us (29%)
    ppermute x14, starting transfers between devices, send(): return lax.ppermute(x, ('chan', 'tm'), pairs)  15 us
    ppermute x14, waiting for transfers between devices, send(): return lax.ppermute(x, ('chan', 'tm'), pairs)  14.6 us
    pallas_call x5, Pallas kernels, stack(): pl.pallas_call(functools.partial(stack_kernel, tour, distances, first), o...  12.2 us
    pallas_call x1, Pallas kernels, receiver_weights(): pl.pallas_call(receiver_kernel, out_shape=jax.ShapeDtypeStruct((bins * 2...  5.8 us
    pallas_call x1, Pallas kernels, whiten(): pl.pallas_call(whiten_kernel, out_shape=(piece, piece), in_specs=[pl.Bloc...  2.37 us
  transfers between devices with their start and end apart: 16, of which 7 were waited for; matrix products, arithmetic and copies ran while one was open for 0% of the time, Pallas kernels for 31%

profile of v4, /device:TPU:0, one launch (start us, length us, event | category | flops | bytes accessed | tf_op | source)
XLA Modules:
  0.0 50.8 jit_solution(5898074969914218002)
XLA Ops:
  0.0 2.4 %whiten.1 = (bf16[32,32,128]{2,1,0:T(8,128)(2,1)S(1)}, bf16[32,32,128]{2,1,0:T(8,128)(2,1)S(1)}) custom-call(s32[64]{0:T(128)} %chan_in.1, s32[16]{0:T(128)} %win_in.1, bf16[64,32,128]{2,1,0:T(8,128)(2,1)} %bitcast.1), custom_call_target="tpu_custom_call" | custom-call | flops 1048576 | bytes 16384 | tf_op jit(solution)/shard_map/whiten/pallas_call | solution.py:140
  2.4 0.5 %collective-permute-start.4 = (bf16[32,32,128]{2,1,0:T(8,128)(2,1)S(1)}, bf16[32,32,128]{2,1,0:T(8,128)(2,1)S(1)}, u32[]{:S(2)}, u32[]{:S(2)}) collective-permute-start(bf16[32,32,128]{2,1,0:T(8,128)(2,1)S(1)} %get-tuple-element.25.same.refs_0_), channel_id=1, source_target_pairs={{0,1},{1,0},{2,3},{3,2},{4,5},{5,4},{6,7},{7,6},{8,9},{9,8},{10,11... | collective-permute-start | bytes 786440 | tf_op jit(solution)/shard_map/ppermute | solution.py:375
  2.9 0.1 collective-permute-start.5
  3.0 3.0 %collective-permute-start.3 = (bf16[32,32,128]{2,1,0:T(8,128)(2,1)S(1)}, bf16[32,32,128]{2,1,0:T(8,128)(2,1)S(1)}, u32[]{:S(2)}, u32[]{:S(2)}) collective-permute-start(bf16[32,32,128]{2,1,0:T(8,128)(2,1)S(1)} %get-tuple-element.25.same.refs_0_), channel_id=1, source_target_pairs={{0,4},{1,5},{4,8},{5,9},{8,12},{9,13},{12,14},{13,15},{14,10},{15,... | collective-permute-start | bytes 786440 | tf_op jit(solution)/shard_map/ppermute | solution.py:383
  6.0 0.0 collective-permute-start.2
  6.0 1.7 %collective-permute-start.1 = (bf16[32,32,128]{2,1,0:T(8,128)(2,1)S(1)}, bf16[32,32,128]{2,1,0:T(8,128)(2,1)S(1)}, u32[]{:S(2)}, u32[]{:S(2)}) collective-permute-start(bf16[32,32,128]{2,1,0:T(8,128)(2,1)S(1)} %get-tuple-element.26.other), channel_id=1, source_target_pairs={{0,5},{1,4},{4,9},{5,8},{8,13},{9,12},{12,15},{13,14},{14,11},{15,... | collective-permute-start | bytes 786440 | tf_op jit(solution)/shard_map/ppermute | solution.py:383
  7.7 0.0 collective-permute-done.4.far_same
  7.7 0.0 collective-permute-start
  7.7 5.8 %receiver_weights.1.weights = bf16[8192,128]{1,0:T(8,128)(2,1)S(1)} custom-call(bf16[32,32,128]{2,1,0:T(8,128)(2,1)S(1)} %get-tuple-element.25.same.refs_0_, bf16[32,32,128]{2,1,0:T(8,128)(2,1)S(1)} %get-tuple-element.26.other, bf16[32,32,128]{2,1,0:T(8,128)(2,1)S(1)} %collective-permute-done.4.far_same, ...), custom_call_target="tpu_custom_call" | custom-call | flops 1048576 | bytes 16384 | tf_op jit(solution)/shard_map/receiver_weights/pallas_call | solution.py:186
  13.5 0.0 collective-permute-done.3.refs_0_
  13.6 2.1 %collective-permute-start.6 = (bf16[32,32,128]{2,1,0:T(8,128)(2,1)S(1)}, bf16[32,32,128]{2,1,0:T(8,128)(2,1)S(1)}, u32[]{:S(2)}, u32[]{:S(2)}) collective-permute-start(bf16[32,32,128]{2,1,0:T(8,128)(2,1)S(1)} %collective-permute-done.3.refs_0_), channel_id=1, source_target_pairs={{0,4},{1,5},{4,8},{5,9},{8,12},{9,13},{12,14},{13,15},{14,10},{15,... | collective-permute-start | bytes 786440 | tf_op jit(solution)/shard_map/ppermute | solution.py:383
  15.6 0.0 collective-permute-start.10
  15.6 2.6 %collective-permute-done.1.refs_1_ = bf16[32,32,128]{2,1,0:T(8,128)(2,1)S(1)} collective-permute-done((bf16[32,32,128]{2,1,0:T(8,128)(2,1)S(1)}, bf16[32,32,128]{2,1,0:T(8,128)(2,1)S(1)}, u32[]{:S(2)}, u32[]{:S(2)}) %collective-permute-start.1) | collective-permute-done | bytes 262176 | tf_op jit(solution)/shard_map/ppermute | solution.py:383
  18.3 2.1 %collective-permute-done.refs_2_ = bf16[32,32,128]{2,1,0:T(8,128)(2,1)S(1)} collective-permute-done((bf16[32,32,128]{2,1,0:T(8,128)(2,1)S(1)}, bf16[32,32,128]{2,1,0:T(8,128)(2,1)S(1)}, u32[]{:S(2)}, u32[]{:S(2)}) %collective-permute-start) | collective-permute-done | bytes 262176 | tf_op jit(solution)/shard_map/ppermute | solution.py:383
  20.3 1.6 %collective-permute-start.9 = (bf16[32,32,128]{2,1,0:T(8,128)(2,1)S(1)}, bf16[32,32,128]{2,1,0:T(8,128)(2,1)S(1)}, u32[]{:S(2)}, u32[]{:S(2)}) collective-permute-start(bf16[32,32,128]{2,1,0:T(8,128)(2,1)S(1)} %collective-permute-done.1.refs_1_), channel_id=1, source_target_pairs={{0,4},{1,5},{4,8},{5,9},{8,12},{9,13},{12,14},{13,15},{14,10},{15,... | collective-permute-start | bytes 786440 | tf_op jit(solution)/shard_map/ppermute | solution.py:383
  21.9 0.4 collective-permute-start.8
  22.4 2.9 %stack.5.refs_4_ = bf16[4,32,64,128]{3,2,1,0:T(8,128)(2,1)} custom-call(s32[4]{0:T(128)S(1)} %copy-done.1, bf16[256,128]{1,0:T(8,128)(2,1)S(1)} %copy-done, bf16[8192,128]{1,0:T(8,128)(2,1)S(1)} %receiver_weights.1.weights, bf16[32,32,128]{2,1,0:T(8,128)(2,1)S(1)} %get-tuple-element.25.same.refs_0_, ...), custom_call_target="tpu_custom_call" | custom-call | flops 1048576 | bytes 16384 | tf_op jit(solution)/shard_map/stack/pallas_call | solution.py:342
  25.3 1.1 %collective-permute-start.7 = (bf16[32,32,128]{2,1,0:T(8,128)(2,1)S(1)}, bf16[32,32,128]{2,1,0:T(8,128)(2,1)S(1)}, u32[]{:S(2)}, u32[]{:S(2)}) collective-permute-start(bf16[32,32,128]{2,1,0:T(8,128)(2,1)S(1)} %collective-permute-done.6.refs_0_), channel_id=1, source_target_pairs={{0,4},{1,5},{4,8},{5,9},{8,12},{9,13},{12,14},{13,15},{14,10},{15,... | collective-permute-start | bytes 786440 | tf_op jit(solution)/shard_map/ppermute | solution.py:383
  26.4 1.0 %collective-permute-start.12 = (bf16[32,32,128]{2,1,0:T(8,128)(2,1)S(1)}, bf16[32,32,128]{2,1,0:T(8,128)(2,1)S(1)}, u32[]{:S(2)}, u32[]{:S(2)}) collective-permute-start(bf16[32,32,128]{2,1,0:T(8,128)(2,1)S(1)} %collective-permute-done.10.refs_3_), channel_id=1, source_target_pairs={{0,2},{1,3},{4,0},{5,1},{8,4},{9,5},{12,8},{13,9},{14,12},{15,13},... | collective-permute-start | bytes 786440 | tf_op jit(solution)/shard_map/ppermute | solution.py:383
  27.4 2.5 %collective-permute-done.9.refs_1_ = bf16[32,32,128]{2,1,0:T(8,128)(2,1)S(1)} collective-permute-done((bf16[32,32,128]{2,1,0:T(8,128)(2,1)S(1)}, bf16[32,32,128]{2,1,0:T(8,128)(2,1)S(1)}, u32[]{:S(2)}, u32[]{:S(2)}) %collective-permute-start.9) | collective-permute-done | bytes 262176 | tf_op jit(solution)/shard_map/ppermute | solution.py:383
  29.9 1.7 %collective-permute-done.8.refs_2_ = bf16[32,32,128]{2,1,0:T(8,128)(2,1)S(1)} collective-permute-done((bf16[32,32,128]{2,1,0:T(8,128)(2,1)S(1)}, bf16[32,32,128]{2,1,0:T(8,128)(2,1)S(1)}, u32[]{:S(2)}, u32[]{:S(2)}) %collective-permute-start.8) | collective-permute-done | bytes 262176 | tf_op jit(solution)/shard_map/ppermute | solution.py:383
  31.6 0.4 collective-permute-start.15
  32.0 1.6 %collective-permute-start.14 = (bf16[32,32,128]{2,1,0:T(8,128)(2,1)S(1)}, bf16[32,32,128]{2,1,0:T(8,128)(2,1)S(1)}, u32[]{:S(2)}, u32[]{:S(2)}) collective-permute-start(bf16[32,32,128]{2,1,0:T(8,128)(2,1)S(1)} %collective-permute-done.9.refs_1_), channel_id=1, source_target_pairs={{0,4},{1,5},{4,8},{5,9},{8,12},{9,13},{12,14},{13,15},{14,10},{15,... | collective-permute-start | bytes 786440 | tf_op jit(solution)/shard_map/ppermute | solution.py:383
  33.6 3.0 %stack.6.refs_4_ = bf16[4,32,64,128]{3,2,1,0:T(8,128)(2,1)} custom-call(s32[4]{0:T(128)S(1)} %copy-done.1, bf16[256,128]{1,0:T(8,128)(2,1)S(1)} %copy-done, bf16[8192,128]{1,0:T(8,128)(2,1)S(1)} %receiver_weights.1.weights, bf16[32,32,128]{2,1,0:T(8,128)(2,1)S(1)} %collective-permute-done.3.refs_0_, ...), custom_call_target="tpu_custom_call", output_to_operand_aliasing={{}: (7, {})} | custom-call | flops 1048576 | bytes 16384 | tf_op jit(solution)/shard_map/stack/pallas_call | solution.py:342
  36.6 0.6 %collective-permute-done.12.refs_3_ = bf16[32,32,128]{2,1,0:T(8,128)(2,1)S(1)} collective-permute-done((bf16[32,32,128]{2,1,0:T(8,128)(2,1)S(1)}, bf16[32,32,128]{2,1,0:T(8,128)(2,1)S(1)}, u32[]{:S(2)}, u32[]{:S(2)}) %collective-permute-start.12) | collective-permute-done | bytes 262176 | tf_op jit(solution)/shard_map/ppermute | solution.py:383
  37.2 1.4 %collective-permute-start.13 = (bf16[32,32,128]{2,1,0:T(8,128)(2,1)S(1)}, bf16[32,32,128]{2,1,0:T(8,128)(2,1)S(1)}, u32[]{:S(2)}, u32[]{:S(2)}) collective-permute-start(bf16[32,32,128]{2,1,0:T(8,128)(2,1)S(1)} %collective-permute-done.12.refs_3_), channel_id=1, source_target_pairs={{0,2},{1,3},{4,0},{5,1},{8,4},{9,5},{12,8},{13,9},{14,12},{15,13},... | collective-permute-start | bytes 786440 | tf_op jit(solution)/shard_map/ppermute | solution.py:383
  38.6 0.6 %collective-permute-start.11 = (bf16[32,32,128]{2,1,0:T(8,128)(2,1)S(1)}, bf16[32,32,128]{2,1,0:T(8,128)(2,1)S(1)}, u32[]{:S(2)}, u32[]{:S(2)}) collective-permute-start(bf16[32,32,128]{2,1,0:T(8,128)(2,1)S(1)} %collective-permute-done.7.refs_0_), channel_id=1, source_target_pairs={{0,4},{1,5},{4,8},{5,9},{8,12},{9,13},{12,14},{13,15},{14,10},{15,... | collective-permute-start | bytes 786440 | tf_op jit(solution)/shard_map/ppermute | solution.py:383
  39.2 3.2 %stack.7.refs_4_ = bf16[4,32,64,128]{3,2,1,0:T(8,128)(2,1)} custom-call(s32[4]{0:T(128)S(1)} %copy-done.1, bf16[256,128]{1,0:T(8,128)(2,1)S(1)} %copy-done, bf16[8192,128]{1,0:T(8,128)(2,1)S(1)} %receiver_weights.1.weights, bf16[32,32,128]{2,1,0:T(8,128)(2,1)S(1)} %collective-permute-done.6.refs_0_, ...), custom_call_target="tpu_custom_call", output_to_operand_aliasing={{}: (7, {})} | custom-call | flops 1048576 | bytes 16384 | tf_op jit(solution)/shard_map/stack/pallas_call | solution.py:342
  42.4 0.4 collective-permute-done.15.refs_2_
  42.8 0.8 %stack.8.refs_2_ = bf16[4,32,64,128]{3,2,1,0:T(8,128)(2,1)} custom-call(s32[4]{0:T(128)S(1)} %copy-done.1, bf16[256,128]{1,0:T(8,128)(2,1)S(1)} %copy-done, bf16[8192,128]{1,0:T(8,128)(2,1)S(1)} %receiver_weights.1.weights, bf16[32,32,128]{2,1,0:T(8,128)(2,1)S(1)} %collective-permute-done.7.refs_0_, ...), custom_call_target="tpu_custom_call", output_to_operand_aliasing={{}: (7, {})} | custom-call | flops 1048576 | bytes 16384 | tf_op jit(solution)/shard_map/stack/pallas_call | solution.py:342
  43.6 4.7 %collective-permute-done.13.refs_1_ = bf16[32,32,128]{2,1,0:T(8,128)(2,1)S(1)} collective-permute-done((bf16[32,32,128]{2,1,0:T(8,128)(2,1)S(1)}, bf16[32,32,128]{2,1,0:T(8,128)(2,1)S(1)}, u32[]{:S(2)}, u32[]{:S(2)}) %collective-permute-start.13) | collective-permute-done | bytes 262176 | tf_op jit(solution)/shard_map/ppermute | solution.py:383
  48.3 2.3 %stack.9 = bf16[4,32,64,128]{3,2,1,0:T(8,128)(2,1)} custom-call(s32[4]{0:T(128)S(1)} %copy-done.1, bf16[256,128]{1,0:T(8,128)(2,1)S(1)} %copy-done, bf16[8192,128]{1,0:T(8,128)(2,1)S(1)} %receiver_weights.1.weights, bf16[32,32,128]{2,1,0:T(8,128)(2,1)S(1)} %collective-permute-done.11.refs_0_, ...), custom_call_target="tpu_custom_call", output_to_operand_aliasing={{}: (5, {})} | custom-call | flops 1048576 | bytes 16384 | tf_op jit(solution)/shard_map/stack/pallas_call | solution.py:342
  (11 shorter events, 0.0 us)
Async XLA Ops:
  0.0 22.4 %copy-start = (bf16[256,128]{1,0:T(8,128)(2,1)S(1)}, bf16[256,128]{1,0:T(8,128)(2,1)}, u32[]{:S(2)}) copy-start(bf16[256,128]{1,0:T(8,128)(2,1)} %constant.3.table) | copy-start | bytes 196612
  0.0 22.4 %copy-start.1 = (s32[4]{0:T(128)S(1)}, s32[4]{0:T(128)}, u32[]{:S(2)}) copy-start(s32[4]{0:T(128)} %steps_in.9) | copy-start | bytes 52
  2.4 5.3 %collective-permute-start.4 = (bf16[32,32,128]{2,1,0:T(8,128)(2,1)S(1)}, bf16[32,32,128]{2,1,0:T(8,128)(2,1)S(1)}, u32[]{:S(2)}, u32[]{:S(2)}) collective-permute-start(bf16[32,32,128]{2,1,0:T(8,128)(2,1)S(1)} %get-tuple-element.25.same.refs_0_), channel_id=1, source_target_pairs={{0,1},{1,0},{2,3},{3,2},{4,5},{5,4},{6,7},{7,6},{8,9},{9,8},{10,11... | collective-permute-start | bytes 786440 | tf_op jit(solution)/shard_map/ppermute | solution.py:375
  2.9 4.8 %collective-permute-start.5 = (bf16[32,32,128]{2,1,0:T(8,128)(2,1)S(1)}, bf16[32,32,128]{2,1,0:T(8,128)(2,1)S(1)}, u32[]{:S(2)}, u32[]{:S(2)}) collective-permute-start(bf16[32,32,128]{2,1,0:T(8,128)(2,1)S(1)} %get-tuple-element.26.other), channel_id=1, source_target_pairs={{0,1},{1,0},{2,3},{3,2},{4,5},{5,4},{6,7},{7,6},{8,9},{9,8},{10,11... | collective-permute-start | bytes 786440 | tf_op jit(solution)/shard_map/ppermute | solution.py:375
  3.0 10.6 %collective-permute-start.3 = (bf16[32,32,128]{2,1,0:T(8,128)(2,1)S(1)}, bf16[32,32,128]{2,1,0:T(8,128)(2,1)S(1)}, u32[]{:S(2)}, u32[]{:S(2)}) collective-permute-start(bf16[32,32,128]{2,1,0:T(8,128)(2,1)S(1)} %get-tuple-element.25.same.refs_0_), channel_id=1, source_target_pairs={{0,4},{1,5},{4,8},{5,9},{8,12},{9,13},{12,14},{13,15},{14,10},{15,... | collective-permute-start | bytes 786440 | tf_op jit(solution)/shard_map/ppermute | solution.py:383
  6.0 9.6 %collective-permute-start.2 = (bf16[32,32,128]{2,1,0:T(8,128)(2,1)S(1)}, bf16[32,32,128]{2,1,0:T(8,128)(2,1)S(1)}, u32[]{:S(2)}, u32[]{:S(2)}) collective-permute-start(bf16[32,32,128]{2,1,0:T(8,128)(2,1)S(1)} %get-tuple-element.26.other), channel_id=1, source_target_pairs={{0,3},{1,2},{4,1},{5,0},{8,5},{9,4},{12,9},{13,8},{14,13},{15,12},... | collective-permute-start | bytes 786440 | tf_op jit(solution)/shard_map/ppermute | solution.py:383
  6.0 12.3 %collective-permute-start.1 = (bf16[32,32,128]{2,1,0:T(8,128)(2,1)S(1)}, bf16[32,32,128]{2,1,0:T(8,128)(2,1)S(1)}, u32[]{:S(2)}, u32[]{:S(2)}) collective-permute-start(bf16[32,32,128]{2,1,0:T(8,128)(2,1)S(1)} %get-tuple-element.26.other), channel_id=1, source_target_pairs={{0,5},{1,4},{4,9},{5,8},{8,13},{9,12},{12,15},{13,14},{14,11},{15,... | collective-permute-start | bytes 786440 | tf_op jit(solution)/shard_map/ppermute | solution.py:383
  7.7 12.6 %collective-permute-start = (bf16[32,32,128]{2,1,0:T(8,128)(2,1)S(1)}, bf16[32,32,128]{2,1,0:T(8,128)(2,1)S(1)}, u32[]{:S(2)}, u32[]{:S(2)}) collective-permute-start(bf16[32,32,128]{2,1,0:T(8,128)(2,1)S(1)} %get-tuple-element.25.same.refs_0_), channel_id=1, source_target_pairs={{0,2},{1,3},{4,0},{5,1},{8,4},{9,5},{12,8},{13,9},{14,12},{15,13},... | collective-permute-start | bytes 786440 | tf_op jit(solution)/shard_map/ppermute | solution.py:383
  13.6 11.7 %collective-permute-start.6 = (bf16[32,32,128]{2,1,0:T(8,128)(2,1)S(1)}, bf16[32,32,128]{2,1,0:T(8,128)(2,1)S(1)}, u32[]{:S(2)}, u32[]{:S(2)}) collective-permute-start(bf16[32,32,128]{2,1,0:T(8,128)(2,1)S(1)} %collective-permute-done.3.refs_0_), channel_id=1, source_target_pairs={{0,4},{1,5},{4,8},{5,9},{8,12},{9,13},{12,14},{13,15},{14,10},{15,... | collective-permute-start | bytes 786440 | tf_op jit(solution)/shard_map/ppermute | solution.py:383
  15.6 10.8 %collective-permute-start.10 = (bf16[32,32,128]{2,1,0:T(8,128)(2,1)S(1)}, bf16[32,32,128]{2,1,0:T(8,128)(2,1)S(1)}, u32[]{:S(2)}, u32[]{:S(2)}) collective-permute-start(bf16[32,32,128]{2,1,0:T(8,128)(2,1)S(1)} %collective-permute-done.2.refs_3_), channel_id=1, source_target_pairs={{0,2},{1,3},{4,0},{5,1},{8,4},{9,5},{12,8},{13,9},{14,12},{15,13},... | collective-permute-start | bytes 786440 | tf_op jit(solution)/shard_map/ppermute | solution.py:383
  20.3 9.5 %collective-permute-start.9 = (bf16[32,32,128]{2,1,0:T(8,128)(2,1)S(1)}, bf16[32,32,128]{2,1,0:T(8,128)(2,1)S(1)}, u32[]{:S(2)}, u32[]{:S(2)}) collective-permute-start(bf16[32,32,128]{2,1,0:T(8,128)(2,1)S(1)} %collective-permute-done.1.refs_1_), channel_id=1, source_target_pairs={{0,4},{1,5},{4,8},{5,9},{8,12},{9,13},{12,14},{13,15},{14,10},{15,... | collective-permute-start | bytes 786440 | tf_op jit(solution)/shard_map/ppermute | solution.py:383
  21.9 9.7 %collective-permute-start.8 = (bf16[32,32,128]{2,1,0:T(8,128)(2,1)S(1)}, bf16[32,32,128]{2,1,0:T(8,128)(2,1)S(1)}, u32[]{:S(2)}, u32[]{:S(2)}) collective-permute-start(bf16[32,32,128]{2,1,0:T(8,128)(2,1)S(1)} %collective-permute-done.refs_2_), channel_id=1, source_target_pairs={{0,2},{1,3},{4,0},{5,1},{8,4},{9,5},{12,8},{13,9},{14,12},{15,13},... | collective-permute-start | bytes 786440 | tf_op jit(solution)/shard_map/ppermute | solution.py:383
  25.3 11.3 %collective-permute-start.7 = (bf16[32,32,128]{2,1,0:T(8,128)(2,1)S(1)}, bf16[32,32,128]{2,1,0:T(8,128)(2,1)S(1)}, u32[]{:S(2)}, u32[]{:S(2)}) collective-permute-start(bf16[32,32,128]{2,1,0:T(8,128)(2,1)S(1)} %collective-permute-done.6.refs_0_), channel_id=1, source_target_pairs={{0,4},{1,5},{4,8},{5,9},{8,12},{9,13},{12,14},{13,15},{14,10},{15,... | collective-permute-start | bytes 786440 | tf_op jit(solution)/shard_map/ppermute | solution.py:383
  26.4 10.8 %collective-permute-start.12 = (bf16[32,32,128]{2,1,0:T(8,128)(2,1)S(1)}, bf16[32,32,128]{2,1,0:T(8,128)(2,1)S(1)}, u32[]{:S(2)}, u32[]{:S(2)}) collective-permute-start(bf16[32,32,128]{2,1,0:T(8,128)(2,1)S(1)} %collective-permute-done.10.refs_3_), channel_id=1, source_target_pairs={{0,2},{1,3},{4,0},{5,1},{8,4},{9,5},{12,8},{13,9},{14,12},{15,13},... | collective-permute-start | bytes 786440 | tf_op jit(solution)/shard_map/ppermute | solution.py:383
  31.6 11.2 %collective-permute-start.15 = (bf16[32,32,128]{2,1,0:T(8,128)(2,1)S(1)}, bf16[32,32,128]{2,1,0:T(8,128)(2,1)S(1)}, u32[]{:S(2)}, u32[]{:S(2)}) collective-permute-start(bf16[32,32,128]{2,1,0:T(8,128)(2,1)S(1)} %collective-permute-done.8.refs_2_), channel_id=1, source_target_pairs={{0,2},{1,3},{4,0},{5,1},{8,4},{9,5},{12,8},{13,9},{14,12},{15,13},... | collective-permute-start | bytes 786440 | tf_op jit(solution)/shard_map/ppermute | solution.py:383
  32.0 10.8 %collective-permute-start.14 = (bf16[32,32,128]{2,1,0:T(8,128)(2,1)S(1)}, bf16[32,32,128]{2,1,0:T(8,128)(2,1)S(1)}, u32[]{:S(2)}, u32[]{:S(2)}) collective-permute-start(bf16[32,32,128]{2,1,0:T(8,128)(2,1)S(1)} %collective-permute-done.9.refs_1_), channel_id=1, source_target_pairs={{0,4},{1,5},{4,8},{5,9},{8,12},{9,13},{12,14},{13,15},{14,10},{15,... | collective-permute-start | bytes 786440 | tf_op jit(solution)/shard_map/ppermute | solution.py:383
  37.2 11.1 %collective-permute-start.13 = (bf16[32,32,128]{2,1,0:T(8,128)(2,1)S(1)}, bf16[32,32,128]{2,1,0:T(8,128)(2,1)S(1)}, u32[]{:S(2)}, u32[]{:S(2)}) collective-permute-start(bf16[32,32,128]{2,1,0:T(8,128)(2,1)S(1)} %collective-permute-done.12.refs_3_), channel_id=1, source_target_pairs={{0,2},{1,3},{4,0},{5,1},{8,4},{9,5},{12,8},{13,9},{14,12},{15,13},... | collective-permute-start | bytes 786440 | tf_op jit(solution)/shard_map/ppermute | solution.py:383
  38.6 9.7 %collective-permute-start.11 = (bf16[32,32,128]{2,1,0:T(8,128)(2,1)S(1)}, bf16[32,32,128]{2,1,0:T(8,128)(2,1)S(1)}, u32[]{:S(2)}, u32[]{:S(2)}) collective-permute-start(bf16[32,32,128]{2,1,0:T(8,128)(2,1)S(1)} %collective-permute-done.7.refs_0_), channel_id=1, source_target_pairs={{0,4},{1,5},{4,8},{5,9},{8,12},{9,13},{12,14},{13,15},{14,10},{15,... | collective-permute-start | bytes 786440 | tf_op jit(solution)/shard_map/ppermute | solution.py:383

commit v5 on v4

--- a/solution.py
+++ b/solution.py
@@ -66,7 +66,7 @@
     return exchange(a, b, GROUP) + exchange(c, d, GROUP)
 
 
-def whiten_kernel(chan_in, win_in, spectra, same, other, held, chan_mask, win_mask, sems):
+def whiten_kernel(chan_in, win_in, spectra, same, other, both, held, chan_mask, win_mask, sems):
     rows, bins = spectra.shape[1:]
     half = same.shape[0]
     own = lax.axis_index("tm") * half
@@ -131,7 +131,9 @@
                     *(values[n * rows : (n + 1) * rows] for n in range(j, j + GROUP))
                 )
                 for n, one in enumerate(mixed):
-                    piece[i + j + n] = one.astype(jnp.bfloat16)
+                    one = one.astype(jnp.bfloat16)
+                    piece[i + j + n] = one
+                    both[side * half + i + j + n] = one
 
 
 def whiten(spectra, chan_mask, win_mask):
@@ -139,9 +141,9 @@
     piece = VMEM((channels // 2, rows, bins), jnp.bfloat16)
     return pl.pallas_call(
         whiten_kernel,
-        out_shape=(piece, piece),
+        out_shape=(piece, piece, VMEM((channels, rows, bins), jnp.bfloat16)),
         in_specs=[pl.BlockSpec(memory_space=pl.ANY)] * 3,
-        out_specs=(pl.BlockSpec(memory_space=VMEM),) * 2,
+        out_specs=(pl.BlockSpec(memory_space=VMEM),) * 3,
         scratch_shapes=[
             VMEM((2, channels // 2, rows, bins), jnp.bfloat16),
             SMEM(chan_mask.shape, chan_mask.dtype),
@@ -153,11 +155,11 @@
     )(chan_mask, win_mask, spectra)
 
 
-def receiver_kernel(same, other, far_same, far_other, weights, flat, wide, held, sems):
-    half, rows, bins = same.shape
+def receiver_kernel(both, far, weights, flat, wide, held, sems):
+    half, rows, bins = held.shape[1:]
     copies = [
-        pltpu.make_async_copy(piece, held.at[i], sems.at[i])
-        for i, piece in enumerate((same, far_other, other, far_same))
+        pltpu.make_async_copy(piece.at[pl.ds(start, half)], held.at[i], sems.at[i])
+        for i, (piece, start) in enumerate(((both, 0), (far, half), (both, half), (far, 0)))
     ]
     for copy in copies:
         copy.start()
@@ -181,12 +183,13 @@
     weights[...] = wide[...].astype(jnp.bfloat16)
 
 
-def receiver_weights(same, other, far_same, far_other):
-    half, rows, bins = same.shape
+def receiver_weights(both, far):
+    channels, rows, bins = both.shape
+    half = channels // 2
     return pl.pallas_call(
         receiver_kernel,
         out_shape=jax.ShapeDtypeStruct((bins * 2 * rows, 4 * half), jnp.bfloat16),
-        in_specs=[pl.BlockSpec(memory_space=pl.ANY)] * 4,
+        in_specs=[pl.BlockSpec(memory_space=pl.ANY)] * 2,
         out_specs=pl.BlockSpec(memory_space=VMEM),
         scratch_shapes=[
             VMEM((2 * half * 2 * rows, bins), jnp.float32),
@@ -197,20 +200,19 @@
         compiler_params=pltpu.CompilerParams(vmem_limit_bytes=24 << 20),
         cost_estimate=SMALL,
         name="receiver_weights",
-    )(same, other, far_same, far_other)
-
-
-def stack_kernel(tour, distances, first, steps_in, table, weights, *refs):
+    )(both, far)
+
+
+def stack_kernel(tour, distances, first, offset, steps_in, table, weights, *refs):
     blocks = len(distances)
     pieces = refs[: 2 * blocks]
     out = refs[2 * blocks + (0 if first else 1)]
-    steps, src, turned, cross, done, in_sem, out_sem, step_sem = refs[
-        2 * blocks + (1 if first else 2) :
-    ]
-    sources, rows, bins = pieces[0].shape
+    steps, turned, cross, done, out_sem, step_sem = refs[2 * blocks + (1 if first else 2) :]
+    sources, receivers, _ = done.shape[1:]
+    rows, bins = pieces[0].shape[1:]
     count = steps.shape[0]
     ring = len(tour)
-    staged = blocks > 1 or first
+    alone = blocks == 1 and not first
     lanes = 2 * rows
     per_tile = 128 // lanes
     tiles = GROUP // per_tile
@@ -218,7 +220,8 @@
     span = GROUP * GROUP
     row = lax.broadcasted_iota(jnp.int32, (span, 128), 0) % GROUP
     col = lax.broadcasted_iota(jnp.int32, (span, 128), 1) // lanes
-    receivers = weights.shape[1] // 2
+    near = pieces[0::2]
+    far = [piece.at[pl.ds(sources, sources)] if first else piece for piece in pieces[1::2]]
     me = lax.axis_index("chan")
     folded = tour[1] == 2
 
@@ -232,30 +235,23 @@
     part = sources // parts_out
     asked = pltpu.make_async_copy(steps_in, steps, step_sem)
     asked.start()
-    if staged:
+    if not alone:
         asked.wait()
         needed = [
             functools.reduce(jnp.logical_or, [steps[k] == owner for k in range(count)])
             for owner in owners
         ]
 
-    def arrival(b, h):
-        return pltpu.make_async_copy(pieces[2 * b + h], src.at[b, h], in_sem.at[b, h])
-
-    for b in range(blocks if staged else 0):
-        @pl.when(needed[b])
-        def _(b=b):
-            for h in range(2):
-                arrival(b, h).start()
-
     def departure(b, k, c):
         return pltpu.make_async_copy(
-            done.at[b, pl.ds(c * part, part)], out.at[k, pl.ds(c * part, part)], out_sem.at[b, k, c]
+            done.at[b, pl.ds(c * part, part)],
+            out.at[k, pl.ds(offset + c * part, part)],
+            out_sem.at[b, k, c],
         )
 
     def compute(b, owner):
         for s in range(sources):
-            parts = (src[b, 0, s], src[b, 1, s]) if staged else (pieces[0][s], pieces[1][s])
+            parts = (near[b][s], far[b][s])
             turned[s // GROUP, s % GROUP] = jnp.concatenate(parts * per_tile).T
         for m in range(bins // span):
             at = m * span
@@ -286,7 +282,7 @@
                     jnp.stack((one, two), axis=1).reshape(sources, 2 * GROUP, 2 * receivers)
                 )
             cross[:, at : at + span, :] = jnp.concatenate(eights, axis=1).astype(jnp.bfloat16)
-        if not staged:
+        if alone:
             asked.wait()
         for c in range(parts_out):
             turns = [cross[c * part + i].T for i in range(part)]
@@ -302,24 +298,11 @@
                 def _(k=k, c=c):
                     departure(b, k, c).start()
 
-    def turn(b, _):
-        later = b == blocks - 1
-        owner = jnp.where(later, owners[-1], owners[0])
-
-        @pl.when(jnp.where(later, needed[-1], needed[0]))
-        def _():
-            for i in range(blocks if staged else 0):
-                @pl.when(b == i)
-                def _(i=i):
-                    for h in range(2):
-                        arrival(i, h).wait()
-            compute(b, owner)
-        return 0
-
-    if staged:
-        lax.fori_loop(0, blocks, turn, 0)
-    else:
-        compute(0, owners[0])
+    for b in range(blocks):
+        if alone:
+            compute(b, owners[b])
+        else:
+            pl.when(needed[b])(functools.partial(compute, b, owners[b]))
     for b in range(blocks):
         for k in range(count):
             @pl.when(steps[k] == owners[b])
@@ -328,32 +311,26 @@
                     departure(b, k, c).wait()
 
 
-def stack(distances, tour, steps, table, weights, pieces, previous, out_shape):
+def stack(distances, tour, steps, table, weights, pieces, previous, out_shape, offset=0):
     blocks = len(distances)
+    first = previous is None
     sources, rows, bins = pieces[0].shape
     receivers = weights.shape[1] // 2
     count = steps.shape[0]
-    first = previous is None
-    if first:
-        kinds = [pl.ANY, pl.ANY]
-    else:
-        kinds = [VMEM if blocks == 1 else pl.ANY] * len(pieces) + [pl.ANY]
     args = [steps, table, weights, *pieces] + ([] if first else [previous])
     return pl.pallas_call(
-        functools.partial(stack_kernel, tour, distances, first),
+        functools.partial(stack_kernel, tour, distances, first, offset),
         out_shape=out_shape,
         in_specs=[pl.BlockSpec(memory_space=pl.ANY)]
-        + [pl.BlockSpec(memory_space=VMEM)] * 2
-        + [pl.BlockSpec(memory_space=kind) for kind in kinds],
+        + [pl.BlockSpec(memory_space=VMEM)] * (2 + len(pieces))
+        + [pl.BlockSpec(memory_space=pl.ANY)] * (0 if first else 1),
         out_specs=pl.BlockSpec(memory_space=pl.ANY),
         scratch_shapes=[
             SMEM(steps.shape, steps.dtype),
-            VMEM((blocks, 2, sources, rows, bins), jnp.bfloat16),
             VMEM((sources // GROUP, GROUP, bins, 128), jnp.bfloat16),
             VMEM((sources, bins, 2 * receivers), jnp.bfloat16),
             VMEM((blocks, sources, receivers, LAGS), jnp.bfloat16),
-            pltpu.SemaphoreType.DMA((blocks, 2)),
-            pltpu.SemaphoreType.DMA((blocks, count, 4 if blocks == 1 else 2)),
+            pltpu.SemaphoreType.DMA((blocks, count, 2)),
             pltpu.SemaphoreType.DMA,
         ],
         input_output_aliases={} if first else {len(args) - 1: 0},
@@ -369,10 +346,7 @@
     steps = source_block.shape[0]
     halves = lax.axis_size("tm")
     rows = spectra.reshape(channels, windows * parts, bins)
-    same, other = whiten(rows, channel_mask, window_mask)
-
-    def across(x):
-        return lax.ppermute(x, "tm", [(0, 1), (1, 0)])
+    same, other, both = whiten(rows, channel_mask, window_mask)
 
     def send(x, direction, cross=False):
         pairs = []
@@ -386,10 +360,9 @@
 
     half = count // 2
     early = [send(same, 1), send(other, -1, True)]
-    far_same = across(same)
-    far_other = across(other)
+    far = lax.ppermute(both, "tm", [(0, 1), (1, 0)])
     late = [send(other, 1, True), send(same, -1)]
-    weights = receiver_weights(same, other, far_same, far_other)
+    weights = receiver_weights(both, far)
     run = functools.partial(
         stack,
         out_shape=jax.ShapeDtypeStruct((steps, channels // 2, channels, LAGS), jnp.bfloat16),
@@ -411,21 +384,31 @@
             early, weights = tie(early, weights)
         else:
             early, out = tie(early, out)
-        coming = [send(early[0], 1), send(early[1], -1)]
+        shares = 2 if closing else 1
+        share = channels // 2 // shares
+        coming = [
+            [send(piece[i * share : (i + 1) * share], way) for piece, way in zip(early, (1, -1))]
+            for i in range(shares)
+        ]
         if hop == 1:
             late, weights = tie(late, weights)
         held.append((early[0], late[0], late[1], early[1]))
+        if hop == 1:
+            out = run((0,), *rest, weights, (same, far), None)
+        elif not closing:
+            out = run((1 - hop, hop - 1), *rest, weights, held[hop - 2], out)
+            late, out = tie(late, out)
         if not closing:
             later = [send(late[0], 1), send(late[1], -1)]
-        if hop == 1:
-            out = run((0,), *rest, weights, (same, far_other), None)
-        elif not closing:
-            late, out = tie(late, out)
-            out = run((1 - hop, hop - 1), *rest, weights, held[hop - 2], out)
-        early, late = coming, later
-    for hop in range(half - 2, half):
-        out = run((-hop, hop), *rest, weights, held[hop - 1], out)
-    return run((half,), *rest, weights, early, out)
+        if 1 < hop == half - 2:
+            out = run((-hop, hop), *rest, weights, held[hop - 1], out)
+        if not closing:
+            (early,), late = coming, later
+    hop = half - 1
+    out = run((-hop, hop), *rest, weights, held[hop - 1], out)
+    for i, pieces in enumerate(coming):
+        out = run((half,), *rest, weights, pieces, out, offset=i * share)
+    return out
 
 
 def solution(mesh):

time: 50.9 us -> 50.4 us (level)
  waiting for transfers between devices: 14.6 us -> 11.2 us
  starting transfers between devices: 15.6 us -> 18 us
  Pallas kernels: 20.4 us -> 21.2 us
    ppermute x14 -> x16, waiting for transfers between devices: 14.6 us -> 11.2 us  [send(): return lax.ppermute(x, ('chan', 'tm'), pairs)]
    ppermute x14 -> x16, starting transfers between devices: 15 us -> 17.5 us  [send(): return lax.ppermute(x, ('chan', 'tm'), pairs)]
    pallas_call x6 -> x7, Pallas kernels: 14.6 us -> 15.4 us  [the longest x6 13.1 us: stack(): pl.pallas_call(functools.partial(stack_kernel, tour, distances, first, of...]
  transfers between devices with their start and end apart: 16 -> 17, of which waited for: 7 -> 6; matrix products, arithmetic and copies ran while one was open for 0% -> 0% of each run, Pallas kernels for 31% -> 34%
where the time goes in v5:
time: 50.4 us; the launch traced here: 50.7 us
  Pallas kernels  21.2 us (42%)
  starting transfers between devices  18 us (36%)
  waiting for transfers between devices  11.2 us (22%)
    ppermute x16, starting transfers between devices, send(): return lax.ppermute(x, ('chan', 'tm'), pairs)  17.5 us
    pallas_call x6, Pallas kernels, stack(): pl.pallas_call(functools.partial(stack_kernel, tour, distances, first, of...  13.1 us
    ppermute x16, waiting for transfers between devices, send(): return lax.ppermute(x, ('chan', 'tm'), pairs)  11.2 us
    pallas_call x1, Pallas kernels, receiver_weights(): pl.pallas_call(receiver_kernel, out_shape=jax.ShapeDtypeStruct((bins * 2...  5.79 us
    pallas_call x1, Pallas kernels, whiten(): pl.pallas_call(whiten_kernel, out_shape=(piece, piece, VMEM((channels, ro...  2.37 us
  transfers between devices with their start and end apart: 17, of which 6 were waited for; matrix products, arithmetic and copies ran while one was open for 0% of the time, Pallas kernels for 34%

profile of v5, /device:TPU:0, one launch (start us, length us, event | category | flops | bytes accessed | tf_op | source)
XLA Modules:
  0.0 50.7 jit_solution(16866810185835325099)
XLA Ops:
  0.0 2.4 %whiten.1 = (bf16[32,32,128]{2,1,0:T(8,128)(2,1)S(1)}, bf16[32,32,128]{2,1,0:T(8,128)(2,1)S(1)}, bf16[64,32,128]{2,1,0:T(8,128)(2,1)S(1)}) custom-call(s32[64]{0:T(128)} %chan_in.1, s32[16]{0:T(128)} %win_in.1, bf16[64,32,128]{2,1,0:T(8,128)(2,1)} %bitcast.1), custom_call_target="tpu_custom_call" | custom-call | flops 1048576 | bytes 16384 | tf_op jit(solution)/shard_map/whiten/pallas_call | solution.py:142
  2.4 0.5 %collective-permute-start.4 = (bf16[64,32,128]{2,1,0:T(8,128)(2,1)S(1)}, bf16[64,32,128]{2,1,0:T(8,128)(2,1)S(1)}, u32[]{:S(2)}, u32[]{:S(2)}) collective-permute-start(bf16[64,32,128]{2,1,0:T(8,128)(2,1)S(1)} %get-tuple-element.30.both), channel_id=1, source_target_pairs={{0,1},{1,0},{2,3},{3,2},{4,5},{5,4},{6,7},{7,6},{8,9},{9,8},{10,11... | collective-permute-start | bytes 1572872 | tf_op jit(solution)/shard_map/ppermute | solution.py:363
  2.9 2.6 %collective-permute-start.3 = (bf16[32,32,128]{2,1,0:T(8,128)(2,1)S(1)}, bf16[32,32,128]{2,1,0:T(8,128)(2,1)S(1)}, u32[]{:S(2)}, u32[]{:S(2)}) collective-permute-start(bf16[32,32,128]{2,1,0:T(8,128)(2,1)S(1)} %get-tuple-element.28.refs_0_), channel_id=1, source_target_pairs={{0,4},{1,5},{4,8},{5,9},{8,12},{9,13},{12,14},{13,15},{14,10},{15,... | collective-permute-start | bytes 786440 | tf_op jit(solution)/shard_map/ppermute | solution.py:357
  5.5 0.0 collective-permute-start.2
  5.5 1.7 %collective-permute-start.1 = (bf16[32,32,128]{2,1,0:T(8,128)(2,1)S(1)}, bf16[32,32,128]{2,1,0:T(8,128)(2,1)S(1)}, u32[]{:S(2)}, u32[]{:S(2)}) collective-permute-start(bf16[32,32,128]{2,1,0:T(8,128)(2,1)S(1)} %get-tuple-element.29), channel_id=1, source_target_pairs={{0,5},{1,4},{4,9},{5,8},{8,13},{9,12},{12,15},{13,14},{14,11},{15,... | collective-permute-start | bytes 786440 | tf_op jit(solution)/shard_map/ppermute | solution.py:357
  7.3 0.1 collective-permute-start
  7.3 5.8 %receiver_weights.1.weights = bf16[8192,128]{1,0:T(8,128)(2,1)S(1)} custom-call(bf16[64,32,128]{2,1,0:T(8,128)(2,1)S(1)} %get-tuple-element.30.both, bf16[64,32,128]{2,1,0:T(8,128)(2,1)S(1)} %collective-permute-done.4.far.refs_1_), custom_call_target="tpu_custom_call" | custom-call | flops 1048576 | bytes 16384 | tf_op jit(solution)/shard_map/receiver_weights/pallas_call | solution.py:189
  13.1 0.0 collective-permute-done.3.refs_0_
  13.2 2.0 %collective-permute-start.5 = (bf16[32,32,128]{2,1,0:T(8,128)(2,1)S(1)}, bf16[32,32,128]{2,1,0:T(8,128)(2,1)S(1)}, u32[]{:S(2)}, u32[]{:S(2)}) collective-permute-start(bf16[32,32,128]{2,1,0:T(8,128)(2,1)S(1)} %collective-permute-done.3.refs_0_), channel_id=1, source_target_pairs={{0,4},{1,5},{4,8},{5,9},{8,12},{9,13},{12,14},{13,15},{14,10},{15,... | collective-permute-start | bytes 786440 | tf_op jit(solution)/shard_map/ppermute | solution.py:357
  15.2 0.1 collective-permute-start.9
  15.2 2.5 %collective-permute-done.1.refs_1_ = bf16[32,32,128]{2,1,0:T(8,128)(2,1)S(1)} collective-permute-done((bf16[32,32,128]{2,1,0:T(8,128)(2,1)S(1)}, bf16[32,32,128]{2,1,0:T(8,128)(2,1)S(1)}, u32[]{:S(2)}, u32[]{:S(2)}) %collective-permute-start.1) | collective-permute-done | bytes 262176 | tf_op jit(solution)/shard_map/ppermute | solution.py:357
  17.8 2.3 %collective-permute-done.refs_2_ = bf16[32,32,128]{2,1,0:T(8,128)(2,1)S(1)} collective-permute-done((bf16[32,32,128]{2,1,0:T(8,128)(2,1)S(1)}, bf16[32,32,128]{2,1,0:T(8,128)(2,1)S(1)}, u32[]{:S(2)}, u32[]{:S(2)}) %collective-permute-start) | collective-permute-done | bytes 262176 | tf_op jit(solution)/shard_map/ppermute | solution.py:357
  20.1 1.6 %collective-permute-start.7 = (bf16[32,32,128]{2,1,0:T(8,128)(2,1)S(1)}, bf16[32,32,128]{2,1,0:T(8,128)(2,1)S(1)}, u32[]{:S(2)}, u32[]{:S(2)}) collective-permute-start(bf16[32,32,128]{2,1,0:T(8,128)(2,1)S(1)} %collective-permute-done.1.refs_1_), channel_id=1, source_target_pairs={{0,4},{1,5},{4,8},{5,9},{8,12},{9,13},{12,14},{13,15},{14,10},{15,... | collective-permute-start | bytes 786440 | tf_op jit(solution)/shard_map/ppermute | solution.py:357
  21.7 0.4 collective-permute-start.8
  22.1 2.8 %stack.6.refs_4_ = bf16[4,32,64,128]{3,2,1,0:T(8,128)(2,1)} custom-call(s32[4]{0:T(128)S(1)} %copy-done.1, bf16[256,128]{1,0:T(8,128)(2,1)S(1)} %copy-done, bf16[8192,128]{1,0:T(8,128)(2,1)S(1)} %receiver_weights.1.weights, bf16[32,32,128]{2,1,0:T(8,128)(2,1)S(1)} %get-tuple-element.28.refs_0_, bf16[64,32,128]{2,1,0:T(8,128)(2,1)S(1)} %collective-permute-done.4.far.refs_1_), custom_call_target="tpu_custom_call" | custom-call | flops 1048576 | bytes 16384 | tf_op jit(solution)/shard_map/stack/pallas_call | solution.py:321
  25.0 0.9 %collective-permute-start.6 = (bf16[32,32,128]{2,1,0:T(8,128)(2,1)S(1)}, bf16[32,32,128]{2,1,0:T(8,128)(2,1)S(1)}, u32[]{:S(2)}, u32[]{:S(2)}) collective-permute-start(bf16[32,32,128]{2,1,0:T(8,128)(2,1)S(1)} %collective-permute-done.5.refs_0_), channel_id=1, source_target_pairs={{0,4},{1,5},{4,8},{5,9},{8,12},{9,13},{12,14},{13,15},{14,10},{15,... | collective-permute-start | bytes 786440 | tf_op jit(solution)/shard_map/ppermute | solution.py:357
  25.9 1.2 %collective-permute-start.11 = (bf16[32,32,128]{2,1,0:T(8,128)(2,1)S(1)}, bf16[32,32,128]{2,1,0:T(8,128)(2,1)S(1)}, u32[]{:S(2)}, u32[]{:S(2)}) collective-permute-start(bf16[32,32,128]{2,1,0:T(8,128)(2,1)S(1)} %collective-permute-done.9.refs_3_), channel_id=1, source_target_pairs={{0,2},{1,3},{4,0},{5,1},{8,4},{9,5},{12,8},{13,9},{14,12},{15,13},... | collective-permute-start | bytes 786440 | tf_op jit(solution)/shard_map/ppermute | solution.py:357
  27.1 0.7 %stack.7.refs_4_ = bf16[4,32,64,128]{3,2,1,0:T(8,128)(2,1)} custom-call(s32[4]{0:T(128)S(1)} %copy-done.1, bf16[256,128]{1,0:T(8,128)(2,1)S(1)} %copy-done, bf16[8192,128]{1,0:T(8,128)(2,1)S(1)} %receiver_weights.1.weights, bf16[32,32,128]{2,1,0:T(8,128)(2,1)S(1)} %collective-permute-done.3.refs_0_, ...), custom_call_target="tpu_custom_call", output_to_operand_aliasing={{}: (7, {})} | custom-call | flops 1048576 | bytes 16384 | tf_op jit(solution)/shard_map/stack/pallas_call | solution.py:321
  27.8 1.7 %collective-permute-done.7.refs_1_ = bf16[32,32,128]{2,1,0:T(8,128)(2,1)S(1)} collective-permute-done((bf16[32,32,128]{2,1,0:T(8,128)(2,1)S(1)}, bf16[32,32,128]{2,1,0:T(8,128)(2,1)S(1)}, u32[]{:S(2)}, u32[]{:S(2)}) %collective-permute-start.7) | collective-permute-done | bytes 262176 | tf_op jit(solution)/shard_map/ppermute | solution.py:357
  29.5 1.8 %collective-permute-done.8.refs_2_ = bf16[32,32,128]{2,1,0:T(8,128)(2,1)S(1)} collective-permute-done((bf16[32,32,128]{2,1,0:T(8,128)(2,1)S(1)}, bf16[32,32,128]{2,1,0:T(8,128)(2,1)S(1)}, u32[]{:S(2)}, u32[]{:S(2)}) %collective-permute-start.8) | collective-permute-done | bytes 262176 | tf_op jit(solution)/shard_map/ppermute | solution.py:357
  31.3 1.0 %collective-permute-start.16 = (bf16[32,32,128]{2,1,0:T(8,128)(2,1)S(1)}, bf16[32,32,128]{2,1,0:T(8,128)(2,1)S(1)}, u32[]{:S(2)}, u32[]{:S(2)}) collective-permute-start(bf16[32,32,128]{2,1,0:T(8,128)(2,1)S(1)} %collective-permute-done.8.refs_2_), channel_id=1, source_target_pairs={{0,2},{1,3},{4,0},{5,1},{8,4},{9,5},{12,8},{13,9},{14,12},{15,13},... | collective-permute-start | bytes 786440 | tf_op jit(solution)/shard_map/ppermute | solution.py:357
  32.3 1.1 %collective-permute-start.15 = (bf16[32,32,128]{2,1,0:T(8,128)(2,1)S(1)}, bf16[32,32,128]{2,1,0:T(8,128)(2,1)S(1)}, u32[]{:S(2)}, u32[]{:S(2)}) collective-permute-start(bf16[32,32,128]{2,1,0:T(8,128)(2,1)S(1)} %collective-permute-done.7.refs_1_), channel_id=1, source_target_pairs={{0,4},{1,5},{4,8},{5,9},{8,12},{9,13},{12,14},{13,15},{14,10},{15,... | collective-permute-start | bytes 786440 | tf_op jit(solution)/shard_map/ppermute | solution.py:357
  33.4 3.1 %stack.8.refs_4_ = bf16[4,32,64,128]{3,2,1,0:T(8,128)(2,1)} custom-call(s32[4]{0:T(128)S(1)} %copy-done.1, bf16[256,128]{1,0:T(8,128)(2,1)S(1)} %copy-done, bf16[8192,128]{1,0:T(8,128)(2,1)S(1)} %receiver_weights.1.weights, bf16[32,32,128]{2,1,0:T(8,128)(2,1)S(1)} %collective-permute-done.5.refs_0_, ...), custom_call_target="tpu_custom_call", output_to_operand_aliasing={{}: (7, {})} | custom-call | flops 1048576 | bytes 16384 | tf_op jit(solution)/shard_map/stack/pallas_call | solution.py:321
  36.5 0.5 collective-permute-done.11.refs_3_
  37.0 0.6 %collective-permute-start.14 = (bf16[16,32,128]{2,1,0:T(8,128)(2,1)S(1)}, bf16[16,32,128]{2,1,0:T(8,128)(2,1)S(1)}, u32[]{:S(2)}, u32[]{:S(2)}) collective-permute-start(bf16[16,32,128]{2,1,0:T(8,128)(2,1)S(1)} %get-tuple-element.51), channel_id=1, source_target_pairs={{0,2},{1,3},{4,0},{5,1},{8,4},{9,5},{12,8},{13,9},{14,12},{15,13},... | collective-permute-start | bytes 393224 | tf_op jit(solution)/shard_map/ppermute | solution.py:357
  37.6 1.6 %collective-permute-start.13 = (bf16[16,32,128]{2,1,0:T(8,128)(2,1)S(1)}, bf16[16,32,128]{2,1,0:T(8,128)(2,1)S(1)}, u32[]{:S(2)}, u32[]{:S(2)}) collective-permute-start(bf16[16,32,128]{2,1,0:T(8,128)(2,1)S(1)} %get-tuple-element.53), channel_id=1, source_target_pairs={{0,4},{1,5},{4,8},{5,9},{8,12},{9,13},{12,14},{13,15},{14,10},{15,... | collective-permute-start | bytes 393224 | tf_op jit(solution)/shard_map/ppermute | solution.py:357
  39.1 1.1 %collective-permute-start.12 = (bf16[16,32,128]{2,1,0:T(8,128)(2,1)S(1)}, bf16[16,32,128]{2,1,0:T(8,128)(2,1)S(1)}, u32[]{:S(2)}, u32[]{:S(2)}) collective-permute-start(bf16[16,32,128]{2,1,0:T(8,128)(2,1)S(1)} %get-tuple-element.52), channel_id=1, source_target_pairs={{0,2},{1,3},{4,0},{5,1},{8,4},{9,5},{12,8},{13,9},{14,12},{15,13},... | collective-permute-start | bytes 393224 | tf_op jit(solution)/shard_map/ppermute | solution.py:357
  40.3 2.3 %collective-permute-done.16.refs_2_ = bf16[32,32,128]{2,1,0:T(8,128)(2,1)S(1)} collective-permute-done((bf16[32,32,128]{2,1,0:T(8,128)(2,1)S(1)}, bf16[32,32,128]{2,1,0:T(8,128)(2,1)S(1)}, u32[]{:S(2)}, u32[]{:S(2)}) %collective-permute-start.16) | collective-permute-done | bytes 262176 | tf_op jit(solution)/shard_map/ppermute | solution.py:357
  42.6 1.6 %collective-permute-start.10 = (bf16[16,32,128]{2,1,0:T(8,128)(2,1)S(1)}, bf16[16,32,128]{2,1,0:T(8,128)(2,1)S(1)}, u32[]{:S(2)}, u32[]{:S(2)}) collective-permute-start(bf16[16,32,128]{2,1,0:T(8,128)(2,1)S(1)} %get-tuple-element.54), channel_id=1, source_target_pairs={{0,4},{1,5},{4,8},{5,9},{8,12},{9,13},{12,14},{13,15},{14,10},{15,... | collective-permute-start | bytes 393224 | tf_op jit(solution)/shard_map/ppermute | solution.py:357
  44.2 2.9 %stack.9.refs_2_ = bf16[4,32,64,128]{3,2,1,0:T(8,128)(2,1)} custom-call(s32[4]{0:T(128)S(1)} %copy-done.1, bf16[256,128]{1,0:T(8,128)(2,1)S(1)} %copy-done, bf16[8192,128]{1,0:T(8,128)(2,1)S(1)} %receiver_weights.1.weights, bf16[32,32,128]{2,1,0:T(8,128)(2,1)S(1)} %collective-permute-done.6.refs_0_, ...), custom_call_target="tpu_custom_call", output_to_operand_aliasing={{}: (7, {})} | custom-call | flops 1048576 | bytes 16384 | tf_op jit(solution)/shard_map/stack/pallas_call | solution.py:321
  47.1 1.7 %stack.10.refs_2_ = bf16[4,32,64,128]{3,2,1,0:T(8,128)(2,1)} custom-call(s32[4]{0:T(128)S(1)} %copy-done.1, bf16[256,128]{1,0:T(8,128)(2,1)S(1)} %copy-done, bf16[8192,128]{1,0:T(8,128)(2,1)S(1)} %receiver_weights.1.weights, bf16[16,32,128]{2,1,0:T(8,128)(2,1)S(1)} %collective-permute-done.13.refs_0_, ...), custom_call_target="tpu_custom_call", output_to_operand_aliasing={{}: (5, {})} | custom-call | flops 1048576 | bytes 16384 | tf_op jit(solution)/shard_map/stack/pallas_call | solution.py:321
  48.9 1.7 %stack.11 = bf16[4,32,64,128]{3,2,1,0:T(8,128)(2,1)} custom-call(s32[4]{0:T(128)S(1)} %copy-done.1, bf16[256,128]{1,0:T(8,128)(2,1)S(1)} %copy-done, bf16[8192,128]{1,0:T(8,128)(2,1)S(1)} %receiver_weights.1.weights, bf16[16,32,128]{2,1,0:T(8,128)(2,1)S(1)} %collective-permute-done.10.refs_0_, ...), custom_call_target="tpu_custom_call", output_to_operand_aliasing={{}: (5, {})} | custom-call | flops 1048576 | bytes 16384 | tf_op jit(solution)/shard_map/stack/pallas_call | solution.py:321
  (16 shorter events, 0.1 us)
Async XLA Ops:
  0.0 22.1 %copy-start = (bf16[256,128]{1,0:T(8,128)(2,1)S(1)}, bf16[256,128]{1,0:T(8,128)(2,1)}, u32[]{:S(2)}) copy-start(bf16[256,128]{1,0:T(8,128)(2,1)} %constant.3.table) | copy-start | bytes 196612
  0.0 22.1 %copy-start.1 = (s32[4]{0:T(128)S(1)}, s32[4]{0:T(128)}, u32[]{:S(2)}) copy-start(s32[4]{0:T(128)} %steps_in.11) | copy-start | bytes 52
  2.4 5.0 %collective-permute-start.4 = (bf16[64,32,128]{2,1,0:T(8,128)(2,1)S(1)}, bf16[64,32,128]{2,1,0:T(8,128)(2,1)S(1)}, u32[]{:S(2)}, u32[]{:S(2)}) collective-permute-start(bf16[64,32,128]{2,1,0:T(8,128)(2,1)S(1)} %get-tuple-element.30.both), channel_id=1, source_target_pairs={{0,1},{1,0},{2,3},{3,2},{4,5},{5,4},{6,7},{7,6},{8,9},{9,8},{10,11... | collective-permute-start | bytes 1572872 | tf_op jit(solution)/shard_map/ppermute | solution.py:363
  2.9 10.2 %collective-permute-start.3 = (bf16[32,32,128]{2,1,0:T(8,128)(2,1)S(1)}, bf16[32,32,128]{2,1,0:T(8,128)(2,1)S(1)}, u32[]{:S(2)}, u32[]{:S(2)}) collective-permute-start(bf16[32,32,128]{2,1,0:T(8,128)(2,1)S(1)} %get-tuple-element.28.refs_0_), channel_id=1, source_target_pairs={{0,4},{1,5},{4,8},{5,9},{8,12},{9,13},{12,14},{13,15},{14,10},{15,... | collective-permute-start | bytes 786440 | tf_op jit(solution)/shard_map/ppermute | solution.py:357
  5.5 9.6 %collective-permute-start.2 = (bf16[32,32,128]{2,1,0:T(8,128)(2,1)S(1)}, bf16[32,32,128]{2,1,0:T(8,128)(2,1)S(1)}, u32[]{:S(2)}, u32[]{:S(2)}) collective-permute-start(bf16[32,32,128]{2,1,0:T(8,128)(2,1)S(1)} %get-tuple-element.29), channel_id=1, source_target_pairs={{0,3},{1,2},{4,1},{5,0},{8,5},{9,4},{12,9},{13,8},{14,13},{15,12},... | collective-permute-start | bytes 786440 | tf_op jit(solution)/shard_map/ppermute | solution.py:357
  5.5 12.2 %collective-permute-start.1 = (bf16[32,32,128]{2,1,0:T(8,128)(2,1)S(1)}, bf16[32,32,128]{2,1,0:T(8,128)(2,1)S(1)}, u32[]{:S(2)}, u32[]{:S(2)}) collective-permute-start(bf16[32,32,128]{2,1,0:T(8,128)(2,1)S(1)} %get-tuple-element.29), channel_id=1, source_target_pairs={{0,5},{1,4},{4,9},{5,8},{8,13},{9,12},{12,15},{13,14},{14,11},{15,... | collective-permute-start | bytes 786440 | tf_op jit(solution)/shard_map/ppermute | solution.py:357
  7.3 12.8 %collective-permute-start = (bf16[32,32,128]{2,1,0:T(8,128)(2,1)S(1)}, bf16[32,32,128]{2,1,0:T(8,128)(2,1)S(1)}, u32[]{:S(2)}, u32[]{:S(2)}) collective-permute-start(bf16[32,32,128]{2,1,0:T(8,128)(2,1)S(1)} %get-tuple-element.28.refs_0_), channel_id=1, source_target_pairs={{0,2},{1,3},{4,0},{5,1},{8,4},{9,5},{12,8},{13,9},{14,12},{15,13},... | collective-permute-start | bytes 786440 | tf_op jit(solution)/shard_map/ppermute | solution.py:357
  13.2 11.8 %collective-permute-start.5 = (bf16[32,32,128]{2,1,0:T(8,128)(2,1)S(1)}, bf16[32,32,128]{2,1,0:T(8,128)(2,1)S(1)}, u32[]{:S(2)}, u32[]{:S(2)}) collective-permute-start(bf16[32,32,128]{2,1,0:T(8,128)(2,1)S(1)} %collective-permute-done.3.refs_0_), channel_id=1, source_target_pairs={{0,4},{1,5},{4,8},{5,9},{8,12},{9,13},{12,14},{13,15},{14,10},{15,... | collective-permute-start | bytes 786440 | tf_op jit(solution)/shard_map/ppermute | solution.py:357
  15.2 10.7 %collective-permute-start.9 = (bf16[32,32,128]{2,1,0:T(8,128)(2,1)S(1)}, bf16[32,32,128]{2,1,0:T(8,128)(2,1)S(1)}, u32[]{:S(2)}, u32[]{:S(2)}) collective-permute-start(bf16[32,32,128]{2,1,0:T(8,128)(2,1)S(1)} %collective-permute-done.2.refs_3_), channel_id=1, source_target_pairs={{0,2},{1,3},{4,0},{5,1},{8,4},{9,5},{12,8},{13,9},{14,12},{15,13},... | collective-permute-start | bytes 786440 | tf_op jit(solution)/shard_map/ppermute | solution.py:357
  20.1 9.4 %collective-permute-start.7 = (bf16[32,32,128]{2,1,0:T(8,128)(2,1)S(1)}, bf16[32,32,128]{2,1,0:T(8,128)(2,1)S(1)}, u32[]{:S(2)}, u32[]{:S(2)}) collective-permute-start(bf16[32,32,128]{2,1,0:T(8,128)(2,1)S(1)} %collective-permute-done.1.refs_1_), channel_id=1, source_target_pairs={{0,4},{1,5},{4,8},{5,9},{8,12},{9,13},{12,14},{13,15},{14,10},{15,... | collective-permute-start | bytes 786440 | tf_op jit(solution)/shard_map/ppermute | solution.py:357
  21.7 9.7 %collective-permute-start.8 = (bf16[32,32,128]{2,1,0:T(8,128)(2,1)S(1)}, bf16[32,32,128]{2,1,0:T(8,128)(2,1)S(1)}, u32[]{:S(2)}, u32[]{:S(2)}) collective-permute-start(bf16[32,32,128]{2,1,0:T(8,128)(2,1)S(1)} %collective-permute-done.refs_2_), channel_id=1, source_target_pairs={{0,2},{1,3},{4,0},{5,1},{8,4},{9,5},{12,8},{13,9},{14,12},{15,13},... | collective-permute-start | bytes 786440 | tf_op jit(solution)/shard_map/ppermute | solution.py:357
  25.0 11.5 %collective-permute-start.6 = (bf16[32,32,128]{2,1,0:T(8,128)(2,1)S(1)}, bf16[32,32,128]{2,1,0:T(8,128)(2,1)S(1)}, u32[]{:S(2)}, u32[]{:S(2)}) collective-permute-start(bf16[32,32,128]{2,1,0:T(8,128)(2,1)S(1)} %collective-permute-done.5.refs_0_), channel_id=1, source_target_pairs={{0,4},{1,5},{4,8},{5,9},{8,12},{9,13},{12,14},{13,15},{14,10},{15,... | collective-permute-start | bytes 786440 | tf_op jit(solution)/shard_map/ppermute | solution.py:357
  25.9 11.1 %collective-permute-start.11 = (bf16[32,32,128]{2,1,0:T(8,128)(2,1)S(1)}, bf16[32,32,128]{2,1,0:T(8,128)(2,1)S(1)}, u32[]{:S(2)}, u32[]{:S(2)}) collective-permute-start(bf16[32,32,128]{2,1,0:T(8,128)(2,1)S(1)} %collective-permute-done.9.refs_3_), channel_id=1, source_target_pairs={{0,2},{1,3},{4,0},{5,1},{8,4},{9,5},{12,8},{13,9},{14,12},{15,13},... | collective-permute-start | bytes 786440 | tf_op jit(solution)/shard_map/ppermute | solution.py:357
  31.3 11.2 %collective-permute-start.16 = (bf16[32,32,128]{2,1,0:T(8,128)(2,1)S(1)}, bf16[32,32,128]{2,1,0:T(8,128)(2,1)S(1)}, u32[]{:S(2)}, u32[]{:S(2)}) collective-permute-start(bf16[32,32,128]{2,1,0:T(8,128)(2,1)S(1)} %collective-permute-done.8.refs_2_), channel_id=1, source_target_pairs={{0,2},{1,3},{4,0},{5,1},{8,4},{9,5},{12,8},{13,9},{14,12},{15,13},... | collective-permute-start | bytes 786440 | tf_op jit(solution)/shard_map/ppermute | solution.py:357
  32.3 11.9 %collective-permute-start.15 = (bf16[32,32,128]{2,1,0:T(8,128)(2,1)S(1)}, bf16[32,32,128]{2,1,0:T(8,128)(2,1)S(1)}, u32[]{:S(2)}, u32[]{:S(2)}) collective-permute-start(bf16[32,32,128]{2,1,0:T(8,128)(2,1)S(1)} %collective-permute-done.7.refs_1_), channel_id=1, source_target_pairs={{0,4},{1,5},{4,8},{5,9},{8,12},{9,13},{12,14},{13,15},{14,10},{15,... | collective-permute-start | bytes 786440 | tf_op jit(solution)/shard_map/ppermute | solution.py:357
  37.0 10.1 %collective-permute-start.14 = (bf16[16,32,128]{2,1,0:T(8,128)(2,1)S(1)}, bf16[16,32,128]{2,1,0:T(8,128)(2,1)S(1)}, u32[]{:S(2)}, u32[]{:S(2)}) collective-permute-start(bf16[16,32,128]{2,1,0:T(8,128)(2,1)S(1)} %get-tuple-element.51), channel_id=1, source_target_pairs={{0,2},{1,3},{4,0},{5,1},{8,4},{9,5},{12,8},{13,9},{14,12},{15,13},... | collective-permute-start | bytes 393224 | tf_op jit(solution)/shard_map/ppermute | solution.py:357
  37.6 9.5 %collective-permute-start.13 = (bf16[16,32,128]{2,1,0:T(8,128)(2,1)S(1)}, bf16[16,32,128]{2,1,0:T(8,128)(2,1)S(1)}, u32[]{:S(2)}, u32[]{:S(2)}) collective-permute-start(bf16[16,32,128]{2,1,0:T(8,128)(2,1)S(1)} %get-tuple-element.53), channel_id=1, source_target_pairs={{0,4},{1,5},{4,8},{5,9},{8,12},{9,13},{12,14},{13,15},{14,10},{15,... | collective-permute-start | bytes 393224 | tf_op jit(solution)/shard_map/ppermute | solution.py:357
  39.1 9.7 %collective-permute-start.12 = (bf16[16,32,128]{2,1,0:T(8,128)(2,1)S(1)}, bf16[16,32,128]{2,1,0:T(8,128)(2,1)S(1)}, u32[]{:S(2)}, u32[]{:S(2)}) collective-permute-start(bf16[16,32,128]{2,1,0:T(8,128)(2,1)S(1)} %get-tuple-element.52), channel_id=1, source_target_pairs={{0,2},{1,3},{4,0},{5,1},{8,4},{9,5},{12,8},{13,9},{14,12},{15,13},... | collective-permute-start | bytes 393224 | tf_op jit(solution)/shard_map/ppermute | solution.py:357
  42.6 6.3 %collective-permute-start.10 = (bf16[16,32,128]{2,1,0:T(8,128)(2,1)S(1)}, bf16[16,32,128]{2,1,0:T(8,128)(2,1)S(1)}, u32[]{:S(2)}, u32[]{:S(2)}) collective-permute-start(bf16[16,32,128]{2,1,0:T(8,128)(2,1)S(1)} %get-tuple-element.54), channel_id=1, source_target_pairs={{0,4},{1,5},{4,8},{5,9},{8,12},{9,13},{12,14},{13,15},{14,10},{15,... | collective-permute-start | bytes 393224 | tf_op jit(solution)/shard_map/ppermute | solution.py:357
